TPU v7x, 32 devices: a whole 2x2x4 slice. The times are simulated.
32 devices in a mesh: fsdp: 4 (over z), context: 2 (over y), tensor: 4 (over x, core).
Axes of the slice: x: 2, y: 2, z: 4, core: 2. Of those that a mesh axis runs over, the one named last changes fastest.
Arguments:
- tokens: bfloat16 [8, 4096, 768], P('fsdp', 'context'), may hold values from -6 to 6
- cotangent: bfloat16 [8, 4096, 768], P('fsdp', 'context'), may hold values from -6 to 6
- segments: int32 [8, 4096], P('fsdp'), may hold values from 0 to 4, as said below
- steps: int32 [8], P('fsdp'), may hold values from 0 to 255
- table: bfloat16 [256, 128], replicated, may hold values from -5 to 5
- ada_w: bfloat16 [128, 4608], replicated, may hold values from -0.5 to 0.5
- ada_b: bfloat16 [4608], replicated, may hold values from 0.099609375 to 1.8984375
- gain_one: bfloat16 [768], replicated, may hold values from 0.099609375 to 1.8984375
- w_qkv: bfloat16 [768, 2304], P('fsdp', 'tensor'), may hold values from -0.109375 to 0.109375
- w_out: bfloat16 [768, 768], P('tensor', 'fsdp'), may hold values from -3 to 3
- gain_two: bfloat16 [768], replicated, may hold values from 0.099609375 to 1.8984375
- w_up: bfloat16 [768, 3072], P('fsdp', 'tensor'), may hold values from -0.109375 to 0.109375
- b_up: bfloat16 [3072], replicated, may hold values from -3 to 3
- w_down: bfloat16 [3072, 768], P('tensor', 'fsdp'), may hold values from -0.15625 to 0.15625
- b_down: bfloat16 [768], replicated, may hold values from -3 to 3
Outputs:
- block_out: bfloat16 [8, 4096, 768], P('fsdp', 'context')
- grad_tokens: float32 [8, 4096, 768], P('fsdp', 'context', 'tensor')
- grad_table: float32 [256, 128], replicated
- grad_ada_w: float32 [128, 4608], replicated
- grad_ada_b: float32 [4608], replicated
- grad_gain_one: float32 [768], replicated
- grad_w_qkv: float32 [768, 2304], P('fsdp', 'tensor')
- grad_w_out: float32 [768, 768], P('tensor', 'fsdp')
- grad_gain_two: float32 [768], replicated
- grad_w_up: float32 [768, 3072], P('fsdp', 'tensor')
- grad_b_up: float32 [3072], replicated
- grad_w_down: float32 [3072, 768], P('tensor', 'fsdp')
- grad_b_down: float32 [768], replicated
Inputs may be any that keep to these rules, and one draw needn't show every extreme that they name: `segments`: along each sequence segment numbers never fall; 1 to 4 are its documents in order, each present, and 0 marks the padding at its end, present in every sequence. No document has more than 2048 tokens, and in every sequence one document has exactly 2048.
All inputs are finite; a program needn't handle non-finite values.
Results may differ from a plain program's by a relative error of at most 0.02.
Values may be sent and summed in bfloat16 or wider, within the bound.
A program may use at most 768 MiB of HBM per device.

v0:
```python
from functools import partial

import jax
import jax.numpy as jnp
from jax import lax
from jax.sharding import PartitionSpec as P

HDIM = 64


precise = lax.Precision.HIGHEST


def product(left_side, right_side):
    return jnp.dot(left_side, right_side, preferred_element_type=jnp.float32)


def transposed(left_side, right_side):
    return lax.dot_general(
        left_side, right_side, (((0,), (0,)), ((), ())), preferred_element_type=jnp.float32
    )


def against(left_side, right_side):
    return lax.dot_general(
        left_side, right_side, (((1,), (1,)), ((), ())), preferred_element_type=jnp.float32
    )


def exact_product(left_side, right_side):
    return jnp.dot(left_side, right_side, precision=precise, preferred_element_type=jnp.float32)


def exact_transposed(left_side, right_side):
    return lax.dot_general(
        left_side,
        right_side,
        (((0,), (0,)), ((), ())),
        precision=precise,
        preferred_element_type=jnp.float32,
    )


def exact_against(left_side, right_side):
    return lax.dot_general(
        left_side,
        right_side,
        (((1,), (1,)), ((), ())),
        precision=precise,
        preferred_element_type=jnp.float32,
    )


def normalize(operand):
    center = operand - jnp.mean(operand, axis=-1, keepdims=True)
    scaling = lax.rsqrt(jnp.mean(center * center, axis=-1, keepdims=True) + 1e-05)
    return (center * scaling, scaling)


def norm_back(grad_hat, hatted, scaling):
    return scaling * (
        grad_hat
        - jnp.mean(grad_hat, axis=-1, keepdims=True)
        - hatted * jnp.mean(grad_hat * hatted, axis=-1, keepdims=True)
    )


def positions(segment):
    indices = jnp.arange(segment.shape[0], dtype=jnp.int32)
    change = jnp.concatenate([jnp.ones((1,), jnp.bool_), segment[1:] != segment[:-1]])
    starts = lax.cummax(jnp.where(change, indices, 0), axis=0)
    return indices - starts


def angles_of(offsets, half_width):
    frequency = 10000.0 ** (-jnp.arange(half_width, dtype=jnp.float32) / half_width)
    angles = offsets.astype(jnp.float32)[:, None] * frequency[None, :]
    return (jnp.cos(angles)[:, None, :], jnp.sin(angles)[:, None, :])


def rotate(operand, cosine, sine_part, direction):
    half_width = operand.shape[-1] // 2
    front_half = operand[..., :half_width]
    second = operand[..., half_width:]
    return jnp.concatenate(
        [
            front_half * cosine - direction * second * sine_part,
            direction * front_half * sine_part + second * cosine,
        ],
        axis=-1,
    )


def scores_of(queries, key_rows, allowed):
    raw_scores = (
        jnp.einsum("qhd,khd->hqk", queries, key_rows, preferred_element_type=jnp.float32) * 0.125
    )
    return jnp.where(allowed[None], raw_scores, -1e30)


def attend(queries, key_rows, values, allowed):
    scores = scores_of(queries, key_rows, allowed)
    row_max = jnp.max(scores, axis=-1, keepdims=True)
    weights_raw = jnp.exp(scores - row_max)
    row_total = jnp.sum(weights_raw, axis=-1, keepdims=True)
    weights_low = (weights_raw / row_total).astype(jnp.bfloat16)
    mixture = jnp.einsum("hqk,khd->qhd", weights_low, values, preferred_element_type=jnp.float32)
    return (mixture, row_max + jnp.log(row_total))


def attend_back(queries, key_rows, values, grad_mixture, logsum, allowed, row_delta):
    scores = scores_of(queries, key_rows, allowed)
    chances = jnp.exp(scores - logsum)
    grad_chances = jnp.einsum(
        "qhd,khd->hqk", grad_mixture, values, preferred_element_type=jnp.float32
    )
    row_delta = jnp.sum(chances * grad_chances, axis=-1, keepdims=True)
    grad_scores = (chances * (grad_chances - row_delta)).astype(jnp.bfloat16)
    return (chances.astype(jnp.bfloat16), grad_scores, row_delta)


def local(
    tokens,
    cotangent,
    segments,
    steps,
    table,
    ada_w,
    ada_b,
    gain_one,
    w_qkv,
    w_out,
    gain_two,
    w_up,
    b_up,
    w_down,
    b_down,
):
    w_qkv, w_up, w_out, w_down = (
        lax.all_gather(w_qkv, "fsdp", axis=0, tiled=True),
        lax.all_gather(w_up, "fsdp", axis=0, tiled=True),
        lax.all_gather(w_out, "fsdp", axis=1, tiled=True),
        lax.all_gather(w_down, "fsdp", axis=1, tiled=True),
    )
    tensor_rank = lax.axis_index("tensor")
    context_rank = lax.axis_index("context")
    sequences, own_rows, model_width = tokens.shape
    length = segments.shape[1]
    local_heads = w_out.shape[0] // HDIM
    hidden_width = w_up.shape[1]
    up_bias = lax.dynamic_slice_in_dim(b_up, tensor_rank * hidden_width, hidden_width).astype(
        jnp.float32
    )
    down_bias = b_down.astype(jnp.float32)
    gain_first = gain_one.astype(jnp.float32)
    gain_second = gain_two.astype(jnp.float32)
    leader = (tensor_rank == 0).astype(jnp.float32)
    ada_full = ada_w.astype(jnp.float32)
    choose = (steps[:, None] == jnp.arange(table.shape[0], dtype=jnp.int32)[None, :]).astype(
        jnp.float32
    )
    before = exact_product(choose, table.astype(jnp.float32))
    embedding, silu_back = jax.vjp(jax.nn.silu, before)
    modulation = exact_product(embedding, ada_full) + ada_b.astype(jnp.float32)
    grad_qkv = jnp.zeros(w_qkv.shape, jnp.float32)
    grad_out_w = jnp.zeros(w_out.shape, jnp.float32)
    grad_up = jnp.zeros(w_up.shape, jnp.float32)
    grad_down = jnp.zeros(w_down.shape, jnp.float32)
    grad_bias_up = jnp.zeros((hidden_width,), jnp.float32)
    grad_bias_down = jnp.zeros((model_width,), jnp.float32)
    grad_gain_first = jnp.zeros((model_width,), jnp.float32)
    grad_gain_second = jnp.zeros((model_width,), jnp.float32)
    results = []
    partial_inputs = []
    carried = []
    grad_mods = []
    for number in range(sequences):
        shift_one, scale_one, gate_one, shift_two, scale_two, gate_two = jnp.split(
            modulation[number], 6
        )
        segment = segments[number]
        offsets = positions(segment)
        own_segment = lax.dynamic_slice_in_dim(segment, context_rank * own_rows, own_rows)
        own_offsets = lax.dynamic_slice_in_dim(offsets, context_rank * own_rows, own_rows)
        cosine, sine_part = angles_of(own_offsets, HDIM // 2)
        allowed = own_segment[:, None] == segment[None, :]
        inputs_row = tokens[number].astype(jnp.float32)
        hat_one, scaling_one = normalize(inputs_row)
        lifted_one = hat_one * gain_first
        entry_one = (lifted_one * (1.0 + scale_one) + shift_one).astype(jnp.bfloat16)
        projected = product(entry_one, w_qkv).reshape(own_rows, local_heads, 3, HDIM)
        queries = rotate(projected[:, :, 0], cosine, sine_part, 1.0).astype(jnp.bfloat16)
        key_rows = rotate(projected[:, :, 1], cosine, sine_part, 1.0).astype(jnp.bfloat16)
        values = projected[:, :, 2].astype(jnp.bfloat16)
        key_value = jnp.stack([key_rows, values], axis=1).reshape(own_rows, 2 * local_heads * HDIM)
        gathered = lax.all_gather(key_value, "context", axis=0, tiled=True).reshape(
            length, 2, local_heads, HDIM
        )
        all_keys = gathered[:, 0]
        all_values = gathered[:, 1]
        mixture, logsum = attend(queries, all_keys, all_values, allowed)
        mixture_low = mixture.reshape(own_rows, local_heads * HDIM).astype(jnp.bfloat16)
        attended = lax.psum(product(mixture_low, w_out).astype(jnp.bfloat16), "tensor").astype(
            jnp.float32
        )
        middle = inputs_row + gate_one * attended
        hat_two, scaling_two = normalize(middle)
        lifted_two = hat_two * gain_second
        entry_two = (lifted_two * (1.0 + scale_two) + shift_two).astype(jnp.bfloat16)
        hidden = product(entry_two, w_up) + up_bias
        activated, gelu_back = jax.vjp(partial(jax.nn.gelu, approximate=True), hidden)
        activated_low = activated.astype(jnp.bfloat16)
        output = (
            lax.psum(product(activated_low, w_down).astype(jnp.bfloat16), "tensor").astype(
                jnp.float32
            )
            + down_bias
        )
        results.append((middle + gate_two * output).astype(jnp.bfloat16))
        valid = (own_segment != 0).astype(jnp.float32)[:, None]
        grad_result = cotangent[number].astype(jnp.float32) * valid
        grad_output = (gate_two * grad_result).astype(jnp.bfloat16)
        grad_gate_two = jnp.sum(grad_result * output, axis=0)
        grad_bias_down = grad_bias_down + jnp.sum(grad_output.astype(jnp.float32), axis=0)
        grad_down = grad_down + transposed(activated_low, grad_output)
        grad_active = against(grad_output, w_down)
        grad_hidden = gelu_back(grad_active)[0].astype(jnp.bfloat16)
        grad_bias_up = grad_bias_up + jnp.sum(grad_hidden.astype(jnp.float32), axis=0)
        grad_up = grad_up + transposed(entry_two, grad_hidden)
        grad_entry_two = against(grad_hidden, w_up)
        grad_shift_two = jnp.sum(grad_entry_two, axis=0)
        grad_scale_two = jnp.sum(grad_entry_two * lifted_two, axis=0)
        grad_lifted_two = grad_entry_two * (1.0 + scale_two)
        grad_gain_second = grad_gain_second + jnp.sum(grad_lifted_two * hat_two, axis=0)
        part_two = norm_back(grad_lifted_two * gain_second, hat_two, scaling_two)
        grad_middle = grad_result + lax.psum(part_two.astype(jnp.bfloat16), "tensor").astype(
            jnp.float32
        )
        grad_attended = (gate_one * grad_middle).astype(jnp.bfloat16)
        grad_gate_one = jnp.sum(grad_middle * attended, axis=0)
        grad_out_w = grad_out_w + transposed(mixture_low, grad_attended)
        grad_mixture = (
            against(grad_attended, w_out).astype(jnp.bfloat16).reshape(own_rows, local_heads, HDIM)
        )
        chances_low, grad_scores, row_delta = attend_back(
            queries, all_keys, all_values, grad_mixture, logsum, allowed, None
        )
        grad_queries = (
            jnp.einsum("hqk,khd->qhd", grad_scores, all_keys, preferred_element_type=jnp.float32)
            * 0.125
        )
        grad_all_keys = (
            jnp.einsum("hqk,qhd->khd", grad_scores, queries, preferred_element_type=jnp.float32)
            * 0.125
        )
        grad_all_values = jnp.einsum(
            "hqk,qhd->khd", chances_low, grad_mixture, preferred_element_type=jnp.float32
        )
        both_grads = jnp.stack([grad_all_keys, grad_all_values], axis=1).reshape(
            length, 2 * local_heads * HDIM
        )
        own_grads = (
            lax.psum_scatter(
                both_grads.astype(jnp.bfloat16), "context", scatter_dimension=0, tiled=True
            )
            .astype(jnp.float32)
            .reshape(own_rows, 2, local_heads, HDIM)
        )
        grad_keys = own_grads[:, 0]
        grad_values = own_grads[:, 1]
        grad_queries = rotate(grad_queries, cosine, sine_part, -1.0)
        grad_keys = rotate(grad_keys, cosine, sine_part, -1.0)
        grad_projected = (
            jnp.stack([grad_queries, grad_keys, grad_values], axis=2)
            .reshape(own_rows, local_heads * 3 * HDIM)
            .astype(jnp.bfloat16)
        )
        grad_qkv = grad_qkv + transposed(entry_one, grad_projected)
        grad_entry_one = against(grad_projected, w_qkv)
        grad_shift_one = jnp.sum(grad_entry_one, axis=0)
        grad_scale_one = jnp.sum(grad_entry_one * lifted_one, axis=0)
        grad_lifted_one = grad_entry_one * (1.0 + scale_one)
        grad_gain_first = grad_gain_first + jnp.sum(grad_lifted_one * hat_one, axis=0)
        partial_inputs.append(norm_back(grad_lifted_one * gain_first, hat_one, scaling_one))
        carried.append(grad_middle)
        grad_mods.append(
            jnp.concatenate(
                [
                    grad_shift_one,
                    grad_scale_one,
                    grad_gate_one * leader,
                    grad_shift_two,
                    grad_scale_two,
                    grad_gate_two * leader,
                ]
            )
        )
    summed_inputs = lax.psum_scatter(
        jnp.stack(partial_inputs).astype(jnp.bfloat16), "tensor", scatter_dimension=2, tiled=True
    ).astype(jnp.float32)
    slice_width = model_width // lax.axis_size("tensor")
    own_middle = lax.dynamic_slice_in_dim(
        jnp.stack(carried), tensor_rank * slice_width, slice_width, axis=2
    )
    grad_tokens = summed_inputs + own_middle
    grad_mod = jnp.stack(grad_mods)
    bias_up_full = lax.dynamic_update_slice_in_dim(
        jnp.zeros((b_up.shape[0],), jnp.float32), grad_bias_up, tensor_rank * hidden_width, 0
    )
    grad_qkv, grad_up, grad_out_w, grad_down = (
        lax.psum_scatter(
            grad_qkv.astype(jnp.bfloat16), "fsdp", scatter_dimension=0, tiled=True
        ).astype(jnp.float32),
        lax.psum_scatter(
            grad_up.astype(jnp.bfloat16), "fsdp", scatter_dimension=0, tiled=True
        ).astype(jnp.float32),
        lax.psum_scatter(
            grad_out_w.astype(jnp.bfloat16), "fsdp", scatter_dimension=1, tiled=True
        ).astype(jnp.float32),
        lax.psum_scatter(
            grad_down.astype(jnp.bfloat16), "fsdp", scatter_dimension=1, tiled=True
        ).astype(jnp.float32),
    )
    grad_qkv, grad_up, grad_out_w, grad_down = (
        lax.psum(grad_qkv.astype(jnp.bfloat16), "context").astype(jnp.float32),
        lax.psum(grad_up.astype(jnp.bfloat16), "context").astype(jnp.float32),
        lax.psum(grad_out_w.astype(jnp.bfloat16), "context").astype(jnp.float32),
        lax.psum(grad_down.astype(jnp.bfloat16), "context").astype(jnp.float32),
    )
    grad_ada_b = jnp.sum(grad_mod, axis=0)
    grad_ada_w = exact_transposed(embedding, grad_mod)
    grad_embedding = exact_against(grad_mod, ada_full)
    grad_before = silu_back(grad_embedding)[0]
    grad_table = exact_transposed(choose, grad_before)
    (
        grad_table,
        grad_ada_w,
        grad_ada_b,
        grad_gain_first,
        grad_gain_second,
        bias_up_full,
        grad_bias_down,
    ) = lax.psum(
        (
            grad_table,
            grad_ada_w,
            grad_ada_b,
            grad_gain_first,
            grad_gain_second,
            bias_up_full,
            grad_bias_down * leader,
        ),
        ("fsdp", "context", "tensor"),
    )
    return (
        jnp.stack(results),
        grad_tokens,
        grad_table,
        grad_ada_w,
        grad_ada_b,
        grad_gain_first,
        grad_qkv,
        grad_out_w,
        grad_gain_second,
        grad_up,
        bias_up_full,
        grad_down,
        grad_bias_down,
    )


def solution(mesh):
    return jax.shard_map(
        local,
        mesh=mesh,
        in_specs=(
            P("fsdp", "context", None),
            P("fsdp", "context", None),
            P("fsdp", None),
            P("fsdp"),
            P(),
            P(),
            P(),
            P(),
            P("fsdp", "tensor"),
            P("tensor", "fsdp"),
            P(),
            P("fsdp", "tensor"),
            P(),
            P("tensor", "fsdp"),
            P(),
        ),
        out_specs=(
            P("fsdp", "context", None),
            P("fsdp", "context", "tensor"),
            P(),
            P(),
            P(),
            P(),
            P("fsdp", "tensor"),
            P("tensor", "fsdp"),
            P(),
            P("fsdp", "tensor"),
            P(),
            P("tensor", "fsdp"),
            P(),
        ),
        check_vma=False,
    )
```

profile of v0, /device:TPU:0, one launch (start us, length us, event | category | flops | bytes accessed | tf_op | source)
XLA Modules:
  0.0 1699.0 jit_solution(8537734256310967718)
XLA Ops:
  17.1 23.5 %all_gather.18 = bf16[768,576]{1,0:T(8,128)(2,1)S(1)} all-gather(bf16[192,576]{1,0:T(8,128)(2,1)S(1)} %copy-done.39), channel_id=1, replica_groups=mesh['fsdp'=4,'context'=2,'tensor'=4] {'fsdp'}, dimensions={0}, use_global_device_ids=true | all-gather | bytes 1105920 | tf_op jit(solution)/shard_map/all_gather | solution.py:140
  70.0 16.0 all_gather.20
  88.7 8.8 broadcast_compare_fusion.1
  97.5 16.4 all-gather.5.cloned.1.call-done
  113.9 37.9 %fusion.185 = (f32[3,2048]{1,0:T(4,128)S(1)}, f32[3,2048,4096]{2,1,0:T(8,128)}) fusion(bf16[4096,2,3,64]{0,3,2,1:T(8,128)(2,1)} %bitcast.367, bf16[2048,3,32]{0,2,1:T(8,128)(2,1)S(1)} %get-tuple-element.152, bf16[2048,3,32]{0,2,1:T(8,128)(2,1)S(1)} %get-tuple-element.151, pred[2048,4096]{1,0:T(8,128)(4,1)} %broadcast_compare_fusion.1), kind=kOutput, calls=%fused_computation.352 | convolution fusion | flops 3298289664 | bytes 111435776 | tf_op jit(solution)/shard_map/qhd,khd->hqk/dot_general | solution.py:96
  151.9 31.0 %fusion = f32[3,2048]{1,0:T(4,128)S(1)} fusion(f32[3,2048,4096]{2,1,0:T(8,128)} %get-tuple-element.175, f32[3,2048]{1,0:T(4,128)S(1)} %get-tuple-element.174), kind=kLoop, calls=%fused_computation.12 | loop fusion | flops 50325504 | bytes 100712448 | tf_op jit(solution)/shard_map/reduce_sum | solution.py:105
  182.9 33.9 %fusion.119 = bf16[3,64,2048]{2,1,0:T(8,128)(2,1)S(1)} fusion(f32[3,2048,4096]{2,1,0:T(8,128)} %get-tuple-element.175, f32[3,2048]{1,0:T(4,128)S(1)} %fusion, f32[3,2048]{1,0:T(4,128)S(1)} %get-tuple-element.174, bf16[4096,2,3,64]{0,3,2,1:T(8,128)(2,1)} %bitcast.368), kind=kOutput, calls=%fused_computation.184 | convolution fusion | flops 3297116160 | bytes 103071744 | tf_op jit(solution)/shard_map/hqk,khd->qhd/dot_general | solution.py:107
  219.7 68.5 %all-reduce.13.cloned.1.call-done = bf16[2048,768]{1,0:T(8,128)(2,1)} async-done(((bf16[2048,768]{1,0:T(8,128)(2,1)}), bf16[2048,768]{1,0:T(8,128)(2,1)}) %all-reduce.13.cloned.1.call-update) | async-done | bytes 3145744 | tf_op jit(solution)/shard_map/psum | solution.py:203
  288.3 5.6 fusion.105
  300.0 9.2 broadcast_compare_fusion
  309.3 35.7 %all-gather.11.cloned.1.call-done = bf16[4096,384]{0,1:T(8,128)(2,1)} async-done(((bf16[2048,384]{0,1:T(8,128)(2,1)}), bf16[4096,384]{0,1:T(8,128)(2,1)}) %all-gather.11.cloned.1.call-update) | async-done | bytes 3145744 | tf_op jit(solution)/shard_map/all_gather | solution.py:196
  345.0 37.4 %fusion.186 = (f32[3,2048]{1,0:T(4,128)S(1)}, f32[3,2048,4096]{2,1,0:T(8,128)}) fusion(bf16[4096,2,3,64]{0,3,2,1:T(8,128)(2,1)} %bitcast.371, bf16[2048,3,32]{0,2,1:T(8,128)(2,1)S(1)} %get-tuple-element.148, bf16[2048,3,32]{0,2,1:T(8,128)(2,1)S(1)} %get-tuple-element.147, pred[2048,4096]{1,0:T(8,128)(4,1)} %broadcast_compare_fusion), kind=kOutput, calls=%fused_computation.353 | convolution fusion | flops 3298289664 | bytes 111435776 | tf_op jit(solution)/shard_map/qhd,khd->hqk/dot_general | solution.py:96
  382.4 31.0 %fusion.1 = f32[3,2048]{1,0:T(4,128)S(1)} fusion(f32[3,2048,4096]{2,1,0:T(8,128)} %get-tuple-element.177, f32[3,2048]{1,0:T(4,128)S(1)} %get-tuple-element.176), kind=kLoop, calls=%fused_computation.13 | loop fusion | flops 50325504 | bytes 100712448 | tf_op jit(solution)/shard_map/reduce_sum | solution.py:105
  413.5 34.5 %fusion.118 = bf16[3,64,2048]{2,1,0:T(8,128)(2,1)} fusion(f32[3,2048,4096]{2,1,0:T(8,128)} %get-tuple-element.177, f32[3,2048]{1,0:T(4,128)S(1)} %fusion.1, f32[3,2048]{1,0:T(4,128)S(1)} %get-tuple-element.176, bf16[4096,2,3,64]{0,3,2,1:T(8,128)(2,1)} %bitcast.372), kind=kOutput, calls=%fused_computation.183 | convolution fusion | flops 3297116160 | bytes 103071744 | tf_op jit(solution)/shard_map/hqk,khd->qhd/dot_general | solution.py:107
  454.3 66.5 %all-reduce.15.cloned.1.call-done = bf16[2048,768]{1,0:T(8,128)(2,1)} async-done(((bf16[2048,768]{1,0:T(8,128)(2,1)}), bf16[2048,768]{1,0:T(8,128)(2,1)}) %all-reduce.15.cloned.1.call-update) | async-done | bytes 3145744 | tf_op jit(solution)/shard_map/psum | solution.py:203
  520.8 6.3 multiply_reduce_fusion.9
  529.5 9.8 multiply_convert_fusion.7
  539.3 10.3 convert_reduce_fusion.5
  556.7 8.3 convert_reduce_fusion.4
  565.1 12.1 multiply_reduce_fusion.2
  577.2 7.5 multiply_convert_fusion.3
  586.1 118.6 %all-reduce.21.cloned.1.call-done = (bf16[2048,768]{1,0:T(8,128)(2,1)}, bf16[2048,768]{1,0:T(8,128)(2,1)}) async-done(((bf16[2048,768]{1,0:T(8,128)(2,1)}, bf16[2048,768]{1,0:T(8,128)(2,1)}), (bf16[2048,768]{1,0:T(8,128)(2,1)}, bf16[2048,768]{1,0:T(8,128)(2,1)})) %all-reduce.21.cloned.1.call-update) | async-done | bytes 6291472 | tf_op jit(solution)/shard_map/psum | solution.py:236
  704.8 7.1 multiply_convert_fusion.4
  714.6 33.7 %fusion.86 = bf16[4096,1,3,64]{0,3,2,1:T(8,128)(2,1)} fusion(bf16[2048,3,64]{0,2,1:T(8,128)(2,1)S(1)} %bitcast.365, f32[3,2048,4096]{2,1,0:T(8,128)} %get-tuple-element.177, f32[3,2048]{1,0:T(4,128)S(1)} %log_add_fusion), kind=kOutput, calls=%fused_computation.145 | convolution fusion | flops 3272343552 | bytes 103047168 | tf_op jit(solution)/shard_map/hqk,qhd->khd/dot_general | solution.py:256
  748.4 65.7 %multiply_reduce_fusion = (f32[3,2048]{1,0:T(4,128)}, f32[3,2048,4096]{2,1,0:T(8,128)}) fusion(f32[3,2048,4096]{2,1,0:T(8,128)} %get-tuple-element.177, f32[3,2048]{1,0:T(4,128)} %copy-done.19, bf16[2048,3,64]{0,2,1:T(8,128)(2,1)S(1)} %bitcast.366, bf16[4096,2,3,64]{0,3,2,1:T(8,128)(2,1)} %bitcast.373), kind=kOutput, calls=%fused_computation.1 | convolution fusion | flops 3296716800 | bytes 203743232 | tf_op jit(solution)/shard_map/qhd,khd->hqk/dot_general | solution.py:114
  820.5 77.9 %multiply_convert_fusion = bf16[3,2048,4096]{2,1,0:T(8,128)(2,1)} fusion(f32[3,2048,4096]{2,1,0:T(8,128)} %get-tuple-element.184, f32[3,2048,4096]{2,1,0:T(8,128)} %get-tuple-element.177, f32[3,2048]{1,0:T(4,128)S(1)} %copy-done.45, f32[3,2048]{1,0:T(4,128)S(1)} %copy-done.20), kind=kLoop, calls=%fused_computation | loop fusion | flops 100663296 | bytes 251707392 | tf_op jit(solution)/shard_map/convert_element_type | solution.py:118
  898.3 21.3 %fusion.99 = bf16[4096,1,3,64]{0,3,2,1:T(8,128)(2,1)} fusion(bf16[3,2048,4096]{2,1,0:T(8,128)(2,1)} %multiply_convert_fusion, bf16[2048,3,32]{0,2,1:T(8,128)(2,1)S(1)} %copy-done.33, bf16[2048,3,32]{0,2,1:T(8,128)(2,1)S(1)} %copy-done.31), kind=kOutput, calls=%fused_computation.157 | convolution fusion | flops 3224371200 | bytes 52690944 | tf_op jit(solution)/shard_map/hqk,qhd->khd/dot_general | solution.py:253
  926.6 66.3 %multiply_reduce_fusion.1 = (f32[3,2048]{1,0:T(4,128)S(1)}, f32[3,2048,4096]{2,1,0:T(8,128)}) fusion(f32[3,2048,4096]{2,1,0:T(8,128)} %get-tuple-element.175, f32[3,2048]{1,0:T(4,128)S(1)} %copy-done.18, bf16[2048,3,64]{0,2,1:T(8,128)(2,1)S(1)} %bitcast.363, bf16[4096,2,3,64]{0,3,2,1:T(8,128)(2,1)} %bitcast.369), kind=kOutput, calls=%fused_computation.4 | convolution fusion | flops 3296716800 | bytes 203735040 | tf_op jit(solution)/shard_map/qhd,khd->hqk/dot_general | solution.py:114
  992.9 77.8 %multiply_convert_fusion.1 = bf16[3,2048,4096]{2,1,0:T(8,128)(2,1)} fusion(f32[3,2048,4096]{2,1,0:T(8,128)} %get-tuple-element.182, f32[3,2048,4096]{2,1,0:T(8,128)} %get-tuple-element.175, f32[3,2048]{1,0:T(4,128)S(1)} %get-tuple-element.181, f32[3,2048]{1,0:T(4,128)S(1)} %copy-done.18), kind=kLoop, calls=%fused_computation.3 | loop fusion | flops 100663296 | bytes 251707392 | tf_op jit(solution)/shard_map/convert_element_type | solution.py:118
  1070.7 21.2 %fusion.101 = bf16[4096,1,3,64]{0,3,2,1:T(8,128)(2,1)} fusion(bf16[3,2048,4096]{2,1,0:T(8,128)(2,1)} %multiply_convert_fusion.1, bf16[2048,3,32]{0,2,1:T(8,128)(2,1)S(1)} %copy-done.29, bf16[2048,3,32]{0,2,1:T(8,128)(2,1)S(1)} %copy-done.27), kind=kOutput, calls=%fused_computation.160 | convolution fusion | flops 3224371200 | bytes 52690944 | tf_op jit(solution)/shard_map/hqk,qhd->khd/dot_general | solution.py:253
  1091.9 32.6 %fusion.89 = bf16[4096,1,3,64]{0,3,2,1:T(8,128)(2,1)S(1)} fusion(bf16[2048,3,64]{0,2,1:T(8,128)(2,1)S(1)} %bitcast.364, f32[3,2048,4096]{2,1,0:T(8,128)} %get-tuple-element.175, f32[3,2048]{1,0:T(4,128)S(1)} %copy-done.18), kind=kOutput, calls=%fused_computation.146 | convolution fusion | flops 3272343552 | bytes 103047168 | tf_op jit(solution)/shard_map/hqk,qhd->khd/dot_general | solution.py:256
  1127.0 5.9 fusion.169
  1133.0 8.3 add_convert_fusion.4
  1141.7 7.4 fusion.130
  1149.2 6.7 add_convert_fusion.5
  1155.9 8.7 convolution_convert_fusion
  1168.8 22.7 %fusion.120 = f32[2048,3,64]{0,2,1:T(8,128)} fusion(bf16[3,2048,4096]{2,1,0:T(8,128)(2,1)} %multiply_convert_fusion, bf16[4096,2,3,64]{0,3,2,1:T(8,128)(2,1)} %bitcast.374), kind=kOutput, calls=%fused_computation.190 | convolution fusion | flops 3221618688 | bytes 53477376 | tf_op jit(solution)/shard_map/hqk,khd->qhd/dot_general | solution.py:249
  1191.6 22.0 %fusion.121 = f32[2048,3,64]{0,2,1:T(8,128)S(1)} fusion(bf16[3,2048,4096]{2,1,0:T(8,128)(2,1)} %multiply_convert_fusion.1, bf16[4096,2,3,64]{0,3,2,1:T(8,128)(2,1)} %bitcast.370), kind=kOutput, calls=%fused_computation.192 | convolution fusion | flops 3221618688 | bytes 53477376 | tf_op jit(solution)/shard_map/hqk,khd->qhd/dot_general | solution.py:249
  1237.5 12.7 fusion.42
  1250.3 14.0 reduce-scatter.13.cloned.1.call-done
  1264.4 9.6 fusion.109
  1277.2 16.5 copy.53
  1308.1 218.1 %all-reduce.19.cloned.1.call-done = (bf16[2048,768]{1,0:T(8,128)(2,1)}, bf16[2048,768]{1,0:T(8,128)(2,1)}, bf16[2,2048,768]{1,0,2:T(2,128)(2,1)}) async-done(((bf16[2048,768]{1,0:T(8,128)(2,1)}, bf16[2048,768]{1,0:T(8,128)(2,1)}, bf16[2,2048,768]{1,0,2:T(2,128)(2,1)}), (bf16[2048,768]{1,0:T(8,128)(2,1)}, bf16[2048,768]{1,0:T(8,128)(2,1)}, bf16[2,2048,768]{1,0,2:T(2,128)(2,1)})) %all-reduce.19.cloned.1.call-update) | async-done | bytes 12582928 | tf_op jit(solution)/shard_map/psum | solution.py:214
  1526.2 18.4 %convert_reduce_fusion.3 = (f32[768]{0:T(1024)S(1)}, f32[768]{0:T(1024)S(1)}, f32[768]{0:T(1024)S(1)}, f32[768]{0:T(1024)S(1)}, f32[768]{0:T(1024)S(1)}, /*index...) fusion(f32[2048]{0:T(1024)S(1)} %copy-done.53, ...), kind=kLoop, calls=%fused_computation.113 | loop fusion | flops 66055680 | bytes 50381824 | tf_op jit(solution)/shard_map/reduce_sum | solution.py:224
  1558.3 6.0 fusion.103
  1569.5 41.0 %all-reduce.1 = (f32[4608]{0:T(1024)}, f32[768]{0:T(1024)}, f32[768]{0:T(1024)}, f32[3072]{0:T(1024)}, f32[768]{0:T(1024)}) all-reduce(f32[4608]{0:T(1024)S(1)} %reduce_sum.399, f32[768]{0:T(1024)S(1)} %add.351, f32[768]{0:T(1024)S(1)} %add.354, ...), channel_id=1, replica_groups=mesh['fsdp'=4,'context'=2,'tensor'=4] {'fsdp','context','tensor'}, use_global_device_ids=true, to_apply=%region_49.50 | all-reduce | flops 9984 | bytes 79872 | tf_op jit(solution)/shard_map/psum | solution.py:343
  1610.6 6.1 pad_maximum_fusion
  1616.7 69.8 %all-reduce.17.cloned.1.call-done = (f32[256,128]{1,0:T(8,128)}, f32[128,4608]{1,0:T(8,128)}) async-done(((f32[256,128]{1,0:T(8,128)}, f32[128,4608]{1,0:T(8,128)}), (f32[256,128]{1,0:T(8,128)}, f32[128,4608]{1,0:T(8,128)})) %all-reduce.17.cloned.1.call-update) | async-done | bytes 2490384 | tf_op jit(solution)/shard_map/psum | solution.py:343
  (461 shorter events, 153.6 us)
Async XLA Ops:
  8.0 105.8 %all-gather.5.cloned.1.call-start = ((), (), s32[]{:S(2)}) async-start(), calls=%async_computation.6 | async-start | bytes 4718592 | tf_op jit(solution)/shard_map/all_gather | solution.py:196
  67.5 46.4 %copy-start.26 = (bf16[2048,3,32]{0,2,1:T(8,128)(2,1)}, bf16[2048,3,32]{0,2,1:T(8,128)(2,1)S(1)}, u32[]{:S(2)}) copy-start(bf16[2048,3,32]{0,2,1:T(8,128)(2,1)S(1)} %get-tuple-element.151) | copy-start | bytes 1179652
  67.5 46.4 %copy-start.28 = (bf16[2048,3,32]{0,2,1:T(8,128)(2,1)}, bf16[2048,3,32]{0,2,1:T(8,128)(2,1)S(1)}, u32[]{:S(2)}) copy-start(bf16[2048,3,32]{0,2,1:T(8,128)(2,1)S(1)} %get-tuple-element.152) | copy-start | bytes 1179652
  68.9 219.3 %all-reduce.13.cloned.1.call-start = ((), (), s32[]{:S(2)}) async-start(), calls=%async_computation.7 | async-start | bytes 6291456 | tf_op jit(solution)/shard_map/psum | solution.py:203
  182.9 34.0 %copy-start.8 = (bf16[192,768]{0,1:T(8,128)(2,1)S(1)}, bf16[192,768]{0,1:T(8,128)(2,1)}, u32[]{:S(2)}) copy-start(bf16[192,768]{0,1:T(8,128)(2,1)} %all_gather.20) | copy-start | bytes 884740
  216.9 71.4 %copy-start.40 = (f32[768]{0:T(1024)S(1)}, f32[768]{0:T(1024)}, u32[]{:S(2)}) copy-start(f32[768]{0:T(1024)} %get-tuple-element.104) | copy-start | bytes 9220
  216.9 71.4 %copy-start.57 = (f32[2048]{0:T(1024)S(1)}, f32[2048]{0:T(1024)}, u32[]{:S(2)}) copy-start(f32[2048]{0:T(1024)} %get-tuple-element.190) | copy-start | bytes 24580
  219.6 74.8 %slice-start = ((s8[6291456]{0:T(1024)(128)(4,1)}), s8[2097152]{0:T(1024)(128)(4,1)S(1)}, s32[]{:S(2)}) async-start(s8[6291456]{0:T(1024)(128)(4,1)} %bitcast.351), calls=%async_computation.22 | async-start | bytes 4194304
  219.6 74.8 %copy-start.79 = (f32[768]{0:T(1024)S(1)}, f32[768]{0:T(1024)}, u32[]{:S(2)}) copy-start(f32[768]{0:T(1024)} %copy-done.78) | copy-start | bytes 9220
  219.6 74.8 %copy-start.87 = (f32[768]{0:T(1024)S(1)}, f32[768]{0:T(1024)}, u32[]{:S(2)}) copy-start(f32[768]{0:T(1024)} %get-tuple-element.98) | copy-start | bytes 9220
  219.6 74.8 %copy-start.112 = (f32[768]{0:T(1024)S(1)}, f32[768]{0:T(1024)}, u32[]{:S(2)}) copy-start(f32[768]{0:T(1024)} %get-tuple-element.97) | copy-start | bytes 9220
  219.7 125.3 %all-gather.11.cloned.1.call-start = ((), (), s32[]{:S(2)}) async-start(), calls=%async_computation.10 | async-start | bytes 4718592 | tf_op jit(solution)/shard_map/all_gather | solution.py:196
  298.4 46.6 %copy-start.30 = (bf16[2048,3,32]{0,2,1:T(8,128)(2,1)}, bf16[2048,3,32]{0,2,1:T(8,128)(2,1)S(1)}, u32[]{:S(2)}) copy-start(bf16[2048,3,32]{0,2,1:T(8,128)(2,1)S(1)} %get-tuple-element.147) | copy-start | bytes 1179652
  298.4 46.6 %copy-start.32 = (bf16[2048,3,32]{0,2,1:T(8,128)(2,1)}, bf16[2048,3,32]{0,2,1:T(8,128)(2,1)S(1)}, u32[]{:S(2)}) copy-start(bf16[2048,3,32]{0,2,1:T(8,128)(2,1)S(1)} %get-tuple-element.148) | copy-start | bytes 1179652
  299.8 221.0 %all-reduce.15.cloned.1.call-start = ((), (), s32[]{:S(2)}) async-start(), calls=%async_computation.11 | async-start | bytes 6291456 | tf_op jit(solution)/shard_map/psum | solution.py:203
  448.0 72.8 %copy-start.41 = (f32[768]{0:T(1024)S(1)}, f32[768]{0:T(1024)}, u32[]{:S(2)}) copy-start(f32[768]{0:T(1024)} %get-tuple-element.104) | copy-start | bytes 9220
  448.0 72.8 %copy-start.43 = (f32[768]{0:T(1024)S(1)}, f32[768]{0:T(1024)}, u32[]{:S(2)}) copy-start(f32[768]{0:T(1024)} %get-tuple-element.99) | copy-start | bytes 9220
  448.1 79.2 %slice-start.2 = ((s8[6291456]{0:T(1024)(128)(4,1)}), s8[2097152]{0:T(1024)(128)(4,1)S(1)}, s32[]{:S(2)}) async-start(s8[6291456]{0:T(1024)(128)(4,1)} %bitcast.353), calls=%async_computation.24 | async-start | bytes 4194304
  452.2 77.2 %all-gather.7.cloned.1.call-start = ((), (), s32[]{:S(2)}) async-start(), calls=%async_computation.8 | async-start | bytes 1474560 | tf_op jit(solution)/shard_map/all_gather | solution.py:141
  452.8 86.5 %all-gather.9.cloned.1.call-start = ((), (), s32[]{:S(2)}) async-start(), calls=%async_computation.9 | async-start | bytes 1474560 | tf_op jit(solution)/shard_map/all_gather | solution.py:143
  453.4 251.4 %all-reduce.21.cloned.1.call-start = ((), (), s32[]{:S(2)}) async-start(), calls=%async_computation.20 | async-start | bytes 12582912 | tf_op jit(solution)/shard_map/psum | solution.py:236
  453.4 251.3 %copy-start.52 = (f32[2048]{0:T(1024)}, f32[2048]{0:T(1024)S(1)}, u32[]{:S(2)}) copy-start(f32[2048]{0:T(1024)S(1)} %compare_convert_fusion.1) | copy-start | bytes 24580
  453.5 251.3 %copy-start.54 = (f32[2048]{0:T(1024)}, f32[2048]{0:T(1024)S(1)}, u32[]{:S(2)}) copy-start(f32[2048]{0:T(1024)S(1)} %compare_convert_fusion) | copy-start | bytes 24580
  453.5 123.6 %copy-start.91 = (f32[768]{0:T(1024)}, f32[768]{0:T(1024)S(1)}, u32[]{:S(2)}) copy-start(f32[768]{0:T(1024)S(1)} %convert_element_type.335) | copy-start | bytes 9220
  454.3 102.4 %copy-start.108 = (f32[768]{0:T(1024)}, f32[768]{0:T(1024)S(1)}, u32[]{:S(2)}) copy-start(f32[768]{0:T(1024)S(1)} %dynamic-slice_convert_fusion) | copy-start | bytes 9220
  454.3 122.8 %copy-start.65 = (f32[2048]{0:T(1024)}, f32[2048]{0:T(1024)S(1)}, u32[]{:S(2)}) copy-start(f32[2048]{0:T(1024)S(1)} %broadcast_multiply_fusion.12) | copy-start | bytes 24580
  527.7 49.5 %copy-start.67 = (f32[2048]{0:T(1024)}, f32[2048]{0:T(1024)S(1)}, u32[]{:S(2)}) copy-start(f32[2048]{0:T(1024)S(1)} %broadcast_multiply_fusion.10) | copy-start | bytes 24580
  529.4 47.8 %copy-start.76 = (f32[2048]{0:T(1024)}, f32[2048]{0:T(1024)S(1)}, u32[]{:S(2)}) copy-start(f32[2048]{0:T(1024)S(1)} %add_rsqrt_fusion.2) | copy-start | bytes 24580
  529.4 47.8 %copy-start.74 = (f32[2048]{0:T(1024)}, f32[2048]{0:T(1024)S(1)}, u32[]{:S(2)}) copy-start(f32[2048]{0:T(1024)S(1)} %add_rsqrt_fusion) | copy-start | bytes 24580
  584.7 628.9 %reduce-scatter.19.cloned.1.call-start = ((), (), s32[]{:S(2)}) async-start(), calls=%async_computation.17 | async-start | bytes 491520
  586.1 128.5 %copy-start.19 = (f32[3,2048]{1,0:T(4,128)}, f32[3,2048]{1,0:T(4,128)S(1)}, u32[]{:S(2)}) copy-start(f32[3,2048]{1,0:T(4,128)S(1)} %log_add_fusion) | copy-start | bytes 73732
  748.4 65.7 %copy-start.17 = (bf16[3,64,2048]{2,1,0:T(8,128)(2,1)S(1)}, bf16[3,64,2048]{2,1,0:T(8,128)(2,1)}, u32[]{:S(2)}) copy-start(bf16[3,64,2048]{2,1,0:T(8,128)(2,1)} %copy-done.16) | copy-start | bytes 2359300
  748.4 68.4 %copy-start.15 = (bf16[3,64,2048]{2,1,0:T(8,128)(2,1)S(1)}, bf16[3,64,2048]{2,1,0:T(8,128)(2,1)}, u32[]{:S(2)}) copy-start(bf16[3,64,2048]{2,1,0:T(8,128)(2,1)} %fusion.118) | copy-start | bytes 2359300
  820.4 394.9 %reduce-scatter.11.cloned.1.call-start = ((), (), s32[]{:S(2)}) async-start(), calls=%async_computation.13 | async-start | bytes 4718592 | tf_op jit(solution)/shard_map/reduce_scatter | solution.py:263
  820.4 77.9 %copy-start.31 = (bf16[2048,3,32]{0,2,1:T(8,128)(2,1)S(1)}, bf16[2048,3,32]{0,2,1:T(8,128)(2,1)}, u32[]{:S(2)}) copy-start(bf16[2048,3,32]{0,2,1:T(8,128)(2,1)} %copy-done.30) | copy-start | bytes 1179652
  820.5 77.9 %copy-start.33 = (bf16[2048,3,32]{0,2,1:T(8,128)(2,1)S(1)}, bf16[2048,3,32]{0,2,1:T(8,128)(2,1)}, u32[]{:S(2)}) copy-start(bf16[2048,3,32]{0,2,1:T(8,128)(2,1)} %copy-done.32) | copy-start | bytes 1179652
  926.5 291.9 %reduce-scatter.9.cloned.1.call-start = ((), (), s32[]{:S(2)}) async-start(), calls=%async_computation.12 | async-start | bytes 4718592 | tf_op jit(solution)/shard_map/reduce_scatter | solution.py:263
  992.9 77.8 %copy-start.27 = (bf16[2048,3,32]{0,2,1:T(8,128)(2,1)S(1)}, bf16[2048,3,32]{0,2,1:T(8,128)(2,1)}, u32[]{:S(2)}) copy-start(bf16[2048,3,32]{0,2,1:T(8,128)(2,1)} %copy-done.26) | copy-start | bytes 1179652
  992.9 77.8 %copy-start.29 = (bf16[2048,3,32]{0,2,1:T(8,128)(2,1)S(1)}, bf16[2048,3,32]{0,2,1:T(8,128)(2,1)}, u32[]{:S(2)}) copy-start(bf16[2048,3,32]{0,2,1:T(8,128)(2,1)} %copy-done.28) | copy-start | bytes 1179652
  1126.5 123.8 %reduce-scatter.17.cloned.1.call-start = ((), (), s32[]{:S(2)}) async-start(), calls=%async_computation.16 | async-start | bytes 1474560 | tf_op jit(solution)/shard_map/reduce_scatter | solution.py:320
  1141.4 108.9 %reduce-scatter.15.cloned.1.call-start = ((), (), s32[]{:S(2)}) async-start(), calls=%async_computation.15 | async-start | bytes 1474560 | tf_op jit(solution)/shard_map/reduce_scatter | solution.py:314
  1155.9 108.4 %reduce-scatter.13.cloned.1.call-start = ((), (), s32[]{:S(2)}) async-start(), calls=%async_computation.14 | async-start | bytes 1228800 | tf_op jit(solution)/shard_map/reduce_scatter | solution.py:311
  1237.4 63.7 %all-reduce.23.cloned.1.call-start = ((), (), s32[]{:S(2)}) async-start(), calls=%async_computation.21 | async-start | bytes 1867776 | tf_op jit(solution)/shard_map/psum | solution.py:325
  1264.3 261.9 %all-reduce.19.cloned.1.call-start = ((), (), s32[]{:S(2)}) async-start(), calls=%async_computation.19 | async-start | bytes 25165824 | tf_op jit(solution)/shard_map/psum | solution.py:214
  1293.7 232.4 %copy-start.56 = (f32[2048]{0:T(1024)S(1)}, f32[2048]{0:T(1024)}, u32[]{:S(2)}) copy-start(f32[2048]{0:T(1024)} %copy-done.54) | copy-start | bytes 24580
  1293.8 232.4 %copy-start.83 = (f32[768]{0:T(1024)S(1)}, f32[768]{0:T(1024)}, u32[]{:S(2)}) copy-start(f32[768]{0:T(1024)} %get-tuple-element.93) | copy-start | bytes 9220
  1293.8 232.4 %copy-start.86 = (f32[768]{0:T(1024)S(1)}, f32[768]{0:T(1024)}, u32[]{:S(2)}) copy-start(f32[768]{0:T(1024)} %get-tuple-element.96) | copy-start | bytes 9220
  1293.8 392.7 %all-reduce.17.cloned.1.call-start = ((), (), s32[]{:S(2)}) async-start(), calls=%async_computation.18 | async-start | bytes 4980736 | tf_op jit(solution)/shard_map/psum | solution.py:343
  (111 other events, 886.9 us)
Sparse Core Ops, SparseCore 0:
  69.1 44.7 all-gather.4
  219.8 68.4 all-reduce.12
  299.9 45.0 all-gather.10
  452.3 68.4 all-reduce.14
  584.8 119.8 all-reduce.20
  1264.4 36.6 all-reduce.22
  1304.7 221.4 all-reduce.18
  1550.6 135.9 all-reduce.16
Sparse Core Ops, SparseCore 1:
  454.2 30.2 all-gather.6
  485.9 29.4 all-gather.8
  820.5 20.8 reduce-scatter.18
  926.6 43.5 reduce-scatter.10
  1126.6 43.4 reduce-scatter.8
  1172.5 29.2 reduce-scatter.16
  1204.0 27.8 reduce-scatter.14
  1237.5 26.7 reduce-scatter.12
where the time goes:
time: 1710 us; the launch traced here: 1700 us
  waiting for transfers between devices  614 us (36%)
  matrix products  573 us (34%)
  other arithmetic  354 us (21%)
  blocking collectives  80.5 us (5%)
  local copies, waits for them, and re-layouts  56.9 us (3%)
  between operations  18.7 us (1%)
    psum x1, waiting for transfers between devices, local(): lax.psum(product(activated_low, w_down).astype(jnp.bfloat16), 'tensor')  218 us
    convert_element_type x2, other arithmetic, attend_back(): grad_scores = (chances * (grad_chances - row_delta)).astype(jnp.bfloat16)  156 us
    psum x2, waiting for transfers between devices, local(): lax.psum(product(mixture_low, w_out).astype(jnp.bfloat16), 'tensor')  135 us
    dot_general x2, matrix products, attend_back(): jnp.einsum('qhd,khd->hqk', grad_mixture, values, preferred_element_type=j...  132 us
    psum x1, waiting for transfers between devices, local(): lax.psum(part_two.astype(jnp.bfloat16), 'tensor').astype(jnp.float32)  119 us
    dot_general x2, matrix products, scores_of(): jnp.einsum('qhd,khd->hqk', queries, key_rows, preferred_element_type=jnp....  75.4 us
    psum x1, waiting for transfers between devices, local(): lax.psum((grad_table, grad_ada_w, grad_ada_b, grad_gain_first, grad_gain_...  69.8 us
    dot_general x2, matrix products, attend(): jnp.einsum('hqk,khd->qhd', weights_low, values, preferred_element_type=jn...  68.5 us
  transfers between devices with their start and end apart: 16, of which 9 were waited for; matrix products, arithmetic and copies ran while one was open for 31% of the time, Pallas kernels for 0%

commit v1 on v0

--- a/solution.py
+++ b/solution.py
@@ -1,14 +1,27 @@
+import math
 from functools import partial
 
 import jax
 import jax.numpy as jnp
 from jax import lax
+from jax.experimental import pallas as pl
+from jax.experimental.pallas import tpu as pltpu
 from jax.sharding import PartitionSpec as P
 
 HDIM = 64
+HALF = HDIM // 2
+SEGMENTS = 5
+WIDE = 128
+MASKED = 2.0**100
+LOG2E = math.log2(math.e)
+SAFE_EXPONENT = 60.0
+EPSILON = 1e-05
+VMEM = 56 * 2**20
 
 
 precise = lax.Precision.HIGHEST
+f32 = jnp.float32
+bf16 = jnp.bfloat16
 
 
 def product(left_side, right_side):
@@ -51,6 +64,838 @@
     )
 
 
+def document_bounds(segment):
+    indices = jnp.arange(segment.shape[-1], dtype=jnp.int32)
+    same = segment[..., None, :] == jnp.arange(SEGMENTS, dtype=jnp.int32)[:, None]
+    starts = jnp.min(jnp.where(same, indices, segment.shape[-1]), axis=-1)
+    ends = jnp.max(jnp.where(same, indices + 1, 0), axis=-1)
+    return same, starts, ends
+
+
+def positions(segment):
+    same, starts, _ = document_bounds(segment)
+    first = jnp.sum(jnp.where(same, starts[..., :, None], 0), axis=-2)
+    return jnp.arange(segment.shape[-1], dtype=jnp.int32) - first
+
+
+def frequencies():
+    return 10000.0 ** (-jnp.arange(HALF, dtype=jnp.float32) / HALF)
+
+
+def entry_kernel(
+    base_ref,
+    rows_ref,
+    gain_ref,
+    shift_ref,
+    weight_ref,
+    cosine_ref,
+    sine_ref,
+    segment_ref,
+    *refs,
+    heads,
+):
+    del base_ref
+    query_ref, key_ref, key_t_ref, value_ref, value_t_ref, hat_ref, scale_ref, norm_ref = refs[-8:]
+    inputs = rows_ref[0].astype(f32).T
+    center = inputs - jnp.mean(inputs, axis=0, keepdims=True)
+    scaling = lax.rsqrt(jnp.mean(center * center, axis=0, keepdims=True) + EPSILON)
+    hat = center * scaling
+    hat_ref[...] = hat.astype(bf16)
+    scale_ref[...] = scaling
+    entry = (hat * gain_ref[...] + shift_ref[...]).astype(bf16)
+    projected = product(weight_ref[...], entry)
+    cosine = cosine_ref[...]
+    sine = sine_ref[...]
+    tokens = cosine.shape[1]
+    group = heads * HDIM
+    segment = segment_ref[...]
+    number = lax.broadcasted_iota(jnp.int32, (WIDE - HDIM, tokens), 0)
+    same = (number == segment).astype(f32)
+    extra_query = same
+    extra_key = jnp.where(
+        number < SEGMENTS, (same - 1.0) * MASKED, jnp.where(number < SEGMENTS + 3, 1.0, 0.0)
+    )
+    extra_value = jnp.where(number < 3, 1.0, 0.0)
+    norms = []
+    for head in range(heads):
+
+        def turned(kind, factor):
+            at = kind * group + head * HDIM
+            front = projected[at : at + HALF]
+            back = projected[at + HALF : at + HDIM]
+            return jnp.concatenate(
+                [(front * cosine - back * sine) * factor, (front * sine + back * cosine) * factor],
+                axis=0,
+            )
+
+        queries = turned(0, 0.125 * LOG2E)
+        keys = turned(1, 1.0)
+        values = projected[2 * group + head * HDIM : 2 * group + (head + 1) * HDIM]
+        norms.append(jnp.sum(queries * queries, axis=0, keepdims=True))
+        norms.append(jnp.sum(keys * keys, axis=0, keepdims=True))
+        query_ref[head] = jnp.concatenate([queries, extra_query], axis=0).astype(bf16)
+        key_ref[head] = jnp.concatenate([keys, extra_key], axis=0).T.astype(bf16)
+        key_t_ref[head] = keys.astype(bf16)
+        wide_values = jnp.concatenate([values, extra_value], axis=0)
+        value_ref[head] = wide_values.T.astype(bf16)
+        value_t_ref[head] = wide_values[: value_t_ref.shape[1]].astype(bf16)
+    norms += [jnp.zeros_like(norms[0])] * (norm_ref.shape[0] - len(norms))
+    norm_ref[...] = jnp.concatenate(norms, axis=0)
+
+
+def entry_call(base, rows, row_index, gain, shift, weight, cosine, sine, segment, earlier, tile):
+    length = cosine.shape[1]
+    width, depth = weight.shape
+    heads = width // (3 * HDIM)
+    steps = rows.shape[1] // tile
+    lanes = lambda i, base: (0, base[0] + i)
+    heads_lanes = lambda i, base: (0, 0, base[0] + i)
+    heads_rows = lambda i, base: (0, base[0] + i, 0)
+    whole = lambda i, base: (0, 0)
+    shapes = [
+        jax.ShapeDtypeStruct((heads, WIDE, length), bf16),
+        jax.ShapeDtypeStruct((heads, length, WIDE), bf16),
+        jax.ShapeDtypeStruct((heads, HDIM, length), bf16),
+        jax.ShapeDtypeStruct((heads, length, WIDE), bf16),
+        jax.ShapeDtypeStruct((heads, HDIM + 16, length), bf16),
+        jax.ShapeDtypeStruct((depth, length), bf16),
+        jax.ShapeDtypeStruct((1, length), f32),
+        jax.ShapeDtypeStruct((8, length), f32),
+    ]
+    out_specs = [
+        pl.BlockSpec((heads, WIDE, tile), heads_lanes),
+        pl.BlockSpec((heads, tile, WIDE), heads_rows),
+        pl.BlockSpec((heads, HDIM, tile), heads_lanes),
+        pl.BlockSpec((heads, tile, WIDE), heads_rows),
+        pl.BlockSpec((heads, HDIM + 16, tile), heads_lanes),
+        pl.BlockSpec((depth, tile), lanes),
+        pl.BlockSpec((1, tile), lanes),
+        pl.BlockSpec((8, tile), lanes),
+    ]
+    operands = [rows, gain, shift, weight, cosine, sine, segment]
+    in_specs = [
+        pl.BlockSpec((1, tile, depth), lambda i, base: (base[1], i, 0)),
+        pl.BlockSpec((depth, 1), whole),
+        pl.BlockSpec((depth, 1), whole),
+        pl.BlockSpec((width, depth), whole),
+        pl.BlockSpec((HALF, tile), lanes),
+        pl.BlockSpec((HALF, tile), lanes),
+        pl.BlockSpec((1, tile), lanes),
+    ]
+    aliases = {}
+    if earlier is not None:
+        aliases = {1 + len(operands) + k: k for k in range(len(shapes))}
+        operands += list(earlier)
+        in_specs += [pl.BlockSpec(memory_space=pl.ANY)] * len(shapes)
+    return pl.pallas_call(
+        partial(entry_kernel, heads=heads),
+        grid_spec=pltpu.PrefetchScalarGridSpec(
+            num_scalar_prefetch=1, grid=(steps,), in_specs=in_specs, out_specs=out_specs
+        ),
+        out_shape=shapes,
+        input_output_aliases=aliases,
+        compiler_params=pltpu.CompilerParams(vmem_limit_bytes=VMEM),
+        name="entry",
+    )(jnp.stack([base, row_index]).astype(jnp.int32), *operands)
+
+
+def attend_kernel(range_ref, query_ref, key_ref, value_ref, out_ref, told_ref, total_ref, top_ref, *, block):
+    step = pl.program_id(0)
+    first, last = range_ref[0, step], range_ref[1, step]
+    heads = query_ref.shape[0]
+    total_ref[...] = jnp.zeros_like(total_ref)
+
+    def scores(head, at):
+        return product(key_ref[head, pl.ds(at, block), :], query_ref[head])
+
+    def mix(head, at, weights):
+        return product(value_ref[head, :, pl.ds(at, block)], weights)
+
+    @pl.when(range_ref[2, 0] == 1)
+    def _():
+        top_ref[...] = jnp.zeros_like(top_ref)
+
+        def body(number, carry):
+            at = pl.multiple_of(number * block, block)
+            raw = [scores(head, at) for head in range(heads)]
+            weights = [jnp.exp2(one).astype(bf16) for one in raw]
+            for head in range(heads):
+                total_ref[head] += mix(head, at, weights[head])
+            return carry
+
+        lax.fori_loop(first, last, body, 0)
+
+    @pl.when(range_ref[2, 0] != 1)
+    def _():
+        top_ref[...] = jnp.full_like(top_ref, -3e38)
+
+        def body(number, carry):
+            at = pl.multiple_of(number * block, block)
+            for head in range(heads):
+                raw = scores(head, at)
+                before = top_ref[head]
+                top = jnp.maximum(before, jnp.max(raw, axis=0, keepdims=True))
+                weights = jnp.exp2(raw - top).astype(bf16)
+                total_ref[head] = total_ref[head] * jnp.exp2(before - top) + mix(head, at, weights)
+                top_ref[head] = top
+            return carry
+
+        lax.fori_loop(first, last, body, 0)
+
+    tile = query_ref.shape[2]
+    number = lax.broadcasted_iota(jnp.int32, (16, tile), 0)
+    for head in range(heads):
+        total = total_ref[head]
+        mass = total[HDIM : HDIM + 1]
+        out_ref[0, pl.ds(head * HDIM, HDIM), :] = (total[:HDIM] * (1.0 / mass)).astype(bf16)
+        rows = split_rows(-(top_ref[head] + jnp.log2(mass)), number, SEGMENTS)
+        told_ref[head, :HDIM, :] = query_ref[head, :HDIM, :]
+        told_ref[head, HDIM : HDIM + 16, :] = jnp.where(
+            number < SEGMENTS, query_ref[head, HDIM : HDIM + 16, :].astype(f32), rows
+        ).astype(bf16)
+        told_ref[head, HDIM + 16 :, :] = query_ref[head, HDIM + 16 :, :]
+
+
+def split_rows(values, number, first):
+    high = values.astype(bf16).astype(f32)
+    rest = values - high
+    middle = rest.astype(bf16).astype(f32)
+    low = rest - middle
+    return jnp.where(
+        number == first,
+        high,
+        jnp.where(number == first + 1, middle, jnp.where(number == first + 2, low, 0.0)),
+    )
+
+
+def attend_call(ranges, queries, keys, values_t, tile, block):
+    heads, _, length = queries.shape
+    rows = values_t.shape[1]
+    return pl.pallas_call(
+        partial(attend_kernel, block=block),
+        grid_spec=pltpu.PrefetchScalarGridSpec(
+            num_scalar_prefetch=1,
+            grid=(length // tile,),
+            in_specs=[
+                pl.BlockSpec((heads, WIDE, tile), lambda i, r: (0, 0, i)),
+                pl.BlockSpec((heads, length, WIDE), lambda i, r: (0, 0, 0)),
+                pl.BlockSpec((heads, rows, length), lambda i, r: (0, 0, 0)),
+            ],
+            out_specs=[
+                pl.BlockSpec((1, heads * HDIM, tile), lambda i, r: (i, 0, 0)),
+                pl.BlockSpec((heads, WIDE, tile), lambda i, r: (0, 0, i)),
+            ],
+            scratch_shapes=[
+                pltpu.VMEM((heads, rows, tile), f32),
+                pltpu.VMEM((heads, 1, tile), f32),
+            ],
+        ),
+        out_shape=[
+            jax.ShapeDtypeStruct((length // tile, heads * HDIM, tile), bf16),
+            jax.ShapeDtypeStruct((heads, WIDE, length), bf16),
+        ],
+        compiler_params=pltpu.CompilerParams(vmem_limit_bytes=VMEM),
+        name="attend",
+    )(ranges, queries, keys, values_t)
+
+
+def attend_back_kernel(
+    range_ref,
+    query_ref,
+    key_ref,
+    key_t_ref,
+    value_ref,
+    mixture_ref,
+    grad_ref,
+    cosine_ref,
+    sine_ref,
+    grad_query_ref,
+    grad_key_ref,
+    grad_value_ref,
+    wide_ref,
+    query_total,
+    key_total,
+    value_total,
+    *,
+    block,
+):
+    step = pl.program_id(0)
+    first, last = range_ref[0, step], range_ref[1, step]
+    heads, _, tile = query_ref.shape
+
+    @pl.when(step == 0)
+    def _():
+        wide_ref[...] = jnp.zeros_like(wide_ref)
+        key_total[...] = jnp.zeros_like(key_total)
+        value_total[...] = jnp.zeros_like(value_total)
+
+    number = lax.broadcasted_iota(jnp.int32, (16, tile), 0)
+    query_total[...] = jnp.zeros_like(query_total)
+    for head in range(heads):
+        at = pl.ds(head * HDIM, HDIM)
+        grad = grad_ref[0, at, :]
+        delta = jnp.sum(grad.astype(f32) * mixture_ref[0, at, :].astype(f32), axis=0, keepdims=True)
+        wide_ref[head, :HDIM, :] = grad
+        wide_ref[head, HDIM : HDIM + 16, :] = split_rows(-delta, number, 0).astype(bf16)
+
+    def body(number, carry):
+        at = pl.multiple_of(number * block, block)
+        rows = pl.ds(at, block)
+        raw = [product(key_ref[head, rows, :], query_ref[head]) for head in range(heads)]
+        slope = [product(value_ref[head, rows, :], wide_ref[head]) for head in range(heads)]
+        for head in range(heads):
+            weights = jnp.exp2(raw[head])
+            grad_scores = (weights * slope[head]).astype(bf16)
+            query_total[head] += product(key_t_ref[head, :, rows], grad_scores)
+            key_total[head, :, rows] += against(query_ref[head, :HDIM, :], grad_scores)
+            value_total[head, :, rows] += against(wide_ref[head, :HDIM, :], weights.astype(bf16))
+        return carry
+
+    lax.fori_loop(first, last, body, 0)
+
+    def turned_back(grads, cosine, sine):
+        front, back = grads[:HALF], grads[HALF:]
+        return jnp.concatenate([front * cosine + back * sine, back * cosine - front * sine], axis=0)
+
+    own = pl.ds(pl.multiple_of(step * tile, tile), tile)
+    for head in range(heads):
+        at = pl.ds(head * HDIM, HDIM)
+        grad_query_ref[at, :] = turned_back(
+            query_total[head] * 0.125, cosine_ref[:, own], sine_ref[:, own]
+        ).astype(bf16)
+
+    @pl.when(step == pl.num_programs(0) - 1)
+    def _():
+        for head in range(heads):
+            at = pl.ds(head * HDIM, HDIM)
+            grad_key_ref[at, :] = turned_back(
+                key_total[head] * (1.0 / LOG2E), cosine_ref[...], sine_ref[...]
+            ).astype(bf16)
+            grad_value_ref[at, :] = value_total[head].astype(bf16)
+
+
+def attend_back_call(
+    ranges, queries, keys, keys_t, values, mixture, grad_mixture, cosine, sine, tile, block
+):
+    heads, _, length = queries.shape
+    group = heads * HDIM
+    whole2 = lambda i, r: (0, 0)
+    whole3 = lambda i, r: (0, 0, 0)
+    return pl.pallas_call(
+        partial(attend_back_kernel, block=block),
+        grid_spec=pltpu.PrefetchScalarGridSpec(
+            num_scalar_prefetch=1,
+            grid=(length // tile,),
+            in_specs=[
+                pl.BlockSpec((heads, WIDE, tile), lambda i, r: (0, 0, i)),
+                pl.BlockSpec((heads, length, WIDE), whole3),
+                pl.BlockSpec((heads, HDIM, length), whole3),
+                pl.BlockSpec((heads, length, WIDE), whole3),
+                pl.BlockSpec((1, group, tile), lambda i, r: (i, 0, 0)),
+                pl.BlockSpec((1, group, tile), lambda i, r: (i, 0, 0)),
+                pl.BlockSpec((HALF, length), whole2),
+                pl.BlockSpec((HALF, length), whole2),
+            ],
+            out_specs=[
+                pl.BlockSpec((group, tile), lambda i, r: (0, i)),
+                pl.BlockSpec((group, length), whole2),
+                pl.BlockSpec((group, length), whole2),
+            ],
+            scratch_shapes=[
+                pltpu.VMEM((heads, WIDE, tile), bf16),
+                pltpu.VMEM((heads, HDIM, tile), f32),
+                pltpu.VMEM((heads, HDIM, length), f32),
+                pltpu.VMEM((heads, HDIM, length), f32),
+            ],
+        ),
+        out_shape=[jax.ShapeDtypeStruct((group, length), bf16)] * 3,
+        compiler_params=pltpu.CompilerParams(vmem_limit_bytes=VMEM),
+        name="attend_back",
+    )(ranges, queries, keys, keys_t, values, mixture, grad_mixture, cosine, sine)
+
+
+def middle_kernel(
+    base_ref,
+    mixture_ref,
+    rows_ref,
+    cotangent_ref,
+    valid_ref,
+    mod_ref,
+    up_bias_ref,
+    down_bias_ref,
+    out_weight_ref,
+    up_ref,
+    down_ref,
+    result_ref,
+    grad_mixture_ref,
+    grad_middle_ref,
+    entry_ref,
+    grad_output_ref,
+    active_ref,
+    grad_hidden_ref,
+    grad_out_ref,
+    sums_ref,
+    bias_sums_ref,
+):
+    del base_ref
+    sequence, step = pl.program_id(0), pl.program_id(1)
+    mods = mod_ref[0]
+    gate_one, shift_two, gain_two, gate_two = (mods[k : k + 1] for k in range(4))
+    mixture_t = mixture_ref[0]
+    inputs = rows_ref[0].astype(f32)
+    attended = product(mixture_t.T, out_weight_ref[...])
+    middle = inputs + gate_one * attended
+    center = middle - jnp.mean(middle, axis=-1, keepdims=True)
+    scaling = lax.rsqrt(jnp.mean(center * center, axis=-1, keepdims=True) + EPSILON)
+    hat = center * scaling
+    entry = (hat * gain_two + shift_two).astype(bf16)
+    grad_result = cotangent_ref[0].astype(f32) * valid_ref[0]
+    grad_output = (gate_two * grad_result).astype(bf16)
+    entry_ref[...] = entry.T
+    grad_output_ref[...] = grad_output.T
+
+    @pl.when((sequence == 0) & (step == 0))
+    def _():
+        bias_sums_ref[...] = jnp.zeros_like(bias_sums_ref)
+        grad_out_ref[...] = jnp.zeros_like(grad_out_ref)
+
+    output = down_bias_ref[...]
+    grad_entry = 0.0
+    root = math.sqrt(2.0 / math.pi)
+    for part in range(up_ref.shape[0]):
+        hidden = product(entry, up_ref[part]) + up_bias_ref[part]
+        square = hidden * hidden
+        bent = jnp.tanh(root * hidden * (1.0 + 0.044715 * square))
+        half = 0.5 * (1.0 + bent)
+        active = (hidden * half).astype(bf16)
+        slope = half + (0.5 * root) * hidden * (1.0 - bent * bent) * (1.0 + 0.134145 * square)
+        grad_hidden_wide = product(grad_output, down_ref[part]) * slope
+        grad_hidden = grad_hidden_wide.astype(bf16)
+        output = output + against(active, down_ref[part])
+        grad_entry = grad_entry + against(grad_hidden, up_ref[part])
+        active_ref[part] = active
+        grad_hidden_ref[part] = grad_hidden
+        bias_sums_ref[part] += jnp.sum(grad_hidden.astype(f32), axis=0, keepdims=True)
+    result_ref[0] = (middle + gate_two * output).astype(bf16)
+    grad_lifted = grad_entry * gain_two
+    grad_middle = grad_result + scaling * (
+        grad_lifted
+        - jnp.mean(grad_lifted, axis=-1, keepdims=True)
+        - hat * jnp.mean(grad_lifted * hat, axis=-1, keepdims=True)
+    )
+    grad_attended = (gate_one * grad_middle).astype(bf16)
+    grad_mixture_ref[0] = against(out_weight_ref[...], grad_attended).astype(bf16)
+    grad_middle_ref[0] = grad_middle.T.astype(bf16)
+    grad_out_ref[...] += product(mixture_t, grad_attended)
+
+    @pl.when(step == 0)
+    def _():
+        sums_ref[...] = jnp.zeros_like(sums_ref)
+
+    rows = [
+        jnp.sum(grad_middle * attended, axis=0, keepdims=True),
+        jnp.sum(grad_entry, axis=0, keepdims=True),
+        jnp.sum(grad_entry * hat, axis=0, keepdims=True),
+        jnp.sum(grad_result * output, axis=0, keepdims=True),
+        jnp.sum(grad_output.astype(f32), axis=0, keepdims=True),
+    ]
+    rows += [jnp.zeros_like(rows[0])] * (sums_ref.shape[1] - len(rows))
+    sums_ref[0] += jnp.concatenate(rows, axis=0)
+
+
+def middle_call(
+    base, mixture, rows, cotangent, valid, mods, up_bias, down_bias, out_weight, up, down, tile
+):
+    sequences, depth, own = mixture.shape
+    parts, _, part_width = up.shape
+    steps = own // tile
+    tokens = sequences * own
+    at_rows = lambda s, i, b: (s, b[0] * steps + i, 0)
+    own_rows = lambda s, i, b: (s, i, 0)
+    own_lanes = lambda s, i, b: (s, 0, i)
+    whole2 = lambda s, i, b: (0, 0)
+    whole3 = lambda s, i, b: (0, 0, 0)
+    once = pl.Buffered(1)
+    return pl.pallas_call(
+        middle_kernel,
+        grid_spec=pltpu.PrefetchScalarGridSpec(
+            num_scalar_prefetch=1,
+            grid=(sequences, steps),
+            in_specs=[
+                pl.BlockSpec((1, depth, tile), own_lanes),
+                pl.BlockSpec((1, tile, depth), at_rows),
+                pl.BlockSpec((1, tile, depth), at_rows),
+                pl.BlockSpec((1, tile, 1), own_rows),
+                pl.BlockSpec((1, 8, depth), lambda s, i, b: (s, 0, 0)),
+                pl.BlockSpec((parts, 1, part_width), whole3, pipeline_mode=once),
+                pl.BlockSpec((1, depth), whole2, pipeline_mode=once),
+                pl.BlockSpec((depth, depth), whole2, pipeline_mode=once),
+                pl.BlockSpec((parts, depth, part_width), whole3, pipeline_mode=once),
+                pl.BlockSpec((parts, depth, part_width), whole3, pipeline_mode=once),
+            ],
+            out_specs=[
+                pl.BlockSpec((1, tile, depth), own_rows),
+                pl.BlockSpec((1, depth, tile), own_lanes),
+                pl.BlockSpec((1, depth, tile), own_lanes),
+                pl.BlockSpec((depth, tile), lambda s, i, b: (0, s * steps + i)),
+                pl.BlockSpec((depth, tile), lambda s, i, b: (0, s * steps + i)),
+                pl.BlockSpec((parts, tile, part_width), lambda s, i, b: (0, s * steps + i, 0)),
+                pl.BlockSpec((parts, tile, part_width), lambda s, i, b: (0, s * steps + i, 0)),
+                pl.BlockSpec((depth, depth), whole2),
+                pl.BlockSpec((1, 8, depth), lambda s, i, b: (s, 0, 0)),
+                pl.BlockSpec((parts, 1, part_width), whole3),
+            ],
+        ),
+        out_shape=[
+            jax.ShapeDtypeStruct((sequences, own, depth), bf16),
+            jax.ShapeDtypeStruct((sequences, depth, own), bf16),
+            jax.ShapeDtypeStruct((sequences, depth, own), bf16),
+            jax.ShapeDtypeStruct((depth, tokens), bf16),
+            jax.ShapeDtypeStruct((depth, tokens), bf16),
+            jax.ShapeDtypeStruct((parts, tokens, part_width), bf16),
+            jax.ShapeDtypeStruct((parts, tokens, part_width), bf16),
+            jax.ShapeDtypeStruct((depth, depth), f32),
+            jax.ShapeDtypeStruct((sequences, 8, depth), f32),
+            jax.ShapeDtypeStruct((parts, 1, part_width), f32),
+        ],
+        compiler_params=pltpu.CompilerParams(vmem_limit_bytes=VMEM),
+        name="middle",
+    )(base, mixture, rows, cotangent, valid, mods, up_bias, down_bias, out_weight, up, down)
+
+
+def weights_kernel(entry_ref, grad_output_ref, active_ref, grad_hidden_ref, grad_up_ref, grad_down_ref):
+    grad_up_ref[0] = product(entry_ref[...], grad_hidden_ref[0]).astype(bf16)
+    grad_down_ref[0] = product(grad_output_ref[...], active_ref[0]).astype(bf16)
+
+
+def weights_call(entry_t, grad_output_t, active, grad_hidden):
+    depth, tokens = entry_t.shape
+    parts, _, part_width = active.shape
+    part = lambda i: (i, 0, 0)
+    return pl.pallas_call(
+        weights_kernel,
+        grid=(parts,),
+        in_specs=[
+            pl.BlockSpec((depth, tokens), lambda i: (0, 0)),
+            pl.BlockSpec((depth, tokens), lambda i: (0, 0)),
+            pl.BlockSpec((1, tokens, part_width), part),
+            pl.BlockSpec((1, tokens, part_width), part),
+        ],
+        out_specs=[pl.BlockSpec((1, depth, part_width), part)] * 2,
+        out_shape=[jax.ShapeDtypeStruct((parts, depth, part_width), bf16)] * 2,
+        compiler_params=pltpu.CompilerParams(vmem_limit_bytes=VMEM),
+        name="weights",
+    )(entry_t, grad_output_t, active, grad_hidden)
+
+
+def entry_back_kernel(
+    grad_query_ref,
+    grad_key_ref,
+    grad_value_ref,
+    hat_ref,
+    scale_ref,
+    gain_ref,
+    shift_ref,
+    weight_ref,
+    part_ref,
+    grad_weight_ref,
+    sums_ref,
+):
+    @pl.when(pl.program_id(0) == 0)
+    def _():
+        grad_weight_ref[...] = jnp.zeros_like(grad_weight_ref)
+        sums_ref[...] = jnp.zeros_like(sums_ref)
+
+    grads = jnp.concatenate([grad_query_ref[...], grad_key_ref[...], grad_value_ref[...]], axis=0)
+    grad_entry = product(weight_ref[...], grads)
+    hat = hat_ref[...].astype(f32)
+    gain = gain_ref[...]
+    entry = (hat * gain + shift_ref[...]).astype(bf16)
+    grad_weight_ref[...] += against(grads, entry)
+    grad_lifted = grad_entry * gain
+    part_ref[0] = (
+        scale_ref[...]
+        * (
+            grad_lifted
+            - jnp.mean(grad_lifted, axis=0, keepdims=True)
+            - hat * jnp.mean(grad_lifted * hat, axis=0, keepdims=True)
+        )
+    ).astype(bf16)
+    weighted = grad_entry * hat
+    for lane in range(0, grad_entry.shape[1], WIDE):
+        sums_ref[0] += grad_entry[:, lane : lane + WIDE]
+        sums_ref[1] += weighted[:, lane : lane + WIDE]
+
+
+def entry_back_call(grad_query, grad_key, grad_value, hat_t, scaling, gain, shift, weight, blocks, tile):
+    group, length = grad_query.shape
+    depth = hat_t.shape[0]
+    steps = length // blocks // tile
+    lanes = lambda i: (0, i)
+    whole = lambda i: (0, 0)
+    return pl.pallas_call(
+        entry_back_kernel,
+        grid=(length // tile,),
+        in_specs=[
+            pl.BlockSpec((group, tile), lanes),
+            pl.BlockSpec((group, tile), lanes),
+            pl.BlockSpec((group, tile), lanes),
+            pl.BlockSpec((depth, tile), lanes),
+            pl.BlockSpec((1, tile), lanes),
+            pl.BlockSpec((depth, 1), whole),
+            pl.BlockSpec((depth, 1), whole),
+            pl.BlockSpec((depth, 3 * group), whole),
+        ],
+        out_specs=[
+            pl.BlockSpec((1, depth, tile), lambda i: (i // steps, 0, i % steps)),
+            pl.BlockSpec((3 * group, depth), whole),
+            pl.BlockSpec((2, depth, WIDE), lambda i: (0, 0, 0)),
+        ],
+        out_shape=[
+            jax.ShapeDtypeStruct((blocks, depth, length // blocks), bf16),
+            jax.ShapeDtypeStruct((3 * group, depth), f32),
+            jax.ShapeDtypeStruct((2, depth, WIDE), f32),
+        ],
+        compiler_params=pltpu.CompilerParams(vmem_limit_bytes=VMEM),
+        name="entry_back",
+    )(grad_query, grad_key, grad_value, hat_t, scaling, gain, shift, weight)
+
+
+def by_sequence(
+    tokens,
+    cotangent,
+    segments,
+    steps,
+    table,
+    ada_w,
+    ada_b,
+    gain_one,
+    w_qkv,
+    w_out,
+    gain_two,
+    w_up,
+    b_up,
+    w_down,
+    b_down,
+):
+    fsdp, tensor = lax.axis_size("fsdp"), lax.axis_size("tensor")
+    context = lax.axis_size("context")
+    tensor_rank = lax.axis_index("tensor")
+    context_rank = lax.axis_index("context")
+    fsdp_rank = lax.axis_index("fsdp")
+    sequences, own_rows, depth = tokens.shape
+    length = segments.shape[1]
+    group = w_out.shape[0]
+    part_width = w_up.shape[1]
+    heads = group // HDIM
+    quarter = own_rows // tensor
+
+    mine = lax.dynamic_slice_in_dim(tokens, tensor_rank * quarter, quarter, axis=1)
+    partner = [(k, (k + 1) % context) for k in range(context)]
+    arrived = lax.ppermute(
+        lax.dynamic_index_in_dim(mine, lax.rem(context_rank + 1, context), 0, keepdims=True),
+        "context",
+        partner,
+    )
+    other_rows = lax.all_gather(arrived, "tensor", axis=1, tiled=True)
+
+    by_kind = w_qkv.reshape(-1, heads, 3, HDIM).transpose(0, 2, 1, 3).reshape(-1, 3 * group)
+    qkv = lax.all_gather(by_kind, "fsdp", axis=0, tiled=True)
+    both = ("tensor", "fsdp")
+    up = lax.all_gather(w_up, both, axis=0, tiled=True).reshape(tensor, depth, part_width)
+    down = lax.all_gather(w_down.T, both, axis=0, tiled=True).reshape(tensor, depth, part_width)
+    out_weight = (
+        lax.all_gather(w_out, both, axis=0, tiled=False)
+        .reshape(tensor, fsdp, group, depth // fsdp)
+        .transpose(0, 2, 1, 3)
+        .reshape(depth, depth)
+    )
+
+    all_steps = lax.all_gather(steps, "fsdp", axis=0, tiled=True)
+    ada_full = ada_w.astype(f32)
+    choose = (all_steps[:, None] == jnp.arange(table.shape[0], dtype=jnp.int32)[None, :]).astype(f32)
+    before = exact_product(choose, table.astype(f32))
+    embedding, silu_back = jax.vjp(jax.nn.silu, before)
+    modulation = exact_product(embedding, ada_full) + ada_b.astype(f32)
+    local_mods = lax.dynamic_slice_in_dim(modulation, fsdp_rank * sequences, sequences, axis=0)
+    local_mods = local_mods.reshape(sequences, 6, depth)
+    gain_first, gain_second = gain_one.astype(f32), gain_two.astype(f32)
+    own_mods = lax.dynamic_index_in_dim(local_mods, context_rank, 0, keepdims=False)
+    gain_column = (gain_first * (1.0 + own_mods[1]))[:, None]
+    shift_column = own_mods[0][:, None]
+    mods = jnp.stack(
+        [
+            local_mods[:, 2],
+            local_mods[:, 3],
+            gain_second * (1.0 + local_mods[:, 4]),
+            local_mods[:, 5],
+        ]
+        + [jnp.zeros((sequences, depth), f32)] * 4,
+        axis=1,
+    )
+
+    segment = lax.dynamic_index_in_dim(segments, context_rank, 0, keepdims=False)
+    same, starts, ends = document_bounds(segment)
+    offsets = jnp.arange(length, dtype=jnp.int32) - jnp.sum(jnp.where(same, starts[:, None], 0), axis=0)
+    angles = frequencies()[:, None] * offsets.astype(f32)[None, :]
+    cosine, sine = jnp.cos(angles), jnp.sin(angles)
+    tile = length // (context * tensor)
+    block = tile
+    first_key = jnp.sum(jnp.where(same, starts[:, None], 0), axis=0)[::tile]
+    last_key = jnp.sum(jnp.where(same, ends[:, None], 0), axis=0)[tile - 1 :: tile]
+
+    entry = partial(
+        entry_call,
+        gain=gain_column,
+        shift=shift_column,
+        weight=qkv.T,
+        cosine=cosine,
+        sine=sine,
+        segment=segment[None, :],
+        tile=tile,
+    )
+    per_block = own_rows // tile
+    made = entry(context_rank * per_block, tokens, context_rank, earlier=None)
+    other = lax.rem(context_rank + context - 1, context)
+    made = entry(other * per_block, other_rows, jnp.zeros_like(other), earlier=made)
+    queries, keys, keys_t, values, values_t, hat_t, scaling, norms = made
+    largest = jnp.max(norms, axis=1)[: 2 * heads].reshape(heads, 2)
+    safe = jnp.max(largest[:, 0] * largest[:, 1]) <= SAFE_EXPONENT**2
+    ranges = jnp.stack(
+        [
+            first_key // block,
+            (last_key + block - 1) // block,
+            jnp.broadcast_to(safe.astype(jnp.int32), first_key.shape),
+        ]
+    ).astype(jnp.int32)
+    mixture, told = attend_call(ranges, queries, keys, values_t, tile, block)
+
+    everyone = ("context", "tensor")
+    own_mixture = lax.all_to_all(mixture, everyone, 0, 0, tiled=True).reshape(
+        context, tensor * group, tile
+    )
+    own_segments = lax.dynamic_slice_in_dim(
+        segments, context_rank * own_rows + tensor_rank * quarter, quarter, axis=1
+    )
+    valid = (own_segments != 0).astype(f32)[:, :, None]
+    (
+        result,
+        grad_mixture,
+        grad_middle,
+        entry_t,
+        grad_output_t,
+        active,
+        grad_hidden,
+        grad_out,
+        sums,
+        bias_sums,
+    ) = middle_call(
+        tensor_rank[None].astype(jnp.int32),
+        own_mixture,
+        tokens,
+        cotangent,
+        valid,
+        mods,
+        b_up.astype(f32).reshape(tensor, 1, part_width),
+        b_down.astype(f32)[None, :],
+        out_weight,
+        up,
+        down,
+        tile=min(tile, 256),
+    )
+    block_out = lax.all_gather(result, "tensor", axis=1, tiled=True)
+    grad_mixture = lax.all_to_all(
+        grad_mixture.reshape(context * tensor, group, tile), everyone, 0, 0, tiled=True
+    )
+    middle_slice = lax.all_to_all(grad_middle, "tensor", 1, 2, tiled=True)
+    grad_up, grad_down = weights_call(entry_t, grad_output_t, active, grad_hidden)
+    grad_out = (
+        grad_out.astype(bf16)
+        .reshape(tensor, group, fsdp, depth // fsdp)
+        .transpose(0, 2, 1, 3)
+        .reshape(tensor * fsdp, group * (depth // fsdp) // part_width, part_width)
+    )
+    pieces = jnp.concatenate(
+        [
+            grad_up.reshape(tensor * fsdp, -1, part_width),
+            grad_down.reshape(tensor * fsdp, -1, part_width),
+            grad_out,
+        ],
+        axis=1,
+    )
+    pieces = lax.psum_scatter(pieces, both, scatter_dimension=0, tiled=True)[0]
+    pieces = lax.psum(pieces, "context").astype(f32)
+    rows = depth // fsdp
+    grad_w_up = pieces[:rows]
+    grad_w_down = pieces[rows : 2 * rows].T
+    grad_w_out = pieces[2 * rows :].reshape(group, depth // fsdp)
+
+    grad_query, grad_key, grad_value = attend_back_call(
+        ranges, told, keys, keys_t, values, mixture, grad_mixture, cosine, sine, tile, block
+    )
+    part, grad_qkv, entry_sums = entry_back_call(
+        grad_query, grad_key, grad_value, hat_t, scaling, gain_column, shift_column, qkv, context, tile
+    )
+    part = lax.psum_scatter(part, "tensor", scatter_dimension=1, tiled=True)
+    part = lax.all_to_all(part, "context", 0, 0, tiled=True)
+    grad_tokens = jnp.swapaxes(part.astype(f32) + middle_slice.astype(f32), 1, 2)
+
+    grad_qkv = (
+        grad_qkv.astype(bf16).reshape(3 * group, fsdp, depth // fsdp).transpose(1, 0, 2)
+    )
+    grad_qkv = lax.psum_scatter(grad_qkv, "fsdp", scatter_dimension=0, tiled=True)[0]
+    grad_qkv = lax.psum(grad_qkv, "context").astype(f32)
+    grad_w_qkv = (
+        grad_qkv.reshape(3, heads, HDIM, depth // fsdp).transpose(3, 1, 0, 2).reshape(-1, 3 * group)
+    )
+
+    entry_sums = jnp.sum(entry_sums, axis=2)
+    is_own = (jnp.arange(sequences) == context_rank).astype(f32)[:, None]
+    grad_mod = jnp.concatenate(
+        [
+            is_own * entry_sums[0],
+            is_own * (entry_sums[1] * gain_first),
+            sums[:, 0],
+            sums[:, 1],
+            sums[:, 2] * gain_second,
+            sums[:, 3],
+        ],
+        axis=1,
+    )
+    grad_mod = lax.dynamic_update_slice_in_dim(
+        jnp.zeros((fsdp * sequences, 6 * depth), f32), grad_mod, fsdp_rank * sequences, 0
+    )
+    (grad_mod, grad_gain_one, grad_gain_two, grad_b_up, grad_b_down) = lax.psum(
+        (
+            grad_mod,
+            entry_sums[1] * (1.0 + own_mods[1]),
+            jnp.sum(sums[:, 2] * (1.0 + local_mods[:, 4]), axis=0),
+            bias_sums.reshape(-1),
+            jnp.sum(sums[:, 4], axis=0),
+        ),
+        ("fsdp", "context", "tensor"),
+    )
+    grad_ada_b = jnp.sum(grad_mod, axis=0)
+    grad_ada_w = exact_transposed(embedding, grad_mod)
+    grad_before = silu_back(exact_against(grad_mod, ada_full))[0]
+    grad_table = exact_transposed(choose, grad_before)
+    return (
+        block_out,
+        grad_tokens,
+        grad_table,
+        grad_ada_w,
+        grad_ada_b,
+        grad_gain_one,
+        grad_w_qkv,
+        grad_w_out,
+        grad_gain_two,
+        grad_w_up,
+        grad_b_up,
+        grad_w_down,
+        grad_b_down,
+    )
+
+
 def normalize(operand):
     center = operand - jnp.mean(operand, axis=-1, keepdims=True)
     scaling = lax.rsqrt(jnp.mean(center * center, axis=-1, keepdims=True) + 1e-05)
@@ -63,13 +908,6 @@
         - jnp.mean(grad_hat, axis=-1, keepdims=True)
         - hatted * jnp.mean(grad_hat * hatted, axis=-1, keepdims=True)
     )
-
-
-def positions(segment):
-    indices = jnp.arange(segment.shape[0], dtype=jnp.int32)
-    change = jnp.concatenate([jnp.ones((1,), jnp.bool_), segment[1:] != segment[:-1]])
-    starts = lax.cummax(jnp.where(change, indices, 0), axis=0)
-    return indices - starts
 
 
 def angles_of(offsets, half_width):
@@ -119,7 +957,7 @@
     return (chances.astype(jnp.bfloat16), grad_scores, row_delta)
 
 
-def local(
+def by_block(
     tokens,
     cotangent,
     segments,
@@ -370,6 +1208,17 @@
 
 
 def solution(mesh):
+    axes = dict(zip(mesh.axis_names, mesh.devices.shape))
+
+    def whole(tokens, *others):
+        sequences = tokens.shape[0] // axes["fsdp"]
+        local = by_sequence if sequences == axes["context"] == 2 else by_block
+        return mapped(local, mesh)(tokens, *others)
+
+    return whole
+
+
+def mapped(local, mesh):
     return jax.shard_map(
         local,
         mesh=mesh,

time: 1710 us -> 852 us (0.50)
  matrix products: 573 us -> 7.2 us
  other arithmetic: 354 us -> 30 us
  waiting for transfers between devices: 614 us -> 399 us
  Pallas kernels: 0 us -> 211 us
  blocking collectives: 80.5 us -> 125 us
    dot_general x36 -> x0, matrix products: 566 us -> none  [the longest x2 132 us: attend_back(): jnp.einsum('qhd,khd->hqk', grad_mixture, values, preferred_element_type=j...]
    psum x6 -> x2, waiting for transfers between devices: 547 us -> 106 us  [the longest x1 69.1 us: by_sequence(): lax.psum((grad_mod, entry_sums[1] * (1.0 + own_mods[1]), jnp.sum(sums[:,...]
    pallas_call x0 -> x7, Pallas kernels: none -> 211 us  [the longest x1 82 us: attend_back_call(): pl.pallas_call(partial(attend_back_kernel, block=block), grid_spec=pltpu....]
    convert_element_type x19 -> x7, other arithmetic: 181 us -> 6.84 us  [the longest x1 3.46 us: by_sequence(): grad_out.astype(bf16).reshape(tensor, group, fsdp, depth // fsdp)]
    reduce_scatter x5 -> x3, waiting for transfers between devices: 14.1 us -> 147 us  [the longest x1 121 us: by_sequence(): pieces = lax.psum_scatter(pieces, both, scatter_dimension=0, tiled=True)[0]]
    reduce_sum x9 -> x5, other arithmetic: 99.4 us -> 1.15 us  [the longest x1 0.68 us: by_sequence(): grad_ada_b = jnp.sum(grad_mod, axis=0)]
    all_to_all x0 -> x2, blocking collectives: none -> 51.7 us  [the longest x1 26.2 us: by_sequence(): middle_slice = lax.all_to_all(grad_middle, 'tensor', 1, 2, tiled=True)]
    all_gather x4 -> x5, waiting for transfers between devices: 52.1 us -> 103 us  [the longest x1 58.4 us: by_sequence(): lax.all_gather(w_down.T, both, axis=0, tiled=True)]
  transfers between devices with their start and end apart: 16 -> 13, of which waited for: 9 -> 8; matrix products, arithmetic and copies ran while one was open for 31% -> 8% of each run, Pallas kernels for 0% -> 8%
where the time goes in v1:
time: 852 us; the launch traced here: 848 us
  waiting for transfers between devices  399 us (47%)
  Pallas kernels  211 us (25%)
  blocking collectives  125 us (15%)
  local copies, waits for them, and re-layouts  46.4 us (5%)
  other arithmetic  30 us (4%)
  between operations  16.4 us (2%)
  starting transfers between devices  13 us (2%)
    reduce_scatter x1, waiting for transfers between devices, by_sequence(): pieces = lax.psum_scatter(pieces, both, scatter_dimension=0, tiled=True)[0]  121 us
    pallas_call x1, Pallas kernels, attend_back_call(): pl.pallas_call(partial(attend_back_kernel, block=block), grid_spec=pltpu....  82 us
    psum x1, waiting for transfers between devices, by_sequence(): lax.psum((grad_mod, entry_sums[1] * (1.0 + own_mods[1]), jnp.sum(sums[:,...  69.1 us
    all_gather x1, waiting for transfers between devices, by_sequence(): lax.all_gather(w_down.T, both, axis=0, tiled=True)  58.4 us
    psum x1, blocking collectives, by_sequence(): lax.psum((grad_mod, entry_sums[1] * (1.0 + own_mods[1]), jnp.sum(sums[:,...  45.7 us
    all_gather x1, waiting for transfers between devices, by_sequence(): block_out = lax.all_gather(result, 'tensor', axis=1, tiled=True)  45 us
    pallas_call x1, Pallas kernels, middle_call(): pl.pallas_call(middle_kernel, grid_spec=pltpu.PrefetchScalarGridSpec(num_...  41 us
    psum x1, waiting for transfers between devices, by_sequence(): grad_qkv = lax.psum(grad_qkv, 'context').astype(f32)  36.4 us
  transfers between devices with their start and end apart: 13, of which 8 were waited for; matrix products, arithmetic and copies ran while one was open for 8% of the time, Pallas kernels for 8%

profile of v1, /device:TPU:0, one launch (start us, length us, event | category | flops | bytes accessed | tf_op | source)
XLA Modules:
  0.0 848.0 jit_solution(13929487595534691940)
XLA Ops:
  7.3 1.5 constant_dynamic-slice_fusion
  8.8 3.0 collective-permute-start
  11.8 17.5 %collective-permute-done = bf16[1,512,768]{2,1,0:T(8,128)(2,1)S(1)} collective-permute-done((bf16[1,512,768]{2,1,0:T(8,128)(2,1)S(1)}, bf16[1,512,768]{2,1,0:T(8,128)(2,1)S(1)}, u32[]{:S(2)}, u32[]{:S(2)}) %collective-permute-start) | collective-permute-done | bytes 786464 | tf_op jit(solution)/shard_map/ppermute | solution.py:695
  33.9 8.7 %all-reduce = s32[8]{0:T(128)S(1)} all-reduce(s32[8]{0:T(128)S(1)} %dynamic-update-slice), channel_id=1, replica_groups=mesh['fsdp'=4,'context'=2,'tensor'=4] {'fsdp'}, use_global_device_ids=true, to_apply=%add | all-reduce | flops 8 | bytes 64
  44.4 0.9 copy.101.shift_ref
  45.7 19.4 %all_gather.26.weight_ref = bf16[768,576]{1,0:T(8,128)(2,1)S(1)} all-gather(bf16[192,576]{1,0:T(8,128)(2,1)S(1)} %copy.96), channel_id=1, replica_groups=mesh['fsdp'=4,'context'=2,'tensor'=4] {'fsdp'}, dimensions={0}, use_global_device_ids=true | all-gather | bytes 1105920 | tf_op jit(solution)/shard_map/all_gather | solution.py:703
  65.1 1.3 copy.102.weight_ref
  67.5 2.8 multiply_sine_fusion
  70.3 10.6 %entry.2 = (bf16[3,128,4096]{2,1,0:T(8,128)(2,1)}, bf16[3,4096,128]{2,1,0:T(8,128)(2,1)}, bf16[3,64,4096]{2,1,0:T(8,128)(2,1)}, bf16[3,4096,128]{2,1,0:T(8,128)(...) custom-call(s32[2]{0:T(128)} %pad_add_fusion.1.base_ref, ...), custom_call_target="tpu_custom_call" | custom-call | tf_op jit(solution)/shard_map/entry/pallas_call | solution.py:190
  81.6 10.7 %entry.3 = (bf16[3,128,4096]{2,1,0:T(8,128)(2,1)}, bf16[3,4096,128]{2,1,0:T(8,128)(2,1)}, bf16[3,64,4096]{2,1,0:T(8,128)(2,1)}, bf16[3,4096,128]{2,1,0:T(8,128)(...) custom-call(s32[2]{0:T(128)} %pad_add_fusion.base_ref, ...), custom_call_target="tpu_custom_call", output_to_operand_aliasing={{0}: (8, {}), {1}: (9, {}), {2}: (10, {}), {3}: (11, {}), {... | custom-call | tf_op jit(solution)/shard_map/entry/pallas_call | solution.py:190
  92.3 1.1 reduce_max.28
  95.5 33.0 %attend.1 = (bf16[8,192,512]{2,1,0:T(8,128)(2,1)}, bf16[3,128,4096]{2,1,0:T(8,128)(2,1)}) custom-call(s32[3,8]{1,0:T(4,128)} %add_add_fusion.range_ref, bf16[3,128,4096]{2,1,0:T(8,128)(2,1)} %get-tuple-element.58.query_ref, bf16[3,4096,128]{2,1,0:T(8,128)(2,1)} %get-tuple-element.59.key_ref, bf16[3,80,4096]{2,1,0:T(8,128)(2,1)} %get-tuple-element.60.value_ref), custom_call_target="tpu_custom_call" | custom-call | tf_op jit(solution)/shard_map/attend/pallas_call | solution.py:274
  128.4 4.5 all-to-all-start
  133.3 1.0 copy.104.valid_ref
  136.3 2.6 copy.123
  138.9 2.3 reshape.150.out_weight_ref
  141.1 22.5 %all-to-all-done = bf16[8,192,512]{2,1,0:T(8,128)(2,1)} async-done(((bf16[8,192,512]{2,1,0:T(8,128)(2,1)}), bf16[8,192,512]{2,1,0:T(8,128)(2,1)}, u32[]{:S(2)}, u32[]{:S(2)}) %all-to-all-start) | async-done | bytes 1572896 | tf_op jit(solution)/shard_map/all_to_all | solution.py:774
  163.6 58.4 %all-gather.11.cloned.1.call-done = bf16[3072,768]{1,0:T(8,128)(2,1)} async-done(((bf16[192,768]{1,0:T(8,128)(2,1)}), bf16[3072,768]{1,0:T(8,128)(2,1)}) %all-gather.11.cloned.1.call-update) | async-done | bytes 4718608 | tf_op jit(solution)/shard_map/all_gather | solution.py:706
  222.1 41.0 %middle.1 = (bf16[2,512,768]{2,1,0:T(8,128)(2,1)}, bf16[2,768,512]{2,1,0:T(8,128)(2,1)}, bf16[2,768,512]{2,1,0:T(8,128)(2,1)}, bf16[768,1024]{1,0:T(8,128)(2,1)}...) custom-call(s32[1]{0:T(128)} %bitcast.base_ref, ...), custom_call_target="tpu_custom_call" | custom-call | tf_op jit(solution)/shard_map/middle/pallas_call | solution.py:519
  263.1 25.5 %all_to_all.24.grad_ref = bf16[8,192,512]{2,1,0:T(8,128)(2,1)} all-to-all(bf16[8,192,512]{2,1,0:T(8,128)(2,1)} %bitcast.92), channel_id=1, replica_groups=mesh['fsdp'=4,'context'=2,'tensor'=4] {'context','tensor'}, dimensions={0} | all-to-all | bytes 3145728 | tf_op jit(solution)/shard_map/all_to_all | solution.py:807
  288.6 82.0 %attend_back.1 = (bf16[192,4096]{1,0:T(8,128)(2,1)}, bf16[192,4096]{1,0:T(8,128)(2,1)}, bf16[192,4096]{1,0:T(8,128)(2,1)}) custom-call(s32[3,8]{1,0:T(4,128)} %add_add_fusion.range_ref, bf16[3,128,4096]{2,1,0:T(8,128)(2,1)} %get-tuple-element.63.query_ref, bf16[3,4096,128]{2,1,0:T(8,128)(2,1)} %get-tuple-element.59.key_ref, ...), custom_call_target="tpu_custom_call" | custom-call | tf_op jit(solution)/shard_map/attend_back/pallas_call | solution.py:384
  370.6 18.2 %entry_back.1 = (bf16[2,768,2048]{2,1,0:T(8,128)(2,1)}, f32[576,768]{1,0:T(8,128)}, f32[2,768,128]{2,1,0:T(8,128)}) custom-call(bf16[192,4096]{1,0:T(8,128)(2,1)} %get-tuple-element.67.grad_query_ref, bf16[192,4096]{1,0:T(8,128)(2,1)} %get-tuple-element.68.grad_key_ref, bf16[192,4096]{1,0:T(8,128)(2,1)} %get-tuple-element.69.grad_value_ref, ...), custom_call_target="tpu_custom_call" | custom-call | tf_op jit(solution)/shard_map/entry_back/pallas_call | solution.py:636
  391.3 2.1 convert_element_type.68
  393.4 1.3 copy.113
  394.8 3.5 convert_element_type.69
  398.3 3.5 reshape.160
  401.8 1.4 copy.116
  403.2 3.1 reshape.161
  406.3 15.4 %weights.1 = (bf16[4,768,768]{2,1,0:T(8,128)(2,1)}, bf16[4,768,768]{2,1,0:T(8,128)(2,1)}) custom-call(bf16[768,1024]{1,0:T(8,128)(2,1)} %get-tuple-element.77.entry_ref, bf16[768,1024]{1,0:T(8,128)(2,1)} %get-tuple-element.78.grad_output_ref, bf16[4,1024,768]{2,1,0:T(8,128)(2,1)} %get-tuple-element.79.active_ref, ...), custom_call_target="tpu_custom_call" | custom-call | tf_op jit(solution)/shard_map/weights/pallas_call | solution.py:575
  421.7 9.2 %pad_maximum_fusion = bf16[16,432,768]{2,1,0:T(8,128)(2,1)} fusion(bf16[16,48,768]{2,1,0:T(8,128)(2,1)S(1)} %reshape.161, bf16[16,192,768]{2,1,0:T(8,128)(2,1)} %bitcast.89, bf16[16,192,768]{2,1,0:T(8,128)(2,1)} %bitcast.88), kind=kLoop, calls=%fused_computation | loop fusion | flops 31850496 | bytes 21233664 | tf_op jit(solution)/shard_map/concatenate | solution.py:818
  432.4 1.6 copy.107
  434.0 26.2 %all_to_all.25 = bf16[2,768,512]{2,0,1:T(2,128)(2,1)S(1)} all-to-all(bf16[2,768,512]{2,0,1:T(2,128)(2,1)S(1)} %copy.107), channel_id=1, replica_groups=mesh['fsdp'=4,'context'=2,'tensor'=4] {'tensor'}, dimensions={1} | all-to-all | bytes 3145728 | tf_op jit(solution)/shard_map/all_to_all | solution.py:810
  460.2 4.6 all-to-all-start.2
  464.9 2.9 copy.122
  467.8 5.3 reshape.169
  473.1 45.7 %all-reduce.1 = (f32[768]{0:T(1024)}, f32[768]{0:T(1024)}, f32[3072]{0:T(1024)}, f32[768]{0:T(1024)}) all-reduce(f32[768]{0:T(1024)S(1)} %get-tuple-element.145, f32[768]{0:T(1024)S(1)} %get-tuple-element.136, f32[3072]{0:T(1024)S(1)} %bitcast.102, ...), channel_id=1, replica_groups=mesh['fsdp'=4,'context'=2,'tensor'=4] {'fsdp','context','tensor'}, use_global_device_ids=true, to_apply=%region_10.11 | all-reduce | flops 5376 | bytes 43008 | tf_op jit(solution)/shard_map/psum | solution.py:868
  518.7 69.1 %all-reduce.6.cloned.1.call-done = f32[8,4608]{1,0:T(8,128)} async-done(((f32[8,4608]{1,0:T(8,128)}), f32[8,4608]{1,0:T(8,128)}) %all-reduce.6.cloned.1.call-update) | async-done | bytes 147472 | tf_op jit(solution)/shard_map/psum | solution.py:868
  587.8 4.4 fusion.14
  592.3 26.1 %reduce-scatter.6.cloned.1.call-done = bf16[1,576,192]{1,2,0:T(8,128)(2,1)} async-done(((bf16[4,576,192]{1,2,0:T(8,128)(2,1)}), bf16[1,576,192]{1,2,0:T(8,128)(2,1)}) %reduce-scatter.6.cloned.1.call-update) | async-done | bytes 221200 | tf_op jit(solution)/shard_map/reduce_scatter | solution.py:846
  618.4 1.1 copy.114
  620.2 121.0 %reduce-scatter.8.cloned.1.call-done = bf16[1,432,768]{2,1,0:T(8,128)(2,1)} async-done(((bf16[16,432,768]{2,1,0:T(8,128)(2,1)}), bf16[1,432,768]{2,1,0:T(8,128)(2,1)}) %reduce-scatter.8.cloned.1.call-update) | async-done | bytes 663568 | tf_op jit(solution)/shard_map/reduce_scatter | solution.py:826
  741.3 1.0 fusion.24
  743.0 1.0 fusion
  744.0 45.0 %all-gather.13.cloned.1.call-done = bf16[2,2048,768]{2,1,0:T(8,128)(2,1)} async-done(((bf16[2,512,768]{2,1,0:T(8,128)(2,1)}), bf16[2,2048,768]{2,1,0:T(8,128)(2,1)}) %all-gather.13.cloned.1.call-update) | async-done | bytes 6291472 | tf_op jit(solution)/shard_map/all_gather | solution.py:806
  789.0 4.6 add_bitcast_fusion
  793.6 36.4 %all-reduce.8.cloned.1.call-done = (bf16[192,576]{0,1:T(8,128)(2,1)}, bf16[432,768]{1,0:T(8,128)(2,1)}) async-done(((bf16[192,576]{0,1:T(8,128)(2,1)}, bf16[432,768]{1,0:T(8,128)(2,1)}), (bf16[192,576]{0,1:T(8,128)(2,1)}, bf16[432,768]{1,0:T(8,128)(2,1)})) %all-reduce.8.cloned.1.call-update) | async-done | bytes 884752 | tf_op jit(solution)/shard_map/psum | solution.py:847
  830.1 1.3 convert_element_type.70
  834.8 5.9 copy.143
  (128 shorter events, 20.3 us)
Async XLA Ops:
  7.2 35.6 %copy-start = (bf16[128,4608]{1,0:T(8,128)(2,1)S(1)}, bf16[128,4608]{1,0:T(8,128)(2,1)}, u32[]{:S(2)}) copy-start(bf16[128,4608]{1,0:T(8,128)(2,1)} %param.20) | copy-start | bytes 3538948
  7.2 25.2 %copy-start.21 = (u32[32]{0:T(128)S(1)}, u32[32]{0:T(128)}, u32[]{:S(2)}) copy-start(u32[32]{0:T(128)} %constant.118) | copy-start | bytes 388
  7.2 26.4 %copy-start.20 = (s32[2]{0:T(128)S(1)}, s32[2]{0:T(128)}, u32[]{:S(2)}) copy-start(s32[2]{0:T(128)} %param.18) | copy-start | bytes 28
  7.2 35.3 %copy-start.14 = (bf16[4608]{0:T(1024)(128)(2,1)S(1)}, bf16[4608]{0:T(1024)(128)(2,1)}, u32[]{:S(2)}) copy-start(bf16[4608]{0:T(1024)(128)(2,1)} %param.21) | copy-start | bytes 27652
  7.2 35.3 %copy-start.19 = (bf16[256,128]{1,0:T(8,128)(2,1)S(1)}, bf16[256,128]{1,0:T(8,128)(2,1)}, u32[]{:S(2)}) copy-start(bf16[256,128]{1,0:T(8,128)(2,1)} %param.19) | copy-start | bytes 196612
  7.2 74.4 %all-gather.7.cloned.1.call-start = ((), (), s32[]{:S(2)}) async-start(), calls=%async_computation.7 | async-start | bytes 3932160 | tf_op jit(solution)/shard_map/all_gather | solution.py:700
  7.3 36.1 %copy-start.15 = (bf16[768]{0:T(1024)(128)(2,1)S(1)}, bf16[768]{0:T(1024)(128)(2,1)}, u32[]{:S(2)}) copy-start(bf16[768]{0:T(1024)(128)(2,1)} %param.22) | copy-start | bytes 4612
  8.8 36.6 %copy-start.10 = (bf16[192,576]{1,0:T(8,128)(2,1)S(1)}, bf16[192,576]{1,0:T(8,128)(2,1)}, u32[]{:S(2)}) copy-start(bf16[192,576]{1,0:T(8,128)(2,1)} %param.23) | copy-start | bytes 663556
  8.8 20.6 %collective-permute-start = (bf16[1,512,768]{2,1,0:T(8,128)(2,1)S(1)}, bf16[1,512,768]{2,1,0:T(8,128)(2,1)S(1)}, u32[]{:S(2)}, u32[]{:S(2)}) collective-permute-start(bf16[1,512,768]{2,1,0:T(8,128)(2,1)S(1)} %constant_dynamic-slice_fusion), channel_id=1, source_target_pairs={{0,4},{4,0},{1,5},{5,1},{2,6},{6,2},{3,7},{7,3},{8,12},{12,8},{9,1... | collective-permute-start | bytes 2359304 | tf_op jit(solution)/shard_map/ppermute | solution.py:695
  29.4 0.9 copy-start.5
  30.3 105.9 %all-gather.15.cloned.1.call-start = ((), (), s32[]{:S(2)}) async-start(), calls=%async_computation.15 | async-start | bytes 1671168 | tf_op jit(solution)/shard_map/all_gather | solution.py:708
  31.1 132.6 %all-gather.9.cloned.1.call-start = ((), (), s32[]{:S(2)}) async-start(), calls=%async_computation.8 | async-start | bytes 5013504 | tf_op jit(solution)/shard_map/all_gather | solution.py:705
  31.8 190.3 %all-gather.11.cloned.1.call-start = ((), (), s32[]{:S(2)}) async-start(), calls=%async_computation.9 | async-start | bytes 5013504 | tf_op jit(solution)/shard_map/all_gather | solution.py:706
  45.3 21.0 %copy-start.12 = (s32[2,4096]{1,0:T(2,128)S(1)}, s32[2,4096]{1,0:T(2,128)}, u32[]{:S(2)}) copy-start(s32[2,4096]{1,0:T(2,128)} %param.17) | copy-start | bytes 98308
  65.1 15.9 %copy-start.1 = (bf16[768,576]{1,0:T(8,128)(2,1)}, bf16[768,576]{1,0:T(8,128)(2,1)S(1)}, u32[]{:S(2)}) copy-start(bf16[768,576]{1,0:T(8,128)(2,1)S(1)} %all_gather.26.weight_ref) | copy-start | bytes 2654212
  66.4 3.9 copy-start.8
  128.4 4.8 copy-start.17
  128.4 5.9 copy-start.16
  128.4 6.5 copy-start.18
  128.4 35.2 %all-to-all-start = ((bf16[8,192,512]{2,1,0:T(8,128)(2,1)}), bf16[8,192,512]{2,1,0:T(8,128)(2,1)}, u32[]{:S(2)}, u32[]{:S(2)}) async-start(bf16[8,192,512]{2,1,0:T(8,128)(2,1)} %get-tuple-element.61.mixture_ref), calls=%async_computation | async-start | bytes 3145728 | tf_op jit(solution)/shard_map/all_to_all | solution.py:774
  133.0 327.2 %reduce-scatter.4.cloned.1.call-start = ((), (), s32[]{:S(2)}) async-start(), calls=%async_computation.11 | async-start | bytes 7864320 | tf_op jit(solution)/shard_map/reduce_scatter | solution.py:839
  388.8 0.8 copy-start.11
  388.8 1.2 copy-start.6
  388.9 199.0 %all-reduce.6.cloned.1.call-start = ((), (), s32[]{:S(2)}) async-start(), calls=%async_computation.12 | async-start | bytes 294912 | tf_op jit(solution)/shard_map/psum | solution.py:868
  390.6 0.7 copy-start.7
  391.2 227.1 %reduce-scatter.6.cloned.1.call-start = ((), (), s32[]{:S(2)}) async-start(), calls=%async_computation.13 | async-start | bytes 1228800 | tf_op jit(solution)/shard_map/reduce_scatter | solution.py:846
  394.8 346.5 %reduce-scatter.8.cloned.1.call-start = ((), (), s32[]{:S(2)}) async-start(), calls=%async_computation.14 | async-start | bytes 11280384 | tf_op jit(solution)/shard_map/reduce_scatter | solution.py:826
  431.0 1.4 copy-start.3
  431.0 358.0 %all-gather.13.cloned.1.call-start = ((), (), s32[]{:S(2)}) async-start(), calls=%async_computation.10 | async-start | bytes 7864320 | tf_op jit(solution)/shard_map/all_gather | solution.py:806
  460.2 328.8 %all-to-all-start.2 = ((bf16[2,192,2048]{2,1,0:T(8,128)(2,1)}), bf16[2,192,2048]{2,1,0:T(8,128)(2,1)}, u32[]{:S(2)}, u32[]{:S(2)}) async-start(bf16[2,192,2048]{2,1,0:T(8,128)(2,1)} %reduce-scatter.4.cloned.1.call-done), calls=%async_computation.3 | async-start | bytes 3145728 | tf_op jit(solution)/shard_map/all_to_all | solution.py:840
  464.8 365.2 %all-reduce.8.cloned.1.call-start = ((), (), s32[]{:S(2)}) async-start(), calls=%async_computation.16 | async-start | bytes 1916928 | tf_op jit(solution)/shard_map/psum | solution.py:847
  467.8 5.3 copy-start.13
  587.8 153.4 %copy-start.4 = (f32[8,4608]{1,0:T(8,128)S(1)}, f32[8,4608]{1,0:T(8,128)}, u32[]{:S(2)}) copy-start(f32[8,4608]{1,0:T(8,128)} %all-reduce.6.cloned.1.call-done) | copy-start | bytes 442372
  830.1 1.3 copy-start.2
  830.1 3.0 copy-start.9
Sparse Core Ops, SparseCore 0:
  30.4 29.9 all-gather.6
  62.8 39.7 all-gather.14
  104.9 57.3 all-gather.8
  164.4 57.6 all-gather.10
  389.0 59.7 reduce-scatter.3
  455.7 132.1 all-reduce.5
  590.3 28.0 reduce-scatter.5
  622.4 118.7 reduce-scatter.7
  742.8 46.1 all-gather.12
  791.8 38.2 all-reduce.7

commit v2 on v1

--- a/solution.py
+++ b/solution.py
@@ -17,6 +17,12 @@
 SAFE_EXPONENT = 60.0
 EPSILON = 1e-05
 VMEM = 56 * 2**20
+VMEM_MOST = 60 * 2**20
+
+
+def cost(flops, *arrays):
+    size = sum(math.prod(one.shape) * one.dtype.itemsize for one in arrays)
+    return pl.CostEstimate(flops=int(flops), bytes_accessed=int(size), transcendentals=0)
 
 
 precise = lax.Precision.HIGHEST
@@ -195,6 +201,7 @@
         out_shape=shapes,
         input_output_aliases=aliases,
         compiler_params=pltpu.CompilerParams(vmem_limit_bytes=VMEM),
+        cost_estimate=cost(2 * rows.shape[1] * depth * width, rows, weight, *shapes),
         name="entry",
     )(jnp.stack([base, row_index]).astype(jnp.int32), *operands)
 
@@ -295,6 +302,7 @@
             jax.ShapeDtypeStruct((heads, WIDE, length), bf16),
         ],
         compiler_params=pltpu.CompilerParams(vmem_limit_bytes=VMEM),
+        cost_estimate=cost(4 * heads * length * length * WIDE, queries, keys, values_t),
         name="attend",
     )(ranges, queries, keys, values_t)
 
@@ -410,12 +418,30 @@
         ),
         out_shape=[jax.ShapeDtypeStruct((group, length), bf16)] * 3,
         compiler_params=pltpu.CompilerParams(vmem_limit_bytes=VMEM),
+        cost_estimate=cost(10 * heads * length * length * WIDE, queries, keys, values),
         name="attend_back",
     )(ranges, queries, keys, keys_t, values, mixture, grad_mixture, cosine, sine)
 
 
+def copy_to(source, target, sent, arrived, **device):
+    return pltpu.make_async_remote_copy(
+        src_ref=source,
+        dst_ref=target,
+        send_sem=sent,
+        recv_sem=arrived,
+        device_id=device,
+        device_id_type=pl.DeviceIdType.MESH,
+    )
+
+
+def greet(devices):
+    barrier = pltpu.get_barrier_semaphore()
+    for device in devices:
+        pl.semaphore_signal(barrier, inc=1, device_id=device, device_id_type=pl.DeviceIdType.MESH)
+    pl.semaphore_wait(barrier, len(devices))
+
+
 def middle_kernel(
-    base_ref,
     mixture_ref,
     rows_ref,
     cotangent_ref,
@@ -429,163 +455,425 @@
     result_ref,
     grad_mixture_ref,
     grad_middle_ref,
-    entry_ref,
-    grad_output_ref,
-    active_ref,
-    grad_hidden_ref,
     grad_out_ref,
     sums_ref,
     bias_sums_ref,
+    up_keep_ref,
+    up_send_ref,
+    down_keep_ref,
+    down_send_ref,
+    own_mixture,
+    entry_rows,
+    entry_columns,
+    grad_output_rows,
+    grad_output_columns,
+    attended_rows,
+    output_rows,
+    grad_entry_rows,
+    active,
+    grad_hidden,
+    grad_staged,
+    to_sibling,
+    from_sibling,
+    staged_up,
+    staged_down,
+    sent_mixture,
+    got_mixture,
+    own_copied,
+    sent_grad,
+    got_grad,
+    grad_copied,
+    sent_part,
+    got_part,
+    kept,
+    *,
+    tile,
+    tiles,
+    parts,
 ):
-    del base_ref
-    sequence, step = pl.program_id(0), pl.program_id(1)
-    mods = mod_ref[0]
-    gate_one, shift_two, gain_two, gate_two = (mods[k : k + 1] for k in range(4))
-    mixture_t = mixture_ref[0]
-    inputs = rows_ref[0].astype(f32)
-    attended = product(mixture_t.T, out_weight_ref[...])
-    middle = inputs + gate_one * attended
-    center = middle - jnp.mean(middle, axis=-1, keepdims=True)
-    scaling = lax.rsqrt(jnp.mean(center * center, axis=-1, keepdims=True) + EPSILON)
-    hat = center * scaling
-    entry = (hat * gain_two + shift_two).astype(bf16)
-    grad_result = cotangent_ref[0].astype(f32) * valid_ref[0]
-    grad_output = (gate_two * grad_result).astype(bf16)
-    entry_ref[...] = entry.T
-    grad_output_ref[...] = grad_output.T
-
-    @pl.when((sequence == 0) & (step == 0))
-    def _():
+    step = pl.program_id(0)
+    context, tensor = lax.axis_index("context"), lax.axis_index("tensor")
+    ranks = 4
+    everyone = 2 * ranks
+    place = context * ranks + tensor
+    core = lax.rem(tensor, 2)
+    sibling = tensor + 1 - 2 * core
+    depth = rows_ref.shape[1]
+    group = depth // ranks
+    per_sequence = tiles // 2
+    per_part = tiles + 1
+    back_from = tiles + parts * per_part
+    root = math.sqrt(2.0 / math.pi)
+
+    def member(away):
+        other = lax.rem(place + away, everyone)
+        return other, {"context": other // ranks, "tensor": lax.rem(other, ranks)}
+
+    def mixture_copy(away):
+        other, device = member(away)
+        return copy_to(
+            mixture_ref.at[other],
+            own_mixture.at[place],
+            sent_mixture.at[away - 1],
+            got_mixture.at[lax.rem(place + everyone, everyone)],
+            **device,
+        )
+
+    def mixture_arrival(source):
+        return pltpu.make_async_remote_copy(
+            src_ref=mixture_ref.at[source],
+            dst_ref=own_mixture.at[source],
+            send_sem=sent_mixture.at[0],
+            recv_sem=got_mixture.at[source],
+            device_id={"tensor": sibling},
+            device_id_type=pl.DeviceIdType.MESH,
+        )
+
+    def own_copy():
+        return pltpu.make_async_copy(mixture_ref.at[place], own_mixture.at[place], own_copied)
+
+    def part_copy(slot):
+        return copy_to(
+            to_sibling, from_sibling.at[slot], sent_part.at[slot], got_part.at[slot], tensor=sibling
+        )
+
+    def gradient_lanes(at):
+        return pl.ds(pl.multiple_of(lax.rem(at, per_sequence) * tile, tile), tile)
+
+    def gradient_copy(at, rank):
+        return copy_to(
+            grad_staged.at[at, rank],
+            grad_mixture_ref.at[place, :, gradient_lanes(at)],
+            sent_grad.at[at, rank],
+            got_grad.at[place, lax.rem(at, per_sequence)],
+            context=at // per_sequence,
+            tensor=rank,
+        )
+
+    def gradient_own(at):
+        return pltpu.make_async_copy(
+            grad_staged.at[at, tensor],
+            grad_mixture_ref.at[place, :, gradient_lanes(at)],
+            grad_copied.at[lax.rem(at, per_sequence)],
+        )
+
+    def gradient_arrival(source, number):
+        return pltpu.make_async_remote_copy(
+            src_ref=grad_staged.at[0, 0],
+            dst_ref=grad_mixture_ref.at[source, :, pl.ds(number * tile, tile)],
+            send_sem=sent_grad.at[0, 0],
+            recv_sem=got_grad.at[source, number],
+            device_id={"tensor": sibling},
+            device_id_type=pl.DeviceIdType.MESH,
+        )
+
+    def kept_copies(slot):
+        if slot == 0:
+            return [
+                pltpu.make_async_copy(staged_up, up_send_ref, kept.at[0]),
+                pltpu.make_async_copy(staged_down.at[0], down_keep_ref.at[0], kept.at[1]),
+                pltpu.make_async_copy(staged_down.at[1], down_send_ref.at[0], kept.at[2]),
+            ]
+        return [
+            pltpu.make_async_copy(staged_up, up_keep_ref, kept.at[3]),
+            pltpu.make_async_copy(staged_down.at[0], down_keep_ref.at[1], kept.at[4]),
+            pltpu.make_async_copy(staged_down.at[1], down_send_ref.at[1], kept.at[5]),
+        ]
+
+    def tile_of(at):
+        sequence = at // per_sequence
+        rows = pl.ds(pl.multiple_of(at * tile, tile), tile)
+        mods = mod_ref[sequence]
+        lanes = gradient_lanes(at)
+        mixture_t = jnp.concatenate(
+            [own_mixture[sequence * ranks + rank, :, lanes] for rank in range(ranks)], axis=0
+        )
+        return rows, mixture_t, tuple(mods[k : k + 1] for k in range(4))
+
+    def normal(attended, gate_one):
+        middle = rows_ref[...].astype(f32) + gate_one * attended
+        center = middle - jnp.mean(middle, axis=-1, keepdims=True)
+        scaling = lax.rsqrt(jnp.mean(center * center, axis=-1, keepdims=True) + EPSILON)
+        return middle, center * scaling, scaling
+
+    @pl.when(step == 0)
+    def _():
+        own_copy().start()
+        greet([member(away)[1] for away in range(1, everyone)])
+        for away in range(1, everyone):
+            mixture_copy(away).start()
+        sums_ref[...] = jnp.zeros_like(sums_ref)
         bias_sums_ref[...] = jnp.zeros_like(bias_sums_ref)
         grad_out_ref[...] = jnp.zeros_like(grad_out_ref)
 
-    output = down_bias_ref[...]
-    grad_entry = 0.0
-    root = math.sqrt(2.0 / math.pi)
-    for part in range(up_ref.shape[0]):
-        hidden = product(entry, up_ref[part]) + up_bias_ref[part]
+    for sequence in range(2):
+
+        @pl.when(step == sequence * per_sequence)
+        def _():
+            for rank in range(ranks):
+                source = sequence * ranks + rank
+
+                @pl.when(place == source)
+                def _():
+                    own_copy().wait()
+
+                @pl.when(place != source)
+                def _():
+                    mixture_arrival(source).wait_recv()
+
+    @pl.when(step < tiles)
+    def _():
+        rows, mixture_t, (gate_one, shift_two, gain_two, gate_two) = tile_of(step)
+        attended = product(mixture_t.T, out_weight_ref[...])
+        attended_rows[rows, :] = attended
+        _, hat, _ = normal(attended, gate_one)
+        entry = (hat * gain_two + shift_two).astype(bf16)
+        grad_output = (gate_two * (cotangent_ref[...].astype(f32) * valid_ref[rows, :])).astype(bf16)
+        entry_rows[rows, :] = entry
+        entry_columns[:, rows] = entry.T
+        grad_output_rows[rows, :] = grad_output
+        grad_output_columns[:, rows] = grad_output.T
+        output_rows[rows, :] = jnp.broadcast_to(down_bias_ref[...], (tile, depth))
+        grad_entry_rows[rows, :] = jnp.zeros((tile, depth), f32)
+
+    inner = lax.rem(step - tiles, per_part)
+    position = (step - tiles) // per_part
+    in_parts = (step >= tiles) & (step < back_from)
+
+    @pl.when(in_parts & (inner < tiles))
+    def _():
+        rows = pl.ds(pl.multiple_of(inner * tile, tile), tile)
+        number = part_at(position, tensor)
+        hidden = product(entry_rows[rows, :], up_ref[0]) + up_bias_ref[0]
         square = hidden * hidden
         bent = jnp.tanh(root * hidden * (1.0 + 0.044715 * square))
         half = 0.5 * (1.0 + bent)
-        active = (hidden * half).astype(bf16)
+        activated = (hidden * half).astype(bf16)
         slope = half + (0.5 * root) * hidden * (1.0 - bent * bent) * (1.0 + 0.134145 * square)
-        grad_hidden_wide = product(grad_output, down_ref[part]) * slope
-        grad_hidden = grad_hidden_wide.astype(bf16)
-        output = output + against(active, down_ref[part])
-        grad_entry = grad_entry + against(grad_hidden, up_ref[part])
-        active_ref[part] = active
-        grad_hidden_ref[part] = grad_hidden
-        bias_sums_ref[part] += jnp.sum(grad_hidden.astype(f32), axis=0, keepdims=True)
-    result_ref[0] = (middle + gate_two * output).astype(bf16)
-    grad_lifted = grad_entry * gain_two
-    grad_middle = grad_result + scaling * (
-        grad_lifted
-        - jnp.mean(grad_lifted, axis=-1, keepdims=True)
-        - hat * jnp.mean(grad_lifted * hat, axis=-1, keepdims=True)
-    )
-    grad_attended = (gate_one * grad_middle).astype(bf16)
-    grad_mixture_ref[0] = against(out_weight_ref[...], grad_attended).astype(bf16)
-    grad_middle_ref[0] = grad_middle.T.astype(bf16)
-    grad_out_ref[...] += product(mixture_t, grad_attended)
-
-    @pl.when(step == 0)
-    def _():
-        sums_ref[...] = jnp.zeros_like(sums_ref)
-
-    rows = [
-        jnp.sum(grad_middle * attended, axis=0, keepdims=True),
-        jnp.sum(grad_entry, axis=0, keepdims=True),
-        jnp.sum(grad_entry * hat, axis=0, keepdims=True),
-        jnp.sum(grad_result * output, axis=0, keepdims=True),
-        jnp.sum(grad_output.astype(f32), axis=0, keepdims=True),
-    ]
-    rows += [jnp.zeros_like(rows[0])] * (sums_ref.shape[1] - len(rows))
-    sums_ref[0] += jnp.concatenate(rows, axis=0)
+        grads = (product(grad_output_rows[rows, :], down_ref[0]) * slope).astype(bf16)
+        output_rows[rows, :] += against(activated, down_ref[0])
+        grad_entry_rows[rows, :] += against(grads, up_ref[0])
+        active[rows, :] = activated
+        grad_hidden[rows, :] = grads
+        bias_sums_ref[number] += jnp.sum(grads.astype(f32), axis=0, keepdims=True)
+
+    for turn in range(parts):
+
+        @pl.when(step == tiles + turn * per_part + tiles)
+        def _():
+            slot = turn // 2
+            if turn % 2 == 0:
+                if slot:
+                    part_copy(0).wait_send()
+            else:
+                part_copy(slot).wait_recv()
+                if slot:
+                    for one in kept_copies(0):
+                        one.wait()
+            groups = up_keep_ref.shape[1]
+            height = depth // groups
+            for other in range(groups):
+                at = pl.ds(other * height, height)
+                up = product(entry_columns[at, :], grad_hidden[...])
+                down = product(grad_output_columns[at, :], active[...])
+                if turn % 2 == 0:
+                    to_sibling[0, at, :] = up.astype(bf16)
+                    to_sibling[1, at, :] = down.astype(bf16)
+                else:
+                    up = (up + from_sibling[slot, 0, at, :].astype(f32)).astype(bf16)
+                    down = (down + from_sibling[slot, 1, at, :].astype(f32)).astype(bf16)
+                    staged_up[context, other] = up[: height // 2]
+                    staged_up[1 - context, other] = up[height // 2 :]
+                    staged_down[context, other] = down[: height // 2]
+                    staged_down[1 - context, other] = down[height // 2 :]
+            if turn % 2 == 0:
+                part_copy(slot).start()
+            else:
+                for one in kept_copies(slot):
+                    one.start()
+
+    @pl.when(step >= back_from)
+    def _():
+        at = step - back_from
+        sequence = at // per_sequence
+        rows, mixture_t, (gate_one, _, gain_two, gate_two) = tile_of(at)
+        attended = attended_rows[rows, :]
+        middle, hat, scaling = normal(attended, gate_one)
+        output = output_rows[rows, :]
+        grad_entry = grad_entry_rows[rows, :]
+        grad_result = cotangent_ref[...].astype(f32) * valid_ref[rows, :]
+        result_ref[...] = (middle + gate_two * output).astype(bf16)
+        grad_lifted = grad_entry * gain_two
+        grad_middle = grad_result + scaling * (
+            grad_lifted
+            - jnp.mean(grad_lifted, axis=-1, keepdims=True)
+            - hat * jnp.mean(grad_lifted * hat, axis=-1, keepdims=True)
+        )
+        grad_attended = (gate_one * grad_middle).astype(bf16)
+        grad_mixture = against(out_weight_ref[...], grad_attended).astype(bf16)
+        for rank in range(ranks):
+            grad_staged[at, rank] = grad_mixture[rank * group : (rank + 1) * group]
+        for rank in range(ranks):
+            own = (sequence == context) & (tensor == rank)
+
+            @pl.when(own)
+            def _():
+                gradient_own(at).start()
+
+            @pl.when(jnp.logical_not(own))
+            def _():
+                gradient_copy(at, rank).start()
+
+        grad_middle_ref[0] = grad_middle.T.astype(bf16)
+        grad_out_ref[...] += product(mixture_t, grad_attended)
+        lines = [
+            jnp.sum(grad_middle * attended, axis=0, keepdims=True),
+            jnp.sum(grad_entry, axis=0, keepdims=True),
+            jnp.sum(grad_entry * hat, axis=0, keepdims=True),
+            jnp.sum(grad_result * output, axis=0, keepdims=True),
+            jnp.sum(grad_output_rows[rows, :].astype(f32), axis=0, keepdims=True),
+        ]
+        lines += [jnp.zeros_like(lines[0])] * (sums_ref.shape[1] - len(lines))
+        sums_ref[sequence] += jnp.concatenate(lines, axis=0)
+
+    @pl.when(step == back_from + tiles - 1)
+    def _():
+        for source in range(everyone):
+            for number in range(per_sequence):
+
+                @pl.when(place != source)
+                def _():
+                    gradient_arrival(source, number).wait_recv()
+
+        for at in range(tiles):
+            for rank in range(ranks):
+                own = (at // per_sequence == context) & (tensor == rank)
+
+                @pl.when(own)
+                def _():
+                    gradient_own(at).wait()
+
+                @pl.when(jnp.logical_not(own))
+                def _():
+                    gradient_copy(at, rank).wait_send()
+
+        for away in range(1, everyone):
+            mixture_copy(away).wait_send()
+        part_copy(1).wait_send()
+        for one in kept_copies(1):
+            one.wait()
+
+
+def part_at(position, tensor):
+    core = lax.rem(tensor, 2)
+    chip = tensor // 2
+    away = jnp.where(position < 2, 1 - chip, chip)
+    other = jnp.where(lax.rem(position, 2) == 0, 1 - core, core)
+    return away * 2 + other
 
 
 def middle_call(
-    base, mixture, rows, cotangent, valid, mods, up_bias, down_bias, out_weight, up, down, tile
+    mixture, rows, cotangent, valid, mods, up_bias, down_bias, out_weight, up, down, groups, tile
 ):
-    sequences, depth, own = mixture.shape
+    pieces, group, own = mixture.shape
+    tokens, depth = rows.shape
     parts, _, part_width = up.shape
-    steps = own // tile
-    tokens = sequences * own
-    at_rows = lambda s, i, b: (s, b[0] * steps + i, 0)
-    own_rows = lambda s, i, b: (s, i, 0)
-    own_lanes = lambda s, i, b: (s, 0, i)
-    whole2 = lambda s, i, b: (0, 0)
-    whole3 = lambda s, i, b: (0, 0, 0)
+    tiles = tokens // tile
+    per_sequence = tiles // 2
+    per_part = tiles + 1
+    back_from = tiles + parts * per_part
+    half = depth // groups // 2
+
+    def token_tile(i):
+        return jnp.where(i < tiles, i, jnp.where(i < back_from, 0, i - back_from)), 0
+
+    def part_block(i):
+        position = jnp.clip((i - tiles) // per_part, 0, parts - 1)
+        return part_at(position, lax.axis_index("tensor")), 0, 0
+
+    def back_tile(i):
+        return jnp.maximum(i - back_from, 0)
+
+    whole2 = lambda i: (0, 0)
+    whole3 = lambda i: (0, 0, 0)
     once = pl.Buffered(1)
+    hbm = pl.BlockSpec(memory_space=pl.ANY)
+    kept = jax.ShapeDtypeStruct((2, groups, half, part_width), bf16)
+    wide = (tokens, depth)
     return pl.pallas_call(
-        middle_kernel,
-        grid_spec=pltpu.PrefetchScalarGridSpec(
-            num_scalar_prefetch=1,
-            grid=(sequences, steps),
-            in_specs=[
-                pl.BlockSpec((1, depth, tile), own_lanes),
-                pl.BlockSpec((1, tile, depth), at_rows),
-                pl.BlockSpec((1, tile, depth), at_rows),
-                pl.BlockSpec((1, tile, 1), own_rows),
-                pl.BlockSpec((1, 8, depth), lambda s, i, b: (s, 0, 0)),
-                pl.BlockSpec((parts, 1, part_width), whole3, pipeline_mode=once),
-                pl.BlockSpec((1, depth), whole2, pipeline_mode=once),
-                pl.BlockSpec((depth, depth), whole2, pipeline_mode=once),
-                pl.BlockSpec((parts, depth, part_width), whole3, pipeline_mode=once),
-                pl.BlockSpec((parts, depth, part_width), whole3, pipeline_mode=once),
-            ],
-            out_specs=[
-                pl.BlockSpec((1, tile, depth), own_rows),
-                pl.BlockSpec((1, depth, tile), own_lanes),
-                pl.BlockSpec((1, depth, tile), own_lanes),
-                pl.BlockSpec((depth, tile), lambda s, i, b: (0, s * steps + i)),
-                pl.BlockSpec((depth, tile), lambda s, i, b: (0, s * steps + i)),
-                pl.BlockSpec((parts, tile, part_width), lambda s, i, b: (0, s * steps + i, 0)),
-                pl.BlockSpec((parts, tile, part_width), lambda s, i, b: (0, s * steps + i, 0)),
-                pl.BlockSpec((depth, depth), whole2),
-                pl.BlockSpec((1, 8, depth), lambda s, i, b: (s, 0, 0)),
-                pl.BlockSpec((parts, 1, part_width), whole3),
-            ],
+        partial(middle_kernel, tile=tile, tiles=tiles, parts=parts),
+        grid=(back_from + tiles,),
+        in_specs=[
+            hbm,
+            pl.BlockSpec((tile, depth), token_tile),
+            pl.BlockSpec((tile, depth), token_tile),
+            pl.BlockSpec((tokens, 1), whole2, pipeline_mode=once),
+            pl.BlockSpec(mods.shape, whole3, pipeline_mode=once),
+            pl.BlockSpec((1, 1, part_width), part_block),
+            pl.BlockSpec((1, depth), whole2, pipeline_mode=once),
+            pl.BlockSpec((depth, depth), whole2, pipeline_mode=once),
+            pl.BlockSpec((1, depth, part_width), part_block),
+            pl.BlockSpec((1, depth, part_width), part_block),
+        ],
+        out_specs=[
+            pl.BlockSpec((tile, depth), lambda i: (back_tile(i), 0)),
+            hbm,
+            pl.BlockSpec(
+                (1, depth, tile),
+                lambda i: (back_tile(i) // per_sequence, 0, lax.rem(back_tile(i), per_sequence)),
+            ),
+            pl.BlockSpec((depth, depth), whole2),
+            pl.BlockSpec((2, 8, depth), whole3),
+            pl.BlockSpec((parts, 1, part_width), whole3),
+            hbm,
+            hbm,
+            hbm,
+            hbm,
+        ],
+        out_shape=[
+            jax.ShapeDtypeStruct((tokens, depth), bf16),
+            jax.ShapeDtypeStruct(mixture.shape, bf16),
+            jax.ShapeDtypeStruct((2, depth, own), bf16),
+            jax.ShapeDtypeStruct((depth, depth), f32),
+            jax.ShapeDtypeStruct((2, 8, depth), f32),
+            jax.ShapeDtypeStruct((parts, 1, part_width), f32),
+            kept,
+            kept,
+            kept,
+            kept,
+        ],
+        scratch_shapes=[
+            pltpu.VMEM(mixture.shape, bf16),
+            pltpu.VMEM(wide, bf16),
+            pltpu.VMEM((depth, tokens), bf16),
+            pltpu.VMEM(wide, bf16),
+            pltpu.VMEM((depth, tokens), bf16),
+            pltpu.VMEM(wide, f32),
+            pltpu.VMEM(wide, f32),
+            pltpu.VMEM(wide, f32),
+            pltpu.VMEM((tokens, part_width), bf16),
+            pltpu.VMEM((tokens, part_width), bf16),
+            pltpu.VMEM((tiles, 4, group, tile), bf16),
+            pltpu.VMEM((2, depth, part_width), bf16),
+            pltpu.VMEM((2, 2, depth, part_width), bf16),
+            pltpu.VMEM((2, groups, half, part_width), bf16),
+            pltpu.VMEM((2, groups, half, part_width), bf16),
+            pltpu.SemaphoreType.DMA((pieces - 1,)),
+            pltpu.SemaphoreType.DMA((pieces,)),
+            pltpu.SemaphoreType.DMA,
+            pltpu.SemaphoreType.DMA((tiles, 4)),
+            pltpu.SemaphoreType.DMA((pieces, per_sequence)),
+            pltpu.SemaphoreType.DMA((per_sequence,)),
+            pltpu.SemaphoreType.DMA((2,)),
+            pltpu.SemaphoreType.DMA((2,)),
+            pltpu.SemaphoreType.DMA((6,)),
+        ],
+        compiler_params=pltpu.CompilerParams(
+            vmem_limit_bytes=VMEM_MOST, collective_id=2, has_side_effects=True
         ),
-        out_shape=[
-            jax.ShapeDtypeStruct((sequences, own, depth), bf16),
-            jax.ShapeDtypeStruct((sequences, depth, own), bf16),
-            jax.ShapeDtypeStruct((sequences, depth, own), bf16),
-            jax.ShapeDtypeStruct((depth, tokens), bf16),
-            jax.ShapeDtypeStruct((depth, tokens), bf16),
-            jax.ShapeDtypeStruct((parts, tokens, part_width), bf16),
-            jax.ShapeDtypeStruct((parts, tokens, part_width), bf16),
-            jax.ShapeDtypeStruct((depth, depth), f32),
-            jax.ShapeDtypeStruct((sequences, 8, depth), f32),
-            jax.ShapeDtypeStruct((parts, 1, part_width), f32),
-        ],
-        compiler_params=pltpu.CompilerParams(vmem_limit_bytes=VMEM),
+        cost_estimate=cost(6 * tokens * depth * (depth + 3 * parts * part_width), rows, up, down),
         name="middle",
-    )(base, mixture, rows, cotangent, valid, mods, up_bias, down_bias, out_weight, up, down)
-
-
-def weights_kernel(entry_ref, grad_output_ref, active_ref, grad_hidden_ref, grad_up_ref, grad_down_ref):
-    grad_up_ref[0] = product(entry_ref[...], grad_hidden_ref[0]).astype(bf16)
-    grad_down_ref[0] = product(grad_output_ref[...], active_ref[0]).astype(bf16)
-
-
-def weights_call(entry_t, grad_output_t, active, grad_hidden):
-    depth, tokens = entry_t.shape
-    parts, _, part_width = active.shape
-    part = lambda i: (i, 0, 0)
-    return pl.pallas_call(
-        weights_kernel,
-        grid=(parts,),
-        in_specs=[
-            pl.BlockSpec((depth, tokens), lambda i: (0, 0)),
-            pl.BlockSpec((depth, tokens), lambda i: (0, 0)),
-            pl.BlockSpec((1, tokens, part_width), part),
-            pl.BlockSpec((1, tokens, part_width), part),
-        ],
-        out_specs=[pl.BlockSpec((1, depth, part_width), part)] * 2,
-        out_shape=[jax.ShapeDtypeStruct((parts, depth, part_width), bf16)] * 2,
-        compiler_params=pltpu.CompilerParams(vmem_limit_bytes=VMEM),
-        name="weights",
-    )(entry_t, grad_output_t, active, grad_hidden)
+    )(mixture, rows, cotangent, valid, mods, up_bias, down_bias, out_weight, up, down)
 
 
 def entry_back_kernel(
@@ -597,45 +885,452 @@
     gain_ref,
     shift_ref,
     weight_ref,
-    part_ref,
+    middle_ref,
+    middle_in_ref,
+    small_ref,
+    up_ref,
+    down_ref,
+    grad_out_ref,
+    result_ref,
+    result_in_ref,
+    out_ref,
     grad_weight_ref,
-    sums_ref,
+    all_sums_ref,
+    all_small_ref,
+    pieces_ref,
+    grad_out_sum_ref,
+    block_ref,
+    up_own,
+    up_in,
+    down_own,
+    down_in,
+    slices,
+    slices_in,
+    context_slice,
+    context_in,
+    small_in,
+    small_sum,
+    small_groups,
+    out_in,
+    loaded,
+    sent_up,
+    got_up,
+    sent_down,
+    got_down,
+    sent_slice,
+    got_slice,
+    sent_context,
+    got_context,
+    sent_small,
+    got_small,
+    sent_sum,
+    got_sum,
+    sent_out,
+    got_out,
+    sent_result,
+    got_result,
+    moved,
+    weight_total,
+    sums,
+    part,
+    part_in,
+    pair,
+    pair_in,
+    chip,
+    chip_in,
+    piece,
+    piece_in,
+    block_piece,
+    block_in,
+    rank_sums,
+    rank_in,
+    group_sums,
+    group_in,
+    sent_part,
+    got_part,
+    sent_pair,
+    got_pair,
+    sent_chip,
+    got_chip,
+    sent_piece,
+    got_piece,
+    sent_block,
+    got_block,
+    sent_rank,
+    got_rank,
+    sent_group,
+    got_group,
+    *,
+    tiles,
+    groups,
 ):
-    @pl.when(pl.program_id(0) == 0)
-    def _():
-        grad_weight_ref[...] = jnp.zeros_like(grad_weight_ref)
-        sums_ref[...] = jnp.zeros_like(sums_ref)
-
-    grads = jnp.concatenate([grad_query_ref[...], grad_key_ref[...], grad_value_ref[...]], axis=0)
-    grad_entry = product(weight_ref[...], grads)
-    hat = hat_ref[...].astype(f32)
-    gain = gain_ref[...]
-    entry = (hat * gain + shift_ref[...]).astype(bf16)
-    grad_weight_ref[...] += against(grads, entry)
-    grad_lifted = grad_entry * gain
-    part_ref[0] = (
-        scale_ref[...]
-        * (
+    step = pl.program_id(0)
+    fsdp, context, tensor = (lax.axis_index(name) for name in ("fsdp", "context", "tensor"))
+    ranks = 4
+    half = tiles // 2
+    core = lax.rem(tensor, 2)
+    chip_x = tensor // 2
+    sibling = tensor + 1 - 2 * core
+    across = lax.rem(tensor + 2, ranks)
+    place = fsdp * 2 + context
+    depth = hat_ref.shape[0]
+    slice_rows = depth // ranks
+    weight_rows = depth // groups
+    everyone = groups * 2
+
+    def group_member(away):
+        other = lax.rem(place + away, everyone)
+        return {"fsdp": other // 2, "context": lax.rem(other, 2)}
+
+    def group_away(number):
+        return {"fsdp": lax.rem(fsdp + number // 2, groups), "context": number % 2}
+
+    plane = context * ranks + tensor
+    in_plane = 2 * ranks
+
+    def plane_member(away):
+        other = lax.rem(plane + away, in_plane)
+        return {"context": other // ranks, "tensor": lax.rem(other, ranks)}
+
+    def up_copy():
+        return copy_to(up_ref.at[1], up_in, sent_up, got_up, context=1 - context)
+
+    def down_copy():
+        return copy_to(down_ref.at[0], down_in, sent_down, got_down, tensor=across)
+
+    def loads():
+        return [
+            pltpu.make_async_copy(up_ref.at[0], up_own, loaded.at[0]),
+            pltpu.make_async_copy(down_ref.at[1], down_own, loaded.at[1]),
+        ]
+
+    def slice_copy(away):
+        other = lax.rem(fsdp + away, groups)
+        return copy_to(
+            slices.at[other],
+            slices_in.at[away - 1],
+            sent_slice.at[away - 1],
+            got_slice.at[away - 1],
+            fsdp=other,
+        )
+
+    def context_copy():
+        return copy_to(context_slice, context_in, sent_context, got_context, context=1 - context)
+
+    def small_copy(away):
+        return copy_to(
+            small_ref,
+            small_in.at[away - 1],
+            sent_small.at[away - 1],
+            got_small.at[away - 1],
+            **plane_member(away),
+        )
+
+    def sum_copy(away):
+        return copy_to(
+            small_sum,
+            small_groups.at[away - 1],
+            sent_sum.at[away - 1],
+            got_sum.at[away - 1],
+            fsdp=lax.rem(fsdp + away, groups),
+        )
+
+    def out_copy():
+        return copy_to(grad_out_ref, out_in, sent_out, got_out, context=1 - context)
+
+    quarter = result_ref.shape[1]
+
+    def result_places():
+        for number, (source, rank) in enumerate([(result_ref, tensor), (result_in_ref, across)]):
+            rows = pl.ds(pl.multiple_of(rank * quarter, quarter), quarter)
+            for sequence in range(2):
+                yield number * 2 + sequence, source.at[sequence], block_ref.at[sequence, rows, :]
+
+    def result_copies():
+        return [
+            copy_to(source, target, sent_result.at[k], got_result.at[k], tensor=sibling)
+            for k, source, target in result_places()
+        ]
+
+    def result_moves():
+        return [
+            pltpu.make_async_copy(source, target, moved.at[k]) for k, source, target in result_places()
+        ]
+
+    def part_copy(tile):
+        return copy_to(
+            part.at[tile, 1 - core], part_in.at[tile], sent_part.at[tile], got_part.at[tile], tensor=sibling
+        )
+
+    def pair_copy(tile):
+        return copy_to(
+            pair.at[tile, 1 - chip_x], pair_in.at[tile], sent_pair.at[tile], got_pair.at[tile], tensor=across
+        )
+
+    def chip_copy(tile):
+        return copy_to(
+            chip.at[tile], chip_in.at[tile], sent_chip.at[tile], got_chip.at[tile], context=1 - context
+        )
+
+    def piece_copy(away):
+        other = lax.rem(fsdp + away, groups)
+        return copy_to(
+            piece.at[other],
+            piece_in.at[away - 1],
+            sent_piece.at[away - 1],
+            got_piece.at[away - 1],
+            fsdp=other,
+        )
+
+    def block_copy():
+        return copy_to(block_piece, block_in, sent_block, got_block, context=1 - context)
+
+    def rank_copy(away):
+        return copy_to(
+            rank_sums,
+            rank_in.at[away - 1],
+            sent_rank.at[away - 1],
+            got_rank.at[away - 1],
+            tensor=lax.rem(tensor + away, ranks),
+        )
+
+    def group_copy(away):
+        return copy_to(
+            group_sums,
+            group_in.at[away - 1],
+            sent_group.at[away - 1],
+            got_group.at[away - 1],
+            **group_member(away),
+        )
+
+    @pl.when(step == 0)
+    def _():
+        greet(
+            [plane_member(away) for away in range(1, in_plane)]
+            + [group_away(away) for away in range(2, everyone)]
+        )
+        up_copy().start()
+        down_copy().start()
+        out_copy().start()
+        for away in range(1, in_plane):
+            small_copy(away).start()
+        for one in result_copies() + result_moves() + loads():
+            one.start()
+        weight_total[...] = jnp.zeros_like(weight_total)
+        sums[...] = jnp.zeros_like(sums)
+
+    def grads():
+        return jnp.concatenate([grad_query_ref[...], grad_key_ref[...], grad_value_ref[...]], axis=0)
+
+    @pl.when(step < tiles)
+    def _():
+        entry = (hat_ref[...].astype(f32) * gain_ref[...] + shift_ref[...]).astype(bf16)
+        weight_total[...] += against(entry, grads())
+
+    @pl.when(step == tiles - 1)
+    def _():
+        for other in range(groups):
+            piece[other] = weight_total[other * weight_rows : (other + 1) * weight_rows].astype(bf16)
+        for away in range(1, groups):
+            piece_copy(away).start()
+
+    @pl.when((step >= tiles) & (step < 2 * tiles))
+    def _():
+        tile = step - tiles
+        grad_entry = product(weight_ref[...], grads())
+        hat = hat_ref[...].astype(f32)
+        grad_lifted = grad_entry * gain_ref[...]
+        term = scale_ref[...] * (
             grad_lifted
             - jnp.mean(grad_lifted, axis=0, keepdims=True)
             - hat * jnp.mean(grad_lifted * hat, axis=0, keepdims=True)
         )
-    ).astype(bf16)
-    weighted = grad_entry * hat
-    for lane in range(0, grad_entry.shape[1], WIDE):
-        sums_ref[0] += grad_entry[:, lane : lane + WIDE]
-        sums_ref[1] += weighted[:, lane : lane + WIDE]
-
-
-def entry_back_call(grad_query, grad_key, grad_value, hat_t, scaling, gain, shift, weight, blocks, tile):
+        extra = jnp.where(tile < half, middle_in_ref[...], middle_ref[0]).astype(f32)
+        term = (term + jnp.where(lax.rem(tile, half) == tensor, extra, 0.0)).astype(bf16)
+        for rank in range(ranks):
+            part[tile, rank % 2, rank // 2] = term[rank * slice_rows : (rank + 1) * slice_rows]
+        part_copy(tile).start()
+        weighted = grad_entry * hat
+        for lane in range(0, grad_entry.shape[1], WIDE):
+            sums[0] += grad_entry[:, lane : lane + WIDE]
+            sums[1] += weighted[:, lane : lane + WIDE]
+
+    @pl.when((step >= tiles + 1) & (step < 2 * tiles + 1))
+    def _():
+        tile = step - tiles - 1
+        part_copy(tile).wait_recv()
+        pair[tile] = (part[tile, core].astype(f32) + part_in[tile].astype(f32)).astype(bf16)
+        pair_copy(tile).start()
+
+    @pl.when((step >= tiles + 2) & (step < 2 * tiles + 2))
+    def _():
+        tile = step - tiles - 2
+        pair_copy(tile).wait_recv()
+        total = (pair[tile, chip_x].astype(f32) + pair_in[tile].astype(f32)).astype(bf16)
+
+        @pl.when(tile < half)
+        def _():
+            chip[tile] = total
+            chip_copy(tile).start()
+
+        @pl.when(tile >= half)
+        def _():
+            out_ref[context, tile - half] = total
+
+    @pl.when((step >= tiles + 5) & (step < tiles + 5 + half))
+    def _():
+        tile = step - tiles - 5
+        chip_copy(tile).wait_recv()
+        out_ref[1 - context, tile] = chip_in[tile]
+
+    @pl.when(step == tiles)
+    def _():
+        for away in range(1, in_plane):
+            small_copy(away).wait_recv()
+        small_sum[...] = ordered_sum(small_ref[...], [small_in[k] for k in range(in_plane - 1)], plane)
+        for away in range(1, groups):
+            sum_copy(away).start()
+
+    @pl.when(step == tiles + 2)
+    def _():
+        for one in loads():
+            one.wait()
+        up_copy().wait_recv()
+        down_copy().wait_recv()
+        for other in range(groups):
+            slices[other, 0] = (up_own[other].astype(f32) + up_in[other].astype(f32)).astype(bf16)
+            slices[other, 1] = (down_own[other].astype(f32) + down_in[other].astype(f32)).astype(bf16)
+        for away in range(1, groups):
+            slice_copy(away).start()
+
+    @pl.when(step == tiles + 6)
+    def _():
+        total = slices[fsdp].astype(f32)
+        for away in range(1, groups):
+            slice_copy(away).wait_recv()
+            total = total + slices_in[away - 1].astype(f32)
+        context_slice[...] = total.astype(bf16)
+        context_copy().start()
+
+    @pl.when(step == tiles + 4)
+    def _():
+        total = piece[fsdp].astype(f32)
+        for away in range(1, groups):
+            piece_copy(away).wait_recv()
+            total = total + piece_in[away - 1].astype(f32)
+        block_piece[...] = total.astype(bf16)
+        block_copy().start()
+
+    @pl.when(step == tiles + 7)
+    def _():
+        block_copy().wait_recv()
+        grad_weight_ref[...] = block_piece[...].astype(f32) + block_in[...].astype(f32)
+
+    @pl.when(step == 2 * tiles - 1)
+    def _():
+        rows = [jnp.sum(sums[kind].T, axis=0, keepdims=True) for kind in range(2)]
+        rank_sums[...] = jnp.concatenate(rows + [jnp.zeros((6, depth), f32)], axis=0)
+        for away in range(1, ranks):
+            rank_copy(away).start()
+
+    @pl.when(step == 2 * tiles)
+    def _():
+        for away in range(1, ranks):
+            rank_copy(away).wait_recv()
+        pairs = [rank_sums[...] + rank_in[1], rank_in[0] + rank_in[2]]
+        group_sums[...] = pairs[0] + pairs[1]
+        for away in range(1, everyone):
+            group_copy(away).start()
+
+    @pl.when(step == 2 * tiles + 1)
+    def _():
+        all_small_ref[fsdp] = small_sum[...]
+        for away in range(1, groups):
+            sum_copy(away).wait_recv()
+            all_small_ref[lax.rem(fsdp + groups - away, groups)] = small_groups[away - 1]
+            sum_copy(away).wait_send()
+            slice_copy(away).wait_send()
+        context_copy().wait()
+        pieces_ref[context] = context_slice[...]
+        pieces_ref[1 - context] = context_in[...]
+        out_copy().wait()
+        grad_out_sum_ref[...] = grad_out_ref[...].astype(f32) + out_in[...].astype(f32)
+        up_copy().wait_send()
+        down_copy().wait_send()
+        for away in range(1, in_plane):
+            small_copy(away).wait_send()
+        for one in result_copies() + result_moves():
+            one.wait()
+        all_sums_ref[place] = group_sums[...]
+        for away in range(1, everyone):
+            group_copy(away).wait_recv()
+            all_sums_ref[lax.rem(place + everyone - away, everyone)] = group_in[away - 1]
+        for tile in range(tiles):
+            part_copy(tile).wait_send()
+            pair_copy(tile).wait_send()
+        for tile in range(half):
+            chip_copy(tile).wait_send()
+        for away in range(1, groups):
+            piece_copy(away).wait_send()
+        block_copy().wait_send()
+        for away in range(1, ranks):
+            rank_copy(away).wait_send()
+        for away in range(1, everyone):
+            group_copy(away).wait_send()
+
+
+def ordered_sum(own, others, place):
+    count = len(others) + 1
+    total = 0.0
+    for source in range(count):
+        away = lax.rem(place - source + count, count)
+        term = own
+        for k, other in enumerate(others):
+            term = jnp.where(away == k + 1, other, term)
+        total = total + term
+    return total
+
+
+def entry_back_call(
+    grad_query,
+    grad_key,
+    grad_value,
+    hat_t,
+    scaling,
+    gain,
+    shift,
+    weight,
+    grad_middle,
+    middle_in,
+    small,
+    up,
+    down,
+    grad_out,
+    result,
+    result_in,
+    groups,
+    tile,
+):
     group, length = grad_query.shape
     depth = hat_t.shape[0]
-    steps = length // blocks // tile
-    lanes = lambda i: (0, i)
-    whole = lambda i: (0, 0)
+    tiles = length // tile
+    half = tiles // 2
+    rows = depth // 4
+    weight_rows = depth // groups
+
+    def lanes(step):
+        first = (1 - lax.axis_index("context")) * half
+        return 0, lax.rem(first + lax.rem(jnp.minimum(step, 2 * tiles - 1), tiles), tiles)
+
+    whole = lambda step: (0, 0)
+    whole3 = lambda step: (0, 0, 0)
+    whole4 = lambda step: (0, 0, 0, 0)
+    dma = lambda *shape: [pltpu.SemaphoreType.DMA(shape)] * 2
+    hbm = pl.BlockSpec(memory_space=pl.ANY)
+    piece = up.shape[1:]
     return pl.pallas_call(
-        entry_back_kernel,
-        grid=(length // tile,),
+        partial(entry_back_kernel, tiles=tiles, groups=groups),
+        grid=(2 * tiles + 2,),
         in_specs=[
             pl.BlockSpec((group, tile), lanes),
             pl.BlockSpec((group, tile), lanes),
@@ -645,20 +1340,103 @@
             pl.BlockSpec((depth, 1), whole),
             pl.BlockSpec((depth, 1), whole),
             pl.BlockSpec((depth, 3 * group), whole),
+            pl.BlockSpec((1, depth, tile), lambda step: (lax.axis_index("context"), 0, 0)),
+            pl.BlockSpec((depth, tile), whole),
+            pl.BlockSpec(small.shape, whole),
+            hbm,
+            hbm,
+            pl.BlockSpec(grad_out.shape, whole),
+            hbm,
+            hbm,
         ],
         out_specs=[
-            pl.BlockSpec((1, depth, tile), lambda i: (i // steps, 0, i % steps)),
-            pl.BlockSpec((3 * group, depth), whole),
-            pl.BlockSpec((2, depth, WIDE), lambda i: (0, 0, 0)),
+            pl.BlockSpec((2, half, rows, tile), whole4),
+            pl.BlockSpec((weight_rows, 3 * group), whole),
+            pl.BlockSpec((2 * groups, 8, depth), whole3),
+            pl.BlockSpec((groups, *small.shape), whole3),
+            pl.BlockSpec((2, 2, *piece[1:]), whole4),
+            pl.BlockSpec(grad_out.shape, whole),
+            hbm,
         ],
         out_shape=[
-            jax.ShapeDtypeStruct((blocks, depth, length // blocks), bf16),
-            jax.ShapeDtypeStruct((3 * group, depth), f32),
-            jax.ShapeDtypeStruct((2, depth, WIDE), f32),
+            jax.ShapeDtypeStruct((2, half, rows, tile), bf16),
+            jax.ShapeDtypeStruct((weight_rows, 3 * group), f32),
+            jax.ShapeDtypeStruct((2 * groups, 8, depth), f32),
+            jax.ShapeDtypeStruct((groups, *small.shape), f32),
+            jax.ShapeDtypeStruct((2, 2, *piece[1:]), bf16),
+            jax.ShapeDtypeStruct(grad_out.shape, f32),
+            jax.ShapeDtypeStruct((2, 4 * result.shape[1], depth), bf16),
         ],
-        compiler_params=pltpu.CompilerParams(vmem_limit_bytes=VMEM),
+        scratch_shapes=[
+            *[pltpu.VMEM(piece, bf16)] * 4,
+            pltpu.VMEM((groups, 2, *piece[1:]), bf16),
+            pltpu.VMEM((groups - 1, 2, *piece[1:]), bf16),
+            pltpu.VMEM((2, *piece[1:]), bf16),
+            pltpu.VMEM((2, *piece[1:]), bf16),
+            pltpu.VMEM((7, *small.shape), f32),
+            pltpu.VMEM(small.shape, f32),
+            pltpu.VMEM((groups - 1, *small.shape), f32),
+            pltpu.VMEM(grad_out.shape, bf16),
+            pltpu.SemaphoreType.DMA((2,)),
+            *[pltpu.SemaphoreType.DMA] * 4,
+            *dma(groups - 1),
+            *[pltpu.SemaphoreType.DMA] * 2,
+            *dma(7),
+            *dma(groups - 1),
+            *[pltpu.SemaphoreType.DMA] * 2,
+            *dma(4),
+            pltpu.SemaphoreType.DMA((4,)),
+            pltpu.VMEM((depth, 3 * group), f32),
+            pltpu.VMEM((2, depth, WIDE), f32),
+            pltpu.VMEM((tiles, 2, 2, rows, tile), bf16),
+            pltpu.VMEM((tiles, 2, rows, tile), bf16),
+            pltpu.VMEM((tiles, 2, rows, tile), bf16),
+            pltpu.VMEM((tiles, rows, tile), bf16),
+            pltpu.VMEM((half, rows, tile), bf16),
+            pltpu.VMEM((half, rows, tile), bf16),
+            pltpu.VMEM((groups, weight_rows, 3 * group), bf16),
+            pltpu.VMEM((groups - 1, weight_rows, 3 * group), bf16),
+            pltpu.VMEM((weight_rows, 3 * group), bf16),
+            pltpu.VMEM((weight_rows, 3 * group), bf16),
+            pltpu.VMEM((8, depth), f32),
+            pltpu.VMEM((3, 8, depth), f32),
+            pltpu.VMEM((8, depth), f32),
+            pltpu.VMEM((2 * groups - 1, 8, depth), f32),
+            *dma(tiles),
+            *dma(tiles),
+            *dma(half),
+            *dma(groups - 1),
+            *[pltpu.SemaphoreType.DMA] * 2,
+            *dma(3),
+            *dma(2 * groups - 1),
+        ],
+        compiler_params=pltpu.CompilerParams(
+            vmem_limit_bytes=VMEM, collective_id=3, has_side_effects=True
+        ),
+        cost_estimate=cost(12 * length * depth * group, grad_query, hat_t, hat_t),
         name="entry_back",
-    )(grad_query, grad_key, grad_value, hat_t, scaling, gain, shift, weight)
+    )(
+        grad_query,
+        grad_key,
+        grad_value,
+        hat_t,
+        scaling,
+        gain,
+        shift,
+        weight,
+        grad_middle,
+        middle_in,
+        small,
+        up,
+        down,
+        grad_out,
+        result,
+        result_in,
+    )
+
+
+def add(left_side, right_side):
+    return (left_side.astype(f32) + right_side.astype(f32)).astype(bf16)
 
 
 def by_sequence(
@@ -770,111 +1548,107 @@
     ).astype(jnp.int32)
     mixture, told = attend_call(ranges, queries, keys, values_t, tile, block)
 
-    everyone = ("context", "tensor")
-    own_mixture = lax.all_to_all(mixture, everyone, 0, 0, tiled=True).reshape(
-        context, tensor * group, tile
-    )
     own_segments = lax.dynamic_slice_in_dim(
         segments, context_rank * own_rows + tensor_rank * quarter, quarter, axis=1
     )
-    valid = (own_segments != 0).astype(f32)[:, :, None]
+    own_cotangent = lax.dynamic_slice_in_dim(cotangent, tensor_rank * quarter, quarter, axis=1)
     (
         result,
         grad_mixture,
         grad_middle,
-        entry_t,
-        grad_output_t,
-        active,
-        grad_hidden,
         grad_out,
         sums,
         bias_sums,
+        up_keep,
+        up_send,
+        down_keep,
+        down_send,
     ) = middle_call(
-        tensor_rank[None].astype(jnp.int32),
-        own_mixture,
-        tokens,
-        cotangent,
-        valid,
+        mixture,
+        mine.reshape(-1, depth),
+        own_cotangent.reshape(-1, depth),
+        (own_segments != 0).astype(f32).reshape(-1, 1),
         mods,
         b_up.astype(f32).reshape(tensor, 1, part_width),
         b_down.astype(f32)[None, :],
         out_weight,
         up,
         down,
+        fsdp,
         tile=min(tile, 256),
     )
-    block_out = lax.all_gather(result, "tensor", axis=1, tiled=True)
-    grad_mixture = lax.all_to_all(
-        grad_mixture.reshape(context * tensor, group, tile), everyone, 0, 0, tiled=True
-    )
-    middle_slice = lax.all_to_all(grad_middle, "tensor", 1, 2, tiled=True)
-    grad_up, grad_down = weights_call(entry_t, grad_output_t, active, grad_hidden)
+    result = result.reshape(sequences, quarter, depth)
+    across = [(k, (k + 2) % tensor) for k in range(tensor)]
+    result_in = lax.ppermute(result, "tensor", across)
+    middle_in = lax.ppermute(
+        lax.dynamic_index_in_dim(grad_middle, 1 - context_rank, 0, keepdims=False), "context", partner
+    )
+    small = jnp.concatenate(
+        [
+            sums[:, :5].reshape(-1, depth),
+            bias_sums.reshape(-1, depth),
+        ]
+    )
+    small_rows = small.shape[0]
+    small = jnp.pad(small, ((0, -small_rows % 8), (0, 0)))
+
+    up_sum = add(up_keep, lax.ppermute(up_send, "tensor", across))
+    down_sum = add(down_keep, lax.ppermute(down_send, "context", partner))
     grad_out = (
         grad_out.astype(bf16)
         .reshape(tensor, group, fsdp, depth // fsdp)
         .transpose(0, 2, 1, 3)
         .reshape(tensor * fsdp, group * (depth // fsdp) // part_width, part_width)
     )
-    pieces = jnp.concatenate(
-        [
-            grad_up.reshape(tensor * fsdp, -1, part_width),
-            grad_down.reshape(tensor * fsdp, -1, part_width),
-            grad_out,
-        ],
-        axis=1,
-    )
-    pieces = lax.psum_scatter(pieces, both, scatter_dimension=0, tiled=True)[0]
-    pieces = lax.psum(pieces, "context").astype(f32)
-    rows = depth // fsdp
-    grad_w_up = pieces[:rows]
-    grad_w_down = pieces[rows : 2 * rows].T
-    grad_w_out = pieces[2 * rows :].reshape(group, depth // fsdp)
+    grad_out = lax.psum_scatter(grad_out, both, scatter_dimension=0, tiled=True)[0]
 
     grad_query, grad_key, grad_value = attend_back_call(
         ranges, told, keys, keys_t, values, mixture, grad_mixture, cosine, sine, tile, block
     )
-    part, grad_qkv, entry_sums = entry_back_call(
-        grad_query, grad_key, grad_value, hat_t, scaling, gain_column, shift_column, qkv, context, tile
-    )
-    part = lax.psum_scatter(part, "tensor", scatter_dimension=1, tiled=True)
-    part = lax.all_to_all(part, "context", 0, 0, tiled=True)
-    grad_tokens = jnp.swapaxes(part.astype(f32) + middle_slice.astype(f32), 1, 2)
-
-    grad_qkv = (
-        grad_qkv.astype(bf16).reshape(3 * group, fsdp, depth // fsdp).transpose(1, 0, 2)
-    )
-    grad_qkv = lax.psum_scatter(grad_qkv, "fsdp", scatter_dimension=0, tiled=True)[0]
-    grad_qkv = lax.psum(grad_qkv, "context").astype(f32)
+    (grad_query, up_sum, down_sum, result_in, middle_in, grad_out) = lax.optimization_barrier(
+        (grad_query, up_sum, down_sum, result_in, middle_in, grad_out)
+    )
+    part, grad_qkv, entry_sums, small, pieces, grad_out, block_out = entry_back_call(
+        grad_query,
+        grad_key,
+        grad_value,
+        hat_t,
+        scaling,
+        gain_column,
+        shift_column,
+        qkv,
+        grad_middle,
+        middle_in,
+        small,
+        up_sum,
+        down_sum,
+        grad_out,
+        result,
+        result_in,
+        groups=fsdp,
+        tile=tile,
+    )
+    pieces = pieces.transpose(1, 0, 2, 3)
+    pieces = pieces.reshape(2, depth // fsdp, part_width).astype(f32)
+    grad_w_up = pieces[0]
+    grad_w_down = pieces[1].T
+    grad_w_out = grad_out.reshape(group, depth // fsdp)
+    small_sums = small[:, :10].reshape(fsdp * sequences, 5, depth)
+    grad_b_up = jnp.sum(small[:, 10:small_rows], axis=0).reshape(-1)
+    grad_b_down = jnp.sum(small_sums[:, 4], axis=0)
+    grad_gain_two = jnp.sum(small_sums[:, 2] * (1.0 + modulation[:, 4 * depth : 5 * depth]), axis=0)
+    middle_mod = jnp.concatenate(
+        [small_sums[:, 0], small_sums[:, 1], small_sums[:, 2] * gain_second, small_sums[:, 3]], axis=1
+    )
+    part = part.transpose(0, 1, 3, 2).reshape(sequences, own_rows, depth // tensor)
+    grad_tokens = part.astype(f32)
     grad_w_qkv = (
-        grad_qkv.reshape(3, heads, HDIM, depth // fsdp).transpose(3, 1, 0, 2).reshape(-1, 3 * group)
-    )
-
-    entry_sums = jnp.sum(entry_sums, axis=2)
-    is_own = (jnp.arange(sequences) == context_rank).astype(f32)[:, None]
+        grad_qkv.reshape(-1, 3, heads, HDIM).transpose(0, 2, 1, 3).reshape(-1, 3 * group)
+    )
     grad_mod = jnp.concatenate(
-        [
-            is_own * entry_sums[0],
-            is_own * (entry_sums[1] * gain_first),
-            sums[:, 0],
-            sums[:, 1],
-            sums[:, 2] * gain_second,
-            sums[:, 3],
-        ],
-        axis=1,
-    )
-    grad_mod = lax.dynamic_update_slice_in_dim(
-        jnp.zeros((fsdp * sequences, 6 * depth), f32), grad_mod, fsdp_rank * sequences, 0
-    )
-    (grad_mod, grad_gain_one, grad_gain_two, grad_b_up, grad_b_down) = lax.psum(
-        (
-            grad_mod,
-            entry_sums[1] * (1.0 + own_mods[1]),
-            jnp.sum(sums[:, 2] * (1.0 + local_mods[:, 4]), axis=0),
-            bias_sums.reshape(-1),
-            jnp.sum(sums[:, 4], axis=0),
-        ),
-        ("fsdp", "context", "tensor"),
-    )
+        [entry_sums[:, 0], entry_sums[:, 1] * gain_first, middle_mod], axis=1
+    )
+    grad_gain_one = jnp.sum(entry_sums[:, 1] * (1.0 + modulation[:, depth : 2 * depth]), axis=0)
     grad_ada_b = jnp.sum(grad_mod, axis=0)
     grad_ada_w = exact_transposed(embedding, grad_mod)
     grad_before = silu_back(exact_against(grad_mod, ada_full))[0]
@@ -1212,7 +1986,7 @@
 
     def whole(tokens, *others):
         sequences = tokens.shape[0] // axes["fsdp"]
-        local = by_sequence if sequences == axes["context"] == 2 else by_block
+        local = by_sequence if sequences == axes["context"] == 2 and axes["tensor"] == 4 else by_block
         return mapped(local, mesh)(tokens, *others)
 
     return whole

time: 852 us -> 540 us (0.63)
  waiting for transfers between devices: 399 us -> 67.7 us
  Pallas kernels: 211 us -> 337 us
  blocking collectives: 125 us -> 28.5 us
    reduce_scatter x3 -> x1, waiting for transfers between devices: 147 us -> 0.01 us  [by_sequence(): lax.psum_scatter(grad_out, both, scatter_dimension=0, tiled=True)[0]]
    pallas_call x3 -> x2, Pallas kernels: 74.7 us -> 201 us  [the longest x1 105 us: entry_back_call(): pl.pallas_call(partial(entry_back_kernel, tiles=tiles, groups=groups), gr...]
    psum x2 -> x0, waiting for transfers between devices: 106 us -> none  [the longest x1 69.1 us: by_sequence(): lax.psum((grad_mod, entry_sums[1] * (1.0 + own_mods[1]), jnp.sum(sums[:,...]
    all_to_all x2 -> x0, blocking collectives: 51.7 us -> none  [the longest x1 26.2 us: by_sequence(): middle_slice = lax.all_to_all(grad_middle, 'tensor', 1, 2, tiled=True)]
    psum x1 -> x0, blocking collectives: 45.7 us -> none  [by_sequence(): lax.psum((grad_mod, entry_sums[1] * (1.0 + own_mods[1]), jnp.sum(sums[:,...]
    all_gather x1 -> x0, waiting for transfers between devices: 45 us -> none  [by_sequence(): block_out = lax.all_gather(result, 'tensor', axis=1, tiled=True)]
    all_to_all x2 -> x0, waiting for transfers between devices: 22.5 us -> none  [the longest x1 22.5 us: by_sequence(): lax.all_to_all(mixture, everyone, 0, 0, tiled=True)]
    all_gather x1, waiting for transfers between devices: 58.4 us -> 48.2 us  [by_sequence(): lax.all_gather(w_down.T, both, axis=0, tiled=True)]
  transfers between devices with their start and end apart: 13 -> 10, of which waited for: 8 -> 2; matrix products, arithmetic and copies ran while one was open for 8% -> 9% of each run, Pallas kernels for 8% -> 26%
where the time goes in v2:
time: 540 us; the launch traced here: 530 us
  Pallas kernels  337 us (62%)
  waiting for transfers between devices  67.7 us (13%)
  local copies, waits for them, and re-layouts  44.3 us (8%)
  blocking collectives  28.5 us (5%)
  other arithmetic  21.5 us (4%)
  between operations  16.1 us (3%)
  starting transfers between devices  8.5 us (2%)
  matrix products  6.26 us (1%)
    pallas_call x1, Pallas kernels, entry_back_call(): pl.pallas_call(partial(entry_back_kernel, tiles=tiles, groups=groups), gr...  105 us
    pallas_call x1, Pallas kernels, middle_call(): pl.pallas_call(partial(middle_kernel, tile=tile, tiles=tiles, parts=parts...  95.5 us
    pallas_call x1, Pallas kernels, attend_back_call(): pl.pallas_call(partial(attend_back_kernel, block=block), grid_spec=pltpu....  82.3 us
    all_gather x1, waiting for transfers between devices, by_sequence(): lax.all_gather(w_down.T, both, axis=0, tiled=True)  48.2 us
    pallas_call x1, Pallas kernels, attend_call(): pl.pallas_call(partial(attend_kernel, block=block), grid_spec=pltpu.Prefe...  33.1 us
    pallas_call x2, Pallas kernels, entry_call(): pl.pallas_call(partial(entry_kernel, heads=heads), grid_spec=pltpu.Prefet...  21.3 us
    all_gather x1, blocking collectives, by_sequence(): qkv = lax.all_gather(by_kind, 'fsdp', axis=0, tiled=True)  19.8 us
    ppermute x1, waiting for transfers between devices, by_sequence(): lax.ppermute(lax.dynamic_index_in_dim(mine, lax.rem(context_rank + 1, con...  17.5 us
  transfers between devices with their start and end apart: 10, of which 2 were waited for; matrix products, arithmetic and copies ran while one was open for 9% of the time, Pallas kernels for 26%

profile of v2, /device:TPU:0, one launch (start us, length us, event | category | flops | bytes accessed | tf_op | source)
XLA Modules:
  0.0 530.3 jit_solution(2788415828821314569)
XLA Ops:
  7.3 0.7 all-gather.12.cloned.1.call-update
  8.0 1.4 constant_dynamic-slice_fusion.3
  9.4 3.0 collective-permute-start
  12.4 17.5 %collective-permute-done = bf16[1,512,768]{2,1,0:T(8,128)(2,1)S(1)} collective-permute-done((bf16[1,512,768]{2,1,0:T(8,128)(2,1)S(1)}, bf16[1,512,768]{2,1,0:T(8,128)(2,1)S(1)}, u32[]{:S(2)}, u32[]{:S(2)}) %collective-permute-start) | collective-permute-done | bytes 786464 | tf_op jit(solution)/shard_map/ppermute | solution.py:1473
  30.0 0.9 copy-done.5
  33.8 8.7 %all-reduce.1 = s32[8]{0:T(128)S(1)} all-reduce(s32[8]{0:T(128)S(1)} %dynamic-update-slice), channel_id=1, replica_groups=mesh['fsdp'=4,'context'=2,'tensor'=4] {'fsdp'}, use_global_device_ids=true, to_apply=%add.1 | all-reduce | flops 8 | bytes 64
  45.2 0.9 broadcast_in_dim.66.gain_ref
  46.1 1.0 copy.77.shift_ref
  47.6 19.8 %all_gather.23.weight_ref = bf16[768,576]{1,0:T(8,128)(2,1)S(1)} all-gather(bf16[192,576]{1,0:T(8,128)(2,1)S(1)} %copy.72), channel_id=1, replica_groups=mesh['fsdp'=4,'context'=2,'tensor'=4] {'fsdp'}, dimensions={0}, use_global_device_ids=true | all-gather | bytes 1105920 | tf_op jit(solution)/shard_map/all_gather | solution.py:1481
  67.4 1.3 copy.78.weight_ref
  68.7 1.0 copy.101
  72.2 2.7 constant_dynamic-slice_fusion.1
  74.9 2.7 constant_dynamic-slice_fusion
  77.6 2.8 multiply_sine_fusion
  80.4 10.6 %entry.2 = (bf16[3,128,4096]{2,1,0:T(8,128)(2,1)}, bf16[3,4096,128]{2,1,0:T(8,128)(2,1)}, bf16[3,64,4096]{2,1,0:T(8,128)(2,1)}, bf16[3,4096,128]{2,1,0:T(8,128)(...) custom-call(s32[2]{0:T(128)} %pad_add_fusion.1.base_ref, ...), custom_call_target="tpu_custom_call" | custom-call | flops 1811939328 | bytes 26591232 | tf_op jit(solution)/shard_map/entry/pallas_call | solution.py:196
  91.1 0.7 maximum_maximum_fusion.mod_ref
  91.7 2.7 copy.122
  94.4 2.3 reshape.155.out_weight_ref
  96.7 10.7 %entry.3 = (bf16[3,128,4096]{2,1,0:T(8,128)(2,1)}, bf16[3,4096,128]{2,1,0:T(8,128)(2,1)}, bf16[3,64,4096]{2,1,0:T(8,128)(2,1)}, bf16[3,4096,128]{2,1,0:T(8,128)(...) custom-call(s32[2]{0:T(128)} %pad_add_fusion.base_ref, ...), custom_call_target="tpu_custom_call", output_to_operand_aliasing={{0}: (8, {}), {1}: (9, {}), {2}: (10, {}), {3}: (11, {}), {... | custom-call | flops 1811939328 | bytes 23445504 | tf_op jit(solution)/shard_map/entry/pallas_call | solution.py:196
  107.3 1.1 reduce_max.28
  110.5 33.1 %attend.1 = (bf16[8,192,512]{2,1,0:T(8,128)(2,1)}, bf16[3,128,4096]{2,1,0:T(8,128)(2,1)}) custom-call(s32[3,8]{1,0:T(4,128)} %add_add_fusion.range_ref, bf16[3,128,4096]{2,1,0:T(8,128)(2,1)} %get-tuple-element.66.query_ref, bf16[3,4096,128]{2,1,0:T(8,128)(2,1)} %get-tuple-element.67.key_ref, bf16[3,80,4096]{2,1,0:T(8,128)(2,1)} %get-tuple-element.68.value_ref), custom_call_target="tpu_custom_call" | custom-call | flops 25769803776 | bytes 8257536 | tf_op jit(solution)/shard_map/attend/pallas_call | solution.py:281
  143.7 48.2 %all-gather.10.cloned.1.call-done = bf16[3072,768]{1,0:T(8,128)(2,1)} async-done(((bf16[192,768]{1,0:T(8,128)(2,1)}), bf16[3072,768]{1,0:T(8,128)(2,1)}) %all-gather.10.cloned.1.call-update) | async-done | bytes 4718608 | tf_op jit(solution)/shard_map/all_gather | solution.py:1484
  191.9 95.5 %middle.1 = (bf16[1024,768]{1,0:T(8,128)(2,1)}, bf16[8,192,512]{2,1,0:T(8,128)(2,1)}, bf16[2,768,512]{2,1,0:T(8,128)(2,1)}, f32[768,768]{1,0:T(8,128)}, f32[2,8,...) custom-call(bf16[8,192,512]{2,1,0:T(8,128)(2,1)} %get-tuple-element., ...), custom_call_target="tpu_custom_call" | custom-call | flops 47110422528 | bytes 11010048 | tf_op jit(solution)/shard_map/middle/pallas_call | solution.py:803
  287.5 3.2 collective-permute-start.2
  290.7 1.9 collective-permute-start.3
  292.6 1.2 dynamic-slice_bitcast_fusion
  293.9 2.8 convert_element_type.75
  296.7 3.5 reshape.159
  300.1 1.4 copy.121
  301.6 3.9 reshape.160
  305.5 82.3 %attend_back.1 = (bf16[192,4096]{1,0:T(8,128)(2,1)}, bf16[192,4096]{1,0:T(8,128)(2,1)}, bf16[192,4096]{1,0:T(8,128)(2,1)}) custom-call(s32[3,8]{1,0:T(4,128)} %add_add_fusion.range_ref, bf16[3,128,4096]{2,1,0:T(8,128)(2,1)} %get-tuple-element.69.query_ref, bf16[3,4096,128]{2,1,0:T(8,128)(2,1)} %get-tuple-element.67.key_ref, ...), custom_call_target="tpu_custom_call" | custom-call | flops 64424509440 | bytes 9437184 | tf_op jit(solution)/shard_map/attend_back/pallas_call | solution.py:392
  388.5 2.8 add_convert_fusion.1.up_ref
  391.2 2.6 add_convert_fusion.down_ref
  393.9 105.2 %entry_back.1 = (bf16[2,4,192,512]{3,2,1,0:T(8,128)(2,1)}, f32[192,576]{1,0:T(8,128)}, f32[8,8,768]{2,1,0:T(8,128)}, f32[4,16,768]{2,1,0:T(8,128)}, bf16[2,2,96,...) custom-call(bf16[192,4096]{1,0:T(8,128)(2,1)} %get-tuple-element.82.grad_query_ref, ...), custom_call_target="tpu_custom_call" | custom-call | flops 7247757312 | bytes 14155776 | tf_op jit(solution)/shard_map/entry_back/pallas_call | solution.py:1331
  499.1 0.9 slice.100
  500.1 1.0 copy.85
  501.1 0.9 reshape.163
  502.0 0.7 slice_reduce_fusion.1
  502.7 1.4 fusion.1
  504.1 1.0 fusion.32
  505.1 3.5 fusion.23
  509.3 0.9 slice_reduce_fusion
  510.6 2.0 copy.99
  512.6 1.0 fusion.9
  513.9 1.0 copy.92
  514.9 0.8 reshape.166
  515.8 1.1 fusion.31
  517.5 5.9 %copy.139 = bf16[2,2048,768]{2,1,0:T(8,128)(2,1)} copy(bf16[2,2048,768]{2,1,0:T(8,128)(2,1)} %get-tuple-element.162) | data formatting | bytes 12582912
  (130 shorter events, 12.2 us)
Async XLA Ops:
  7.2 36.1 %copy-start = (bf16[128,4608]{1,0:T(8,128)(2,1)S(1)}, bf16[128,4608]{1,0:T(8,128)(2,1)}, u32[]{:S(2)}) copy-start(bf16[128,4608]{1,0:T(8,128)(2,1)} %param.20) | copy-start | bytes 3538948
  7.2 25.1 %copy-start.29 = (u32[32]{0:T(128)S(1)}, u32[32]{0:T(128)}, u32[]{:S(2)}) copy-start(u32[32]{0:T(128)} %constant.127) | copy-start | bytes 388
  7.2 26.3 %copy-start.28 = (s32[2]{0:T(128)S(1)}, s32[2]{0:T(128)}, u32[]{:S(2)}) copy-start(s32[2]{0:T(128)} %param.18) | copy-start | bytes 28
  7.2 35.3 %copy-start.18 = (s32[2,4096]{1,0:T(2,128)S(1)}, s32[2,4096]{1,0:T(2,128)}, u32[]{:S(2)}) copy-start(s32[2,4096]{1,0:T(2,128)} %param.17) | copy-start | bytes 98308
  7.2 84.5 %all-gather.12.cloned.1.call-start = ((), (), s32[]{:S(2)}) async-start(), calls=%async_computation.5 | async-start | bytes 1671168 | tf_op jit(solution)/shard_map/all_gather | solution.py:1486
  8.0 88.7 %all-gather.6.cloned.1.call-start = ((), (), s32[]{:S(2)}) async-start(), calls=%async_computation.1 | async-start | bytes 3932160 | tf_op jit(solution)/shard_map/all_gather | solution.py:1478
  8.0 35.0 %copy-start.20 = (bf16[4608]{0:T(1024)(128)(2,1)S(1)}, bf16[4608]{0:T(1024)(128)(2,1)}, u32[]{:S(2)}) copy-start(bf16[4608]{0:T(1024)(128)(2,1)} %param.21) | copy-start | bytes 27652
  8.0 35.0 %copy-start.27 = (bf16[256,128]{1,0:T(8,128)(2,1)S(1)}, bf16[256,128]{1,0:T(8,128)(2,1)}, u32[]{:S(2)}) copy-start(bf16[256,128]{1,0:T(8,128)(2,1)} %param.19) | copy-start | bytes 196612
  9.4 20.6 %collective-permute-start = (bf16[1,512,768]{2,1,0:T(8,128)(2,1)S(1)}, bf16[1,512,768]{2,1,0:T(8,128)(2,1)S(1)}, u32[]{:S(2)}, u32[]{:S(2)}) collective-permute-start(bf16[1,512,768]{2,1,0:T(8,128)(2,1)S(1)} %constant_dynamic-slice_fusion.3), channel_id=1, source_target_pairs={{0,4},{4,0},{1,5},{5,1},{2,6},{6,2},{3,7},{7,3},{8,12},{12,8},{9,1... | collective-permute-start | bytes 2359304 | tf_op jit(solution)/shard_map/ppermute | solution.py:1473
  30.0 0.9 copy-start.5
  30.0 14.6 %copy-start.21 = (bf16[768]{0:T(1024)(128)(2,1)S(1)}, bf16[768]{0:T(1024)(128)(2,1)}, u32[]{:S(2)}) copy-start(bf16[768]{0:T(1024)(128)(2,1)} %param.22) | copy-start | bytes 4612
  30.9 16.2 %copy-start.10 = (bf16[192,576]{1,0:T(8,128)(2,1)S(1)}, bf16[192,576]{1,0:T(8,128)(2,1)}, u32[]{:S(2)}) copy-start(bf16[192,576]{1,0:T(8,128)(2,1)} %param.23) | copy-start | bytes 663556
  30.9 112.7 %all-gather.8.cloned.1.call-start = ((), (), s32[]{:S(2)}) async-start(), calls=%async_computation.2 | async-start | bytes 5013504 | tf_op jit(solution)/shard_map/all_gather | solution.py:1483
  31.7 160.2 %all-gather.10.cloned.1.call-start = ((), (), s32[]{:S(2)}) async-start(), calls=%async_computation.3 | async-start | bytes 5013504 | tf_op jit(solution)/shard_map/all_gather | solution.py:1484
  32.2 361.6 %reduce-scatter.2.cloned.1.call-start = ((), (), s32[]{:S(2)}) async-start(), calls=%async_computation.4 | async-start | bytes 1253376 | tf_op jit(solution)/shard_map/reduce_scatter | solution.py:1603
  42.5 4.8 copy-start.25
  42.5 4.8 copy-start.8
  43.3 1.3 copy-start.13
  43.8 0.7 copy-start.9
  47.5 22.2 %copy-start.23 = (bf16[768]{0:T(1024)(128)(2,1)S(1)}, bf16[768]{0:T(1024)(128)(2,1)}, u32[]{:S(2)}) copy-start(bf16[768]{0:T(1024)(128)(2,1)} %param.25) | copy-start | bytes 4612
  47.5 22.2 %copy-start.22 = (bf16[3072]{0:T(1024)(128)(2,1)S(1)}, bf16[3072]{0:T(1024)(128)(2,1)}, u32[]{:S(2)}) copy-start(bf16[3072]{0:T(1024)(128)(2,1)} %param.27) | copy-start | bytes 18436
  47.6 22.8 %copy-start.24 = (bf16[768]{0:T(1024)(128)(2,1)S(1)}, bf16[768]{0:T(1024)(128)(2,1)}, u32[]{:S(2)}) copy-start(bf16[768]{0:T(1024)(128)(2,1)} %param.29) | copy-start | bytes 4612
  67.4 7.5 %copy-start.1 = (bf16[768,576]{1,0:T(8,128)(2,1)}, bf16[768,576]{1,0:T(8,128)(2,1)S(1)}, u32[]{:S(2)}) copy-start(bf16[768,576]{1,0:T(8,128)(2,1)S(1)} %all_gather.23.weight_ref) | copy-start | bytes 2654212
  69.7 21.3 %copy-start.15 = (f32[768]{0:T(1024)}, f32[768]{0:T(1024)S(1)}, u32[]{:S(2)}) copy-start(f32[768]{0:T(1024)S(1)} %convert_element_type.68) | copy-start | bytes 9220
  287.4 101.1 %collective-permute-start.1 = (bf16[2,4,96,768]{3,2,1,0:T(8,128)(2,1)}, bf16[2,4,96,768]{3,2,1,0:T(8,128)(2,1)}, u32[]{:S(2)}, u32[]{:S(2)}) collective-permute-start(bf16[2,4,96,768]{3,2,1,0:T(8,128)(2,1)} %get-tuple-element.76), channel_id=1, source_target_pairs={{0,2},{1,3},{2,0},{3,1},{4,6},{5,7},{6,4},{7,5},{8,10},{9,11},{10,... | collective-permute-start | bytes 3538952 | tf_op jit(solution)/shard_map/ppermute | solution.py:1595
  287.5 103.8 %collective-permute-start.2 = (bf16[2,4,96,768]{3,2,1,0:T(8,128)(2,1)}, bf16[2,4,96,768]{3,2,1,0:T(8,128)(2,1)}, u32[]{:S(2)}, u32[]{:S(2)}) collective-permute-start(bf16[2,4,96,768]{3,2,1,0:T(8,128)(2,1)} %get-tuple-element.78), channel_id=1, source_target_pairs={{0,4},{4,0},{1,5},{5,1},{2,6},{6,2},{3,7},{7,3},{8,12},{12,8},{9,1... | collective-permute-start | bytes 3538952 | tf_op jit(solution)/shard_map/ppermute | solution.py:1596
  290.7 103.2 %collective-permute-start.3 = (bf16[2,512,768]{2,1,0:T(8,128)(2,1)}, bf16[2,512,768]{2,1,0:T(8,128)(2,1)}, u32[]{:S(2)}, u32[]{:S(2)}) collective-permute-start(bf16[2,512,768]{2,1,0:T(8,128)(2,1)} %bitcast.118), channel_id=1, source_target_pairs={{0,2},{1,3},{2,0},{3,1},{4,6},{5,7},{6,4},{7,5},{8,10},{9,11},{10,... | collective-permute-start | bytes 4718600 | tf_op jit(solution)/shard_map/ppermute | solution.py:1582
  293.8 100.0 %collective-permute-start.4 = (bf16[768,512]{1,0:T(8,128)(2,1)S(1)}, bf16[768,512]{1,0:T(8,128)(2,1)}, u32[]{:S(2)}, u32[]{:S(2)}) collective-permute-start(bf16[768,512]{1,0:T(8,128)(2,1)S(1)} %dynamic-slice_bitcast_fusion), channel_id=1, source_target_pairs={{0,4},{4,0},{1,5},{5,1},{2,6},{6,2},{3,7},{7,3},{8,12},{12,8},{9,1... | collective-permute-start | bytes 2359304 | tf_op jit(solution)/shard_map/ppermute | solution.py:1583
  305.5 82.3 %copy-start.19 = (f32[4,1,768]{2,1,0:T(1,128)S(1)}, f32[4,1,768]{2,1,0:T(1,128)}, u32[]{:S(2)}) copy-start(f32[4,1,768]{2,1,0:T(1,128)} %get-tuple-element.89) | copy-start | bytes 36868
  305.5 82.3 %copy-start.12 = (f32[2,8,768]{2,1,0:T(8,128)S(1)}, f32[2,8,768]{2,1,0:T(8,128)}, u32[]{:S(2)}) copy-start(f32[2,8,768]{2,1,0:T(8,128)} %get-tuple-element.88) | copy-start | bytes 147460
  305.5 83.0 %copy-start.4 = (bf16[2,4,96,768]{3,2,1,0:T(8,128)(2,1)S(1)}, bf16[2,4,96,768]{3,2,1,0:T(8,128)(2,1)}, u32[]{:S(2)}) copy-start(bf16[2,4,96,768]{3,2,1,0:T(8,128)(2,1)} %get-tuple-element.75) | copy-start | bytes 3538948
  388.5 2.8 copy-start.3
  393.9 108.8 %copy-start.17 = (f32[768]{0:T(1024)S(1)}, f32[768]{0:T(1024)}, u32[]{:S(2)}) copy-start(f32[768]{0:T(1024)} %convert_element_type.64) | copy-start | bytes 9220
  393.9 110.2 %copy-start.16 = (f32[768]{0:T(1024)S(1)}, f32[768]{0:T(1024)}, u32[]{:S(2)}) copy-start(f32[768]{0:T(1024)} %copy-done.15) | copy-start | bytes 9220
  499.1 6.0 %copy-start.14 = (f32[8,128]{1,0:T(8,128)S(1)}, f32[8,128]{1,0:T(8,128)}, u32[]{:S(2)}) copy-start(f32[8,128]{1,0:T(8,128)} %copy-done.13) | copy-start | bytes 12292
  505.1 5.1 copy-start.2
  510.6 2.0 copy-start.26
  510.6 3.0 copy-start.7
  513.6 1.3 copy-start.11
  513.8 1.8 copy-start.6
Sparse Core Ops, SparseCore 0:
  10.4 42.8 all-gather.11
  54.8 27.1 all-gather.5
  84.3 53.4 all-gather.7
  140.0 51.8 all-gather.9
  305.6 60.3 reduce-scatter.1

commit v3 on v2

--- a/solution.py
+++ b/solution.py
@@ -88,28 +88,265 @@
     return 10000.0 ** (-jnp.arange(HALF, dtype=jnp.float32) / HALF)
 
 
+def copy_to(source, target, sent, arrived, **device):
+    return pltpu.make_async_remote_copy(
+        src_ref=source,
+        dst_ref=target,
+        send_sem=sent,
+        recv_sem=arrived,
+        device_id=device,
+        device_id_type=pl.DeviceIdType.MESH,
+    )
+
+
+def greet(devices):
+    barrier = pltpu.get_barrier_semaphore()
+    for device in devices:
+        pl.semaphore_signal(barrier, inc=1, device_id=device, device_id_type=pl.DeviceIdType.MESH)
+    pl.semaphore_wait(barrier, len(devices))
+
+
+def quarter_at(number, tensor):
+    core = lax.rem(tensor, 2)
+    chip = jnp.where(number < 2, tensor // 2, 1 - tensor // 2)
+    return chip * 2 + jnp.where(lax.rem(number, 2) == 0, core, 1 - core)
+
+
 def entry_kernel(
-    base_ref,
+    tokens_ref,
     rows_ref,
+    shard_ref,
+    own_forward_ref,
     gain_ref,
     shift_ref,
-    weight_ref,
     cosine_ref,
     sine_ref,
     segment_ref,
-    *refs,
+    query_ref,
+    key_ref,
+    key_t_ref,
+    value_ref,
+    value_t_ref,
+    hat_ref,
+    scale_ref,
+    norm_ref,
+    weight_ref,
+    forward_ref,
+    shards,
+    weight_t,
+    rows,
+    arrived,
+    sent_shard,
+    got_shard,
+    own_shard,
+    sent_block,
+    got_block,
+    sent_across,
+    got_across,
+    sent_sibling,
+    got_sibling,
+    sent_on,
+    got_on,
+    sent_forward,
+    got_forward,
+    own_forward,
+    *,
     heads,
+    groups,
 ):
-    del base_ref
-    query_ref, key_ref, key_t_ref, value_ref, value_t_ref, hat_ref, scale_ref, norm_ref = refs[-8:]
-    inputs = rows_ref[0].astype(f32).T
+    step = pl.program_id(0)
+    fsdp, context, tensor = (lax.axis_index(name) for name in ("fsdp", "context", "tensor"))
+    ranks = 4
+    core = lax.rem(tensor, 2)
+    sibling = tensor + 1 - 2 * core
+    across = lax.rem(tensor + 2, ranks)
+    quarter = rows.shape[0]
+    chunks = sent_block.shape[0]
+    height = quarter // chunks
+
+    def shard_copy(away):
+        return copy_to(
+            shard_ref,
+            shards.at[fsdp],
+            sent_shard.at[away - 1],
+            got_shard.at[away - 1],
+            fsdp=lax.rem(fsdp + away, groups),
+        )
+
+    def shard_own():
+        return pltpu.make_async_copy(shard_ref, shards.at[fsdp], own_shard)
+
+    def chunk(rank, number):
+        return arrived.at[rank, pl.ds(number * height, height), :]
+
+    def block_copy(number):
+        at = pl.multiple_of(tensor * quarter, quarter) + number * height
+        return copy_to(
+            tokens_ref.at[1 - context, pl.ds(at, height), :],
+            chunk(tensor, number),
+            sent_block.at[number],
+            got_block.at[number],
+            context=1 - context,
+        )
+
+    def across_copy(number):
+        return copy_to(
+            chunk(tensor, number),
+            chunk(tensor, number),
+            sent_across.at[number],
+            got_across.at[number],
+            tensor=across,
+        )
+
+    def sibling_copy(number):
+        return copy_to(
+            chunk(tensor, number),
+            chunk(tensor, number),
+            sent_sibling.at[number],
+            got_sibling.at[number],
+            tensor=sibling,
+        )
+
+    def on_copy(number):
+        return copy_to(
+            chunk(across, number),
+            chunk(across, number),
+            sent_on.at[number],
+            got_on.at[number],
+            tensor=sibling,
+        )
+
+    forward_rows = own_forward_ref.shape[0]
+
+    def forward_place(rank):
+        return forward_ref.at[pl.ds(pl.multiple_of(rank * forward_rows, forward_rows), forward_rows), :]
+
+    def relay_copy(origin, upward):
+        place = forward_place(origin)
+        side = 0 if upward else 1
+        return copy_to(
+            place,
+            place,
+            sent_forward.at[side, origin],
+            got_forward.at[origin],
+            fsdp=fsdp + 1 if upward else fsdp - 1,
+        )
+
+    def forward_own():
+        return pltpu.make_async_copy(own_forward_ref, forward_place(fsdp), own_forward)
+
+    def relay(origin, upward):
+        @pl.when(fsdp < groups - 1 if upward else fsdp > 0)
+        def _():
+            relay_copy(origin, upward).start()
+
+    def from_below(distance, act):
+        @pl.when(fsdp >= distance)
+        def _():
+            act(fsdp - distance, True)
+
+    def from_above(distance, act):
+        @pl.when(fsdp + distance < groups)
+        def _():
+            act(fsdp + distance, False)
+
+    def hand_over(distance):
+        def act(origin, upward):
+            relay_copy(origin, upward).wait_recv()
+            relay(origin, upward)
+
+        from_below(distance, act)
+        from_above(distance, act)
+
+    def finish_forward():
+        def sent(origin, upward):
+            @pl.when(fsdp < groups - 1 if upward else fsdp > 0)
+            def _():
+                relay_copy(origin, upward).wait_send()
+
+        sent(fsdp, True)
+        sent(fsdp, False)
+        for distance in range(1, groups):
+            from_below(distance, sent)
+            from_above(distance, sent)
+
+    def take(numbers):
+        for number in numbers:
+            block_copy(number).wait_recv()
+            across_copy(number).start()
+            sibling_copy(number).start()
+
+    def pass_on(numbers):
+        for number in numbers:
+            across_copy(number).wait_recv()
+            on_copy(number).start()
+
+    @pl.when(step == 0)
+    def _():
+        shard_own().start()
+        greet(
+            [{"fsdp": lax.rem(fsdp + away, groups)} for away in range(1, groups)]
+            + [{"context": 1 - context}, {"tensor": sibling}, {"tensor": across}]
+        )
+        for away in range(1, groups):
+            shard_copy(away).start()
+        for number in range(chunks):
+            block_copy(number).start()
+        forward_own().start()
+        take(range(chunks - 1))
+        shard_own().wait()
+        for away in range(1, groups):
+            shard_copy(away).wait_recv()
+        for number in range(groups):
+            weight_ref[number * shards.shape[1] : (number + 1) * shards.shape[1], :] = shards[number]
+        forward_own().wait()
+        relay(fsdp, True)
+        relay(fsdp, False)
+        weight_t[...] = weight_ref[...].T
+
+    @pl.when(step == 1)
+    def _():
+        take([chunks - 1])
+        pass_on(range(chunks // 2))
+
+    @pl.when(step == 2)
+    def _():
+        pass_on(range(chunks // 2, chunks))
+
+    half = 4
+
+    for distance in range(1, groups):
+
+        @pl.when(step == 1 + 2 * distance)
+        def _():
+            hand_over(distance)
+
+    @pl.when(step < half)
+    def _():
+        rows[...] = rows_ref[0]
+
+    @pl.when(step == half + 1)
+    def _():
+        for number in range(chunks):
+            sibling_copy(number).wait_recv()
+
+    @pl.when(step == half + 3)
+    def _():
+        for number in range(chunks):
+            on_copy(number).wait_recv()
+
+    @pl.when(step >= half)
+    def _():
+        rows[...] = arrived[quarter_at(step - half, tensor)]
+
+    inputs = rows[...].astype(f32).T
     center = inputs - jnp.mean(inputs, axis=0, keepdims=True)
     scaling = lax.rsqrt(jnp.mean(center * center, axis=0, keepdims=True) + EPSILON)
     hat = center * scaling
     hat_ref[...] = hat.astype(bf16)
     scale_ref[...] = scaling
     entry = (hat * gain_ref[...] + shift_ref[...]).astype(bf16)
-    projected = product(weight_ref[...], entry)
+    projected = product(weight_t[...], entry)
     cosine = cosine_ref[...]
     sine = sine_ref[...]
     tokens = cosine.shape[1]
@@ -148,16 +385,35 @@
     norms += [jnp.zeros_like(norms[0])] * (norm_ref.shape[0] - len(norms))
     norm_ref[...] = jnp.concatenate(norms, axis=0)
 
-
-def entry_call(base, rows, row_index, gain, shift, weight, cosine, sine, segment, earlier, tile):
+    @pl.when(step == pl.num_programs(0) - 1)
+    def _():
+        for away in range(1, groups):
+            shard_copy(away).wait_send()
+        for number in range(chunks):
+            block_copy(number).wait_send()
+            across_copy(number).wait_send()
+            sibling_copy(number).wait_send()
+            on_copy(number).wait_send()
+        finish_forward()
+
+
+def entry_call(tokens, shard, forward_shard, gain, shift, cosine, sine, segment, groups, tile):
     length = cosine.shape[1]
-    width, depth = weight.shape
+    shard_rows, width = shard.shape
+    depth = shard_rows * groups
     heads = width // (3 * HDIM)
-    steps = rows.shape[1] // tile
-    lanes = lambda i, base: (0, base[0] + i)
-    heads_lanes = lambda i, base: (0, 0, base[0] + i)
-    heads_rows = lambda i, base: (0, base[0] + i, 0)
-    whole = lambda i, base: (0, 0)
+    half = tokens.shape[1] // tile
+    chunks = 4
+
+    def place(i):
+        context = lax.axis_index("context")
+        other = (1 - context) * half + quarter_at(jnp.maximum(i - half, 0), lax.axis_index("tensor"))
+        return jnp.where(i < half, context * half + i, other)
+
+    lanes = lambda i: (0, place(i))
+    heads_lanes = lambda i: (0, 0, place(i))
+    heads_rows = lambda i: (0, place(i), 0)
+    whole = lambda i: (0, 0)
     shapes = [
         jax.ShapeDtypeStruct((heads, WIDE, length), bf16),
         jax.ShapeDtypeStruct((heads, length, WIDE), bf16),
@@ -167,43 +423,61 @@
         jax.ShapeDtypeStruct((depth, length), bf16),
         jax.ShapeDtypeStruct((1, length), f32),
         jax.ShapeDtypeStruct((8, length), f32),
+        jax.ShapeDtypeStruct((depth, width), bf16),
+        jax.ShapeDtypeStruct((depth, forward_shard.shape[1]), bf16),
     ]
-    out_specs = [
-        pl.BlockSpec((heads, WIDE, tile), heads_lanes),
-        pl.BlockSpec((heads, tile, WIDE), heads_rows),
-        pl.BlockSpec((heads, HDIM, tile), heads_lanes),
-        pl.BlockSpec((heads, tile, WIDE), heads_rows),
-        pl.BlockSpec((heads, HDIM + 16, tile), heads_lanes),
-        pl.BlockSpec((depth, tile), lanes),
-        pl.BlockSpec((1, tile), lanes),
-        pl.BlockSpec((8, tile), lanes),
-    ]
-    operands = [rows, gain, shift, weight, cosine, sine, segment]
-    in_specs = [
-        pl.BlockSpec((1, tile, depth), lambda i, base: (base[1], i, 0)),
-        pl.BlockSpec((depth, 1), whole),
-        pl.BlockSpec((depth, 1), whole),
-        pl.BlockSpec((width, depth), whole),
-        pl.BlockSpec((HALF, tile), lanes),
-        pl.BlockSpec((HALF, tile), lanes),
-        pl.BlockSpec((1, tile), lanes),
-    ]
-    aliases = {}
-    if earlier is not None:
-        aliases = {1 + len(operands) + k: k for k in range(len(shapes))}
-        operands += list(earlier)
-        in_specs += [pl.BlockSpec(memory_space=pl.ANY)] * len(shapes)
+    dma = lambda *shape: [pltpu.SemaphoreType.DMA(shape)] * 2
     return pl.pallas_call(
-        partial(entry_kernel, heads=heads),
-        grid_spec=pltpu.PrefetchScalarGridSpec(
-            num_scalar_prefetch=1, grid=(steps,), in_specs=in_specs, out_specs=out_specs
+        partial(entry_kernel, heads=heads, groups=groups),
+        grid=(2 * half,),
+        in_specs=[
+            pl.BlockSpec(memory_space=pl.ANY),
+            pl.BlockSpec(
+                (1, tile, depth),
+                lambda i: (lax.axis_index("context"), jnp.minimum(i, half - 1), 0),
+            ),
+            pl.BlockSpec(memory_space=pl.ANY),
+            pl.BlockSpec(forward_shard.shape, whole),
+            pl.BlockSpec((depth, 1), whole),
+            pl.BlockSpec((depth, 1), whole),
+            pl.BlockSpec((HALF, tile), lanes),
+            pl.BlockSpec((HALF, tile), lanes),
+            pl.BlockSpec((1, tile), lanes),
+        ],
+        out_specs=[
+            pl.BlockSpec((heads, WIDE, tile), heads_lanes),
+            pl.BlockSpec((heads, tile, WIDE), heads_rows),
+            pl.BlockSpec((heads, HDIM, tile), heads_lanes),
+            pl.BlockSpec((heads, tile, WIDE), heads_rows),
+            pl.BlockSpec((heads, HDIM + 16, tile), heads_lanes),
+            pl.BlockSpec((depth, tile), lanes),
+            pl.BlockSpec((1, tile), lanes),
+            pl.BlockSpec((8, tile), lanes),
+            pl.BlockSpec((depth, width), whole),
+            pl.BlockSpec(memory_space=pl.ANY),
+        ],
+        out_shape=shapes,
+        scratch_shapes=[
+            pltpu.VMEM((groups, shard_rows, width), bf16),
+            pltpu.VMEM((width, depth), bf16),
+            pltpu.VMEM((tile, depth), bf16),
+            pltpu.VMEM((4, tile, depth), bf16),
+            *dma(groups - 1),
+            pltpu.SemaphoreType.DMA,
+            *dma(chunks),
+            *dma(chunks),
+            *dma(chunks),
+            *dma(chunks),
+            pltpu.SemaphoreType.DMA((2, groups)),
+            pltpu.SemaphoreType.DMA((groups,)),
+            pltpu.SemaphoreType.DMA,
+        ],
+        compiler_params=pltpu.CompilerParams(
+            vmem_limit_bytes=VMEM, collective_id=1, has_side_effects=True
         ),
-        out_shape=shapes,
-        input_output_aliases=aliases,
-        compiler_params=pltpu.CompilerParams(vmem_limit_bytes=VMEM),
-        cost_estimate=cost(2 * rows.shape[1] * depth * width, rows, weight, *shapes),
+        cost_estimate=cost(4 * tokens.shape[1] * depth * width, tokens, *shapes),
         name="entry",
-    )(jnp.stack([base, row_index]).astype(jnp.int32), *operands)
+    )(tokens, tokens, shard, forward_shard, gain, shift, cosine, sine, segment)
 
 
 def attend_kernel(range_ref, query_ref, key_ref, value_ref, out_ref, told_ref, total_ref, top_ref, *, block):
@@ -423,24 +697,6 @@
     )(ranges, queries, keys, keys_t, values, mixture, grad_mixture, cosine, sine)
 
 
-def copy_to(source, target, sent, arrived, **device):
-    return pltpu.make_async_remote_copy(
-        src_ref=source,
-        dst_ref=target,
-        send_sem=sent,
-        recv_sem=arrived,
-        device_id=device,
-        device_id_type=pl.DeviceIdType.MESH,
-    )
-
-
-def greet(devices):
-    barrier = pltpu.get_barrier_semaphore()
-    for device in devices:
-        pl.semaphore_signal(barrier, inc=1, device_id=device, device_id_type=pl.DeviceIdType.MESH)
-    pl.semaphore_wait(barrier, len(devices))
-
-
 def middle_kernel(
     mixture_ref,
     rows_ref,
@@ -450,8 +706,9 @@
     up_bias_ref,
     down_bias_ref,
     out_weight_ref,
-    up_ref,
-    down_ref,
+    own_ref,
+    other_ref,
+    across_ref,
     result_ref,
     grad_mixture_ref,
     grad_middle_ref,
@@ -473,6 +730,9 @@
     active,
     grad_hidden,
     grad_staged,
+    forward_ref,
+    landed,
+    home_grads,
     to_sibling,
     from_sibling,
     staged_up,
@@ -486,10 +746,18 @@
     sent_part,
     got_part,
     kept,
+    sent_next,
+    got_next,
+    loaded,
+    sent_other,
+    got_other,
+    sent_last,
+    got_last,
     *,
     tile,
     tiles,
     parts,
+    groups,
 ):
     step = pl.program_id(0)
     context, tensor = lax.axis_index("context"), lax.axis_index("tensor")
@@ -502,7 +770,8 @@
     group = depth // ranks
     per_sequence = tiles // 2
     per_part = tiles + 1
-    back_from = tiles + parts * per_part
+    back_from = tiles + parts * per_part - 1
+    last_step = back_from + tiles
     root = math.sqrt(2.0 / math.pi)
 
     def member(away):
@@ -537,8 +806,51 @@
             to_sibling, from_sibling.at[slot], sent_part.at[slot], got_part.at[slot], tensor=sibling
         )
 
+    across = lax.rem(tensor + 2, ranks)
+    height = depth // groups
+
+    def rows_of(number):
+        return pl.ds(number * height, height)
+
+    def next_copy(kind):
+        return copy_to(
+            forward_ref.at[kind],
+            landed.at[0, kind],
+            sent_next.at[kind],
+            got_next.at[kind],
+            tensor=sibling,
+        )
+
+    def weight_loads():
+        return [
+            pltpu.make_async_copy(own_ref, forward_ref.at[context], loaded.at[0]),
+            pltpu.make_async_copy(other_ref, forward_ref.at[1 - context], loaded.at[1]),
+            pltpu.make_async_copy(across_ref, landed.at[1, context], loaded.at[2]),
+        ]
+
+    def other_copy(kind, number):
+        place = landed.at[1, kind, rows_of(number), :]
+        return copy_to(place, place, sent_other.at[number], got_other.at[number], context=1 - context)
+
+    def last_copy(kind, number):
+        return copy_to(
+            landed.at[1, kind, rows_of(number), :],
+            landed.at[2, kind, rows_of(number), :],
+            sent_last.at[kind, number],
+            got_last.at[kind, number],
+            tensor=sibling,
+        )
+
+    def take_other(numbers):
+        for number in numbers:
+            other_copy(1 - context, number).wait_recv()
+            last_copy(1 - context, number).start()
+
     def gradient_lanes(at):
         return pl.ds(pl.multiple_of(lax.rem(at, per_sequence) * tile, tile), tile)
+
+    def sequence_of(at):
+        return lax.rem(at // per_sequence + context, 2)
 
     def gradient_copy(at, rank):
         return copy_to(
@@ -546,7 +858,7 @@
             grad_mixture_ref.at[place, :, gradient_lanes(at)],
             sent_grad.at[at, rank],
             got_grad.at[place, lax.rem(at, per_sequence)],
-            context=at // per_sequence,
+            context=sequence_of(at),
             tensor=rank,
         )
 
@@ -568,7 +880,7 @@
         )
 
     def kept_copies(slot):
-        if slot == 0:
+        if slot == 1:
             return [
                 pltpu.make_async_copy(staged_up, up_send_ref, kept.at[0]),
                 pltpu.make_async_copy(staged_down.at[0], down_keep_ref.at[0], kept.at[1]),
@@ -581,7 +893,7 @@
         ]
 
     def tile_of(at):
-        sequence = at // per_sequence
+        sequence = sequence_of(at)
         rows = pl.ds(pl.multiple_of(at * tile, tile), tile)
         mods = mod_ref[sequence]
         lanes = gradient_lanes(at)
@@ -599,16 +911,23 @@
     @pl.when(step == 0)
     def _():
         own_copy().start()
+        for one in weight_loads():
+            one.start()
         greet([member(away)[1] for away in range(1, everyone)])
-        for away in range(1, everyone):
-            mixture_copy(away).start()
+        for near in (True, False):
+            for away in range(1, everyone):
+
+                @pl.when((member(away)[0] // ranks == context) == near)
+                def _():
+                    mixture_copy(away).start()
+
         sums_ref[...] = jnp.zeros_like(sums_ref)
         bias_sums_ref[...] = jnp.zeros_like(bias_sums_ref)
         grad_out_ref[...] = jnp.zeros_like(grad_out_ref)
 
     for sequence in range(2):
 
-        @pl.when(step == sequence * per_sequence)
+        @pl.when(step == lax.rem(sequence + context, 2) * per_sequence)
         def _():
             for rank in range(ranks):
                 source = sequence * ranks + rank
@@ -620,6 +939,35 @@
                 @pl.when(place != source)
                 def _():
                     mixture_arrival(source).wait_recv()
+
+    @pl.when(step == per_sequence)
+    def _():
+        for one in weight_loads():
+            one.wait()
+        for kind in range(2):
+            next_copy(kind).start()
+        for number in range(groups):
+            other_copy(context, number).start()
+            last_copy(context, number).start()
+
+    @pl.when(step == tiles + per_part)
+    def _():
+        for kind in range(2):
+            next_copy(kind).wait_recv()
+
+    @pl.when(step == tiles + 2 * per_part - 2)
+    def _():
+        take_other(range(groups // 2))
+
+    @pl.when(step == tiles + 2 * per_part - 1)
+    def _():
+        take_other(range(groups // 2, groups))
+
+    @pl.when(step == tiles + 2 * per_part)
+    def _():
+        for kind in range(2):
+            for number in range(groups):
+                last_copy(kind, number).wait_recv()
 
     @pl.when(step < tiles)
     def _():
@@ -628,7 +976,7 @@
         attended_rows[rows, :] = attended
         _, hat, _ = normal(attended, gate_one)
         entry = (hat * gain_two + shift_two).astype(bf16)
-        grad_output = (gate_two * (cotangent_ref[...].astype(f32) * valid_ref[rows, :])).astype(bf16)
+        grad_output = (gate_two * (cotangent_ref[...].astype(f32) * valid_ref[...])).astype(bf16)
         entry_rows[rows, :] = entry
         entry_columns[:, rows] = entry.T
         grad_output_rows[rows, :] = grad_output
@@ -640,68 +988,78 @@
     position = (step - tiles) // per_part
     in_parts = (step >= tiles) & (step < back_from)
 
-    @pl.when(in_parts & (inner < tiles))
-    def _():
+    def part_tile(up, down):
         rows = pl.ds(pl.multiple_of(inner * tile, tile), tile)
         number = part_at(position, tensor)
-        hidden = product(entry_rows[rows, :], up_ref[0]) + up_bias_ref[0]
+        hidden = product(entry_rows[rows, :], up[...]) + up_bias_ref[0]
         square = hidden * hidden
         bent = jnp.tanh(root * hidden * (1.0 + 0.044715 * square))
         half = 0.5 * (1.0 + bent)
         activated = (hidden * half).astype(bf16)
         slope = half + (0.5 * root) * hidden * (1.0 - bent * bent) * (1.0 + 0.134145 * square)
-        grads = (product(grad_output_rows[rows, :], down_ref[0]) * slope).astype(bf16)
-        output_rows[rows, :] += against(activated, down_ref[0])
-        grad_entry_rows[rows, :] += against(grads, up_ref[0])
+        grads = (product(grad_output_rows[rows, :], down[...]) * slope).astype(bf16)
+        output_rows[rows, :] += against(activated, down[...])
+        grad_entry_rows[rows, :] += against(grads, up[...])
         active[rows, :] = activated
         grad_hidden[rows, :] = grads
         bias_sums_ref[number] += jnp.sum(grads.astype(f32), axis=0, keepdims=True)
 
+    @pl.when(in_parts & (inner < tiles) & (position == 0))
+    def _():
+        part_tile(forward_ref.at[0], forward_ref.at[1])
+
+    @pl.when(in_parts & (inner < tiles) & (position > 0))
+    def _():
+        place = lax.rem((position - 1) * 2, 3)
+        part_tile(landed.at[place, 0], landed.at[place, 1])
+
+    def products(other):
+        at = rows_of(other)
+        return [
+            product(entry_columns[at, :], grad_hidden[...]),
+            product(grad_output_columns[at, :], active[...]),
+        ]
+
+    def gather_home(slot, own):
+        part_copy(slot).wait_recv()
+        if slot:
+            for one in kept_copies(0):
+                one.wait()
+        for other in range(groups):
+            for kind, (staged, term) in enumerate(zip((staged_up, staged_down), own(other))):
+                total = (term + from_sibling[slot, kind, rows_of(other), :].astype(f32)).astype(bf16)
+                staged[context, other] = total[: height // 2]
+                staged[1 - context, other] = total[height // 2 :]
+        for one in kept_copies(slot):
+            one.start()
+
     for turn in range(parts):
 
-        @pl.when(step == tiles + turn * per_part + tiles)
+        @pl.when(step == (tiles + turn * per_part + tiles if turn < parts - 1 else last_step))
         def _():
-            slot = turn // 2
-            if turn % 2 == 0:
-                if slot:
-                    part_copy(0).wait_send()
-            else:
-                part_copy(slot).wait_recv()
-                if slot:
-                    for one in kept_copies(0):
-                        one.wait()
-            groups = up_keep_ref.shape[1]
-            height = depth // groups
+            if turn == 2:
+                gather_home(0, lambda other: [home_grads[kind, rows_of(other), :].astype(f32) for kind in range(2)])
+                part_copy(0).wait_send()
+            if turn == 3:
+                gather_home(1, products)
+                return
+            target = home_grads if turn == 0 else to_sibling
             for other in range(groups):
-                at = pl.ds(other * height, height)
-                up = product(entry_columns[at, :], grad_hidden[...])
-                down = product(grad_output_columns[at, :], active[...])
-                if turn % 2 == 0:
-                    to_sibling[0, at, :] = up.astype(bf16)
-                    to_sibling[1, at, :] = down.astype(bf16)
-                else:
-                    up = (up + from_sibling[slot, 0, at, :].astype(f32)).astype(bf16)
-                    down = (down + from_sibling[slot, 1, at, :].astype(f32)).astype(bf16)
-                    staged_up[context, other] = up[: height // 2]
-                    staged_up[1 - context, other] = up[height // 2 :]
-                    staged_down[context, other] = down[: height // 2]
-                    staged_down[1 - context, other] = down[height // 2 :]
-            if turn % 2 == 0:
-                part_copy(slot).start()
-            else:
-                for one in kept_copies(slot):
-                    one.start()
-
-    @pl.when(step >= back_from)
-    def _():
-        at = step - back_from
-        sequence = at // per_sequence
+                for kind, term in enumerate(products(other)):
+                    target[kind, rows_of(other), :] = term.astype(bf16)
+            if turn:
+                part_copy(turn - 1).start()
+
+    @pl.when((step >= back_from) & (step < last_step))
+    def _():
+        at = lax.rem(step - back_from + per_sequence, tiles)
+        sequence = sequence_of(at)
         rows, mixture_t, (gate_one, _, gain_two, gate_two) = tile_of(at)
         attended = attended_rows[rows, :]
         middle, hat, scaling = normal(attended, gate_one)
         output = output_rows[rows, :]
         grad_entry = grad_entry_rows[rows, :]
-        grad_result = cotangent_ref[...].astype(f32) * valid_ref[rows, :]
+        grad_result = cotangent_ref[...].astype(f32) * valid_ref[...]
         result_ref[...] = (middle + gate_two * output).astype(bf16)
         grad_lifted = grad_entry * gain_two
         grad_middle = grad_result + scaling * (
@@ -736,7 +1094,7 @@
         lines += [jnp.zeros_like(lines[0])] * (sums_ref.shape[1] - len(lines))
         sums_ref[sequence] += jnp.concatenate(lines, axis=0)
 
-    @pl.when(step == back_from + tiles - 1)
+    @pl.when(step == last_step)
     def _():
         for source in range(everyone):
             for number in range(per_sequence):
@@ -747,7 +1105,7 @@
 
         for at in range(tiles):
             for rank in range(ranks):
-                own = (at // per_sequence == context) & (tensor == rank)
+                own = (sequence_of(at) == context) & (tensor == rank)
 
                 @pl.when(own)
                 def _():
@@ -759,40 +1117,51 @@
 
         for away in range(1, everyone):
             mixture_copy(away).wait_send()
+        for kind in range(2):
+            next_copy(kind).wait_send()
+        for number in range(groups):
+            other_copy(context, number).wait_send()
+            for kind in range(2):
+                last_copy(kind, number).wait_send()
         part_copy(1).wait_send()
         for one in kept_copies(1):
             one.wait()
 
 
 def part_at(position, tensor):
-    core = lax.rem(tensor, 2)
-    chip = tensor // 2
-    away = jnp.where(position < 2, 1 - chip, chip)
-    other = jnp.where(lax.rem(position, 2) == 0, 1 - core, core)
-    return away * 2 + other
+    return quarter_at(jnp.where(position < 2, position, 5 - position), tensor)
 
 
 def middle_call(
-    mixture, rows, cotangent, valid, mods, up_bias, down_bias, out_weight, up, down, groups, tile
+    mixture, rows, cotangent, valid, mods, up_bias, down_bias, out_weight, own_weight, other_weight, across, groups, tile
 ):
     pieces, group, own = mixture.shape
     tokens, depth = rows.shape
-    parts, _, part_width = up.shape
+    parts, _, part_width = up_bias.shape
     tiles = tokens // tile
     per_sequence = tiles // 2
     per_part = tiles + 1
-    back_from = tiles + parts * per_part
+    back_from = tiles + parts * per_part - 1
     half = depth // groups // 2
 
+    def in_order(at):
+        sequence = lax.rem(at // per_sequence + lax.axis_index("context"), 2)
+        return sequence, lax.rem(at, per_sequence)
+
+    def back_number(i):
+        return lax.rem(jnp.clip(i - back_from, 0, tiles - 1) + per_sequence, tiles)
+
     def token_tile(i):
-        return jnp.where(i < tiles, i, jnp.where(i < back_from, 0, i - back_from)), 0
+        at = jnp.where(i < tiles, i, back_number(i))
+        sequence, number = in_order(at)
+        return sequence * per_sequence + number, 0
 
     def part_block(i):
         position = jnp.clip((i - tiles) // per_part, 0, parts - 1)
         return part_at(position, lax.axis_index("tensor")), 0, 0
 
     def back_tile(i):
-        return jnp.maximum(i - back_from, 0)
+        return in_order(back_number(i))
 
     whole2 = lambda i: (0, 0)
     whole3 = lambda i: (0, 0, 0)
@@ -801,26 +1170,29 @@
     kept = jax.ShapeDtypeStruct((2, groups, half, part_width), bf16)
     wide = (tokens, depth)
     return pl.pallas_call(
-        partial(middle_kernel, tile=tile, tiles=tiles, parts=parts),
-        grid=(back_from + tiles,),
+        partial(middle_kernel, tile=tile, tiles=tiles, parts=parts, groups=groups),
+        grid=(back_from + tiles + 1,),
         in_specs=[
             hbm,
             pl.BlockSpec((tile, depth), token_tile),
             pl.BlockSpec((tile, depth), token_tile),
-            pl.BlockSpec((tokens, 1), whole2, pipeline_mode=once),
+            pl.BlockSpec((tile, 1), token_tile),
             pl.BlockSpec(mods.shape, whole3, pipeline_mode=once),
             pl.BlockSpec((1, 1, part_width), part_block),
             pl.BlockSpec((1, depth), whole2, pipeline_mode=once),
             pl.BlockSpec((depth, depth), whole2, pipeline_mode=once),
-            pl.BlockSpec((1, depth, part_width), part_block),
-            pl.BlockSpec((1, depth, part_width), part_block),
+            hbm,
+            hbm,
+            hbm,
         ],
         out_specs=[
-            pl.BlockSpec((tile, depth), lambda i: (back_tile(i), 0)),
+            pl.BlockSpec(
+                (tile, depth), lambda i: (back_tile(i)[0] * per_sequence + back_tile(i)[1], 0)
+            ),
             hbm,
             pl.BlockSpec(
                 (1, depth, tile),
-                lambda i: (back_tile(i) // per_sequence, 0, lax.rem(back_tile(i), per_sequence)),
+                lambda i: (back_tile(i)[0], 0, back_tile(i)[1]),
             ),
             pl.BlockSpec((depth, depth), whole2),
             pl.BlockSpec((2, 8, depth), whole3),
@@ -855,6 +1227,9 @@
             pltpu.VMEM((tokens, part_width), bf16),
             pltpu.VMEM((tiles, 4, group, tile), bf16),
             pltpu.VMEM((2, depth, part_width), bf16),
+            pltpu.VMEM((3, 2, depth, part_width), bf16),
+            pltpu.VMEM((2, depth, part_width), bf16),
+            pltpu.VMEM((2, depth, part_width), bf16),
             pltpu.VMEM((2, 2, depth, part_width), bf16),
             pltpu.VMEM((2, groups, half, part_width), bf16),
             pltpu.VMEM((2, groups, half, part_width), bf16),
@@ -867,13 +1242,17 @@
             pltpu.SemaphoreType.DMA((2,)),
             pltpu.SemaphoreType.DMA((2,)),
             pltpu.SemaphoreType.DMA((6,)),
+            *[pltpu.SemaphoreType.DMA((2,))] * 2,
+            pltpu.SemaphoreType.DMA((3,)),
+            *[pltpu.SemaphoreType.DMA((groups,))] * 2,
+            *[pltpu.SemaphoreType.DMA((2, groups))] * 2,
         ],
         compiler_params=pltpu.CompilerParams(
             vmem_limit_bytes=VMEM_MOST, collective_id=2, has_side_effects=True
         ),
-        cost_estimate=cost(6 * tokens * depth * (depth + 3 * parts * part_width), rows, up, down),
+        cost_estimate=cost(6 * tokens * depth * (depth + 3 * parts * part_width), rows, rows, rows),
         name="middle",
-    )(mixture, rows, cotangent, valid, mods, up_bias, down_bias, out_weight, up, down)
+    )(mixture, rows, cotangent, valid, mods, up_bias, down_bias, out_weight, own_weight, other_weight, across)
 
 
 def entry_back_kernel(
@@ -930,6 +1309,8 @@
     sent_result,
     got_result,
     moved,
+    taken,
+    held,
     weight_total,
     sums,
     part,
@@ -992,11 +1373,15 @@
         other = lax.rem(plane + away, in_plane)
         return {"context": other // ranks, "tensor": lax.rem(other, ranks)}
 
-    def up_copy():
-        return copy_to(up_ref.at[1], up_in, sent_up, got_up, context=1 - context)
-
-    def down_copy():
-        return copy_to(down_ref.at[0], down_in, sent_down, got_down, tensor=across)
+    def up_copy(other):
+        return copy_to(
+            up_ref.at[1, other], up_in.at[other], sent_up.at[other], got_up.at[other], context=1 - context
+        )
+
+    def down_copy(other):
+        return copy_to(
+            down_ref.at[0, other], down_in.at[other], sent_down.at[other], got_down.at[other], tensor=across
+        )
 
     def loads():
         return [
@@ -1048,13 +1433,19 @@
 
     def result_copies():
         return [
-            copy_to(source, target, sent_result.at[k], got_result.at[k], tensor=sibling)
+            copy_to(held.at[k], target, sent_result.at[k], got_result.at[k], tensor=sibling)
             for k, source, target in result_places()
         ]
 
+    def result_loads():
+        return [
+            pltpu.make_async_copy(source, held.at[k], taken.at[k])
+            for k, source, target in result_places()
+        ]
+
     def result_moves():
         return [
-            pltpu.make_async_copy(source, target, moved.at[k]) for k, source, target in result_places()
+            pltpu.make_async_copy(held.at[k], target, moved.at[k]) for k, source, target in result_places()
         ]
 
     def part_copy(tile):
@@ -1109,36 +1500,36 @@
             [plane_member(away) for away in range(1, in_plane)]
             + [group_away(away) for away in range(2, everyone)]
         )
-        up_copy().start()
-        down_copy().start()
+        for away in range(1, groups + 1):
+            other = lax.rem(fsdp + away, groups)
+            up_copy(other).start()
+            down_copy(other).start()
         out_copy().start()
         for away in range(1, in_plane):
             small_copy(away).start()
-        for one in result_copies() + result_moves() + loads():
+        for one in result_loads() + loads():
             one.start()
         weight_total[...] = jnp.zeros_like(weight_total)
         sums[...] = jnp.zeros_like(sums)
 
+    @pl.when(step == 2)
+    def _():
+        for one in result_loads():
+            one.wait()
+        for one in result_copies() + result_moves():
+            one.start()
+
     def grads():
         return jnp.concatenate([grad_query_ref[...], grad_key_ref[...], grad_value_ref[...]], axis=0)
 
     @pl.when(step < tiles)
     def _():
-        entry = (hat_ref[...].astype(f32) * gain_ref[...] + shift_ref[...]).astype(bf16)
-        weight_total[...] += against(entry, grads())
-
-    @pl.when(step == tiles - 1)
-    def _():
-        for other in range(groups):
-            piece[other] = weight_total[other * weight_rows : (other + 1) * weight_rows].astype(bf16)
-        for away in range(1, groups):
-            piece_copy(away).start()
-
-    @pl.when((step >= tiles) & (step < 2 * tiles))
-    def _():
-        tile = step - tiles
-        grad_entry = product(weight_ref[...], grads())
+        tile = step
+        columns = grads()
+        grad_entry = product(weight_ref[...], columns)
         hat = hat_ref[...].astype(f32)
+        lifted = hat * gain_ref[...]
+        weight_total[...] += against((lifted + shift_ref[...]).astype(bf16), columns)
         grad_lifted = grad_entry * gain_ref[...]
         term = scale_ref[...] * (
             grad_lifted
@@ -1155,16 +1546,23 @@
             sums[0] += grad_entry[:, lane : lane + WIDE]
             sums[1] += weighted[:, lane : lane + WIDE]
 
-    @pl.when((step >= tiles + 1) & (step < 2 * tiles + 1))
-    def _():
-        tile = step - tiles - 1
+    @pl.when(step == tiles - 1)
+    def _():
+        for other in range(groups):
+            piece[other] = weight_total[other * weight_rows : (other + 1) * weight_rows].astype(bf16)
+        for away in range(1, groups):
+            piece_copy(away).start()
+
+    @pl.when((step >= 1) & (step < tiles + 1))
+    def _():
+        tile = step - 1
         part_copy(tile).wait_recv()
         pair[tile] = (part[tile, core].astype(f32) + part_in[tile].astype(f32)).astype(bf16)
         pair_copy(tile).start()
 
-    @pl.when((step >= tiles + 2) & (step < 2 * tiles + 2))
-    def _():
-        tile = step - tiles - 2
+    @pl.when((step >= 3) & (step < tiles + 3))
+    def _():
+        tile = step - 3
         pair_copy(tile).wait_recv()
         total = (pair[tile, chip_x].astype(f32) + pair_in[tile].astype(f32)).astype(bf16)
 
@@ -1177,13 +1575,13 @@
         def _():
             out_ref[context, tile - half] = total
 
-    @pl.when((step >= tiles + 5) & (step < tiles + 5 + half))
-    def _():
-        tile = step - tiles - 5
+    @pl.when((step >= tiles - 1) & (step < tiles - 1 + half))
+    def _():
+        tile = step - tiles + 1
         chip_copy(tile).wait_recv()
         out_ref[1 - context, tile] = chip_in[tile]
 
-    @pl.when(step == tiles)
+    @pl.when(step == 4)
     def _():
         for away in range(1, in_plane):
             small_copy(away).wait_recv()
@@ -1191,19 +1589,22 @@
         for away in range(1, groups):
             sum_copy(away).start()
 
-    @pl.when(step == tiles + 2)
-    def _():
-        for one in loads():
-            one.wait()
-        up_copy().wait_recv()
-        down_copy().wait_recv()
-        for other in range(groups):
+    for away in range(1, groups + 1):
+
+        @pl.when(step == 1 + away)
+        def _():
+            if away == 1:
+                for one in loads():
+                    one.wait()
+            other = lax.rem(fsdp + away, groups)
+            up_copy(other).wait_recv()
+            down_copy(other).wait_recv()
             slices[other, 0] = (up_own[other].astype(f32) + up_in[other].astype(f32)).astype(bf16)
             slices[other, 1] = (down_own[other].astype(f32) + down_in[other].astype(f32)).astype(bf16)
-        for away in range(1, groups):
-            slice_copy(away).start()
-
-    @pl.when(step == tiles + 6)
+            if away < groups:
+                slice_copy(away).start()
+
+    @pl.when(step == tiles)
     def _():
         total = slices[fsdp].astype(f32)
         for away in range(1, groups):
@@ -1212,7 +1613,7 @@
         context_slice[...] = total.astype(bf16)
         context_copy().start()
 
-    @pl.when(step == tiles + 4)
+    @pl.when(step == tiles + 2)
     def _():
         total = piece[fsdp].astype(f32)
         for away in range(1, groups):
@@ -1221,19 +1622,19 @@
         block_piece[...] = total.astype(bf16)
         block_copy().start()
 
-    @pl.when(step == tiles + 7)
+    @pl.when(step == tiles + 2)
     def _():
         block_copy().wait_recv()
         grad_weight_ref[...] = block_piece[...].astype(f32) + block_in[...].astype(f32)
 
-    @pl.when(step == 2 * tiles - 1)
+    @pl.when(step == tiles - 1)
     def _():
         rows = [jnp.sum(sums[kind].T, axis=0, keepdims=True) for kind in range(2)]
         rank_sums[...] = jnp.concatenate(rows + [jnp.zeros((6, depth), f32)], axis=0)
         for away in range(1, ranks):
             rank_copy(away).start()
 
-    @pl.when(step == 2 * tiles)
+    @pl.when(step == tiles)
     def _():
         for away in range(1, ranks):
             rank_copy(away).wait_recv()
@@ -1242,7 +1643,7 @@
         for away in range(1, everyone):
             group_copy(away).start()
 
-    @pl.when(step == 2 * tiles + 1)
+    @pl.when(step == tiles + 2)
     def _():
         all_small_ref[fsdp] = small_sum[...]
         for away in range(1, groups):
@@ -1255,8 +1656,9 @@
         pieces_ref[1 - context] = context_in[...]
         out_copy().wait()
         grad_out_sum_ref[...] = grad_out_ref[...].astype(f32) + out_in[...].astype(f32)
-        up_copy().wait_send()
-        down_copy().wait_send()
+        for other in range(groups):
+            up_copy(other).wait_send()
+            down_copy(other).wait_send()
         for away in range(1, in_plane):
             small_copy(away).wait_send()
         for one in result_copies() + result_moves():
@@ -1320,7 +1722,7 @@
 
     def lanes(step):
         first = (1 - lax.axis_index("context")) * half
-        return 0, lax.rem(first + lax.rem(jnp.minimum(step, 2 * tiles - 1), tiles), tiles)
+        return 0, lax.rem(first + jnp.minimum(step, tiles - 1), tiles)
 
     whole = lambda step: (0, 0)
     whole3 = lambda step: (0, 0, 0)
@@ -1330,7 +1732,7 @@
     piece = up.shape[1:]
     return pl.pallas_call(
         partial(entry_back_kernel, tiles=tiles, groups=groups),
-        grid=(2 * tiles + 2,),
+        grid=(tiles + 3,),
         in_specs=[
             pl.BlockSpec((group, tile), lanes),
             pl.BlockSpec((group, tile), lanes),
@@ -1378,7 +1780,8 @@
             pltpu.VMEM((groups - 1, *small.shape), f32),
             pltpu.VMEM(grad_out.shape, bf16),
             pltpu.SemaphoreType.DMA((2,)),
-            *[pltpu.SemaphoreType.DMA] * 4,
+            *dma(groups),
+            *dma(groups),
             *dma(groups - 1),
             *[pltpu.SemaphoreType.DMA] * 2,
             *dma(7),
@@ -1386,6 +1789,8 @@
             *[pltpu.SemaphoreType.DMA] * 2,
             *dma(4),
             pltpu.SemaphoreType.DMA((4,)),
+            pltpu.SemaphoreType.DMA((4,)),
+            pltpu.VMEM((4, *result.shape[1:]), bf16),
             pltpu.VMEM((depth, 3 * group), f32),
             pltpu.VMEM((2, depth, WIDE), f32),
             pltpu.VMEM((tiles, 2, 2, rows, tile), bf16),
@@ -1470,18 +1875,9 @@
 
     mine = lax.dynamic_slice_in_dim(tokens, tensor_rank * quarter, quarter, axis=1)
     partner = [(k, (k + 1) % context) for k in range(context)]
-    arrived = lax.ppermute(
-        lax.dynamic_index_in_dim(mine, lax.rem(context_rank + 1, context), 0, keepdims=True),
-        "context",
-        partner,
-    )
-    other_rows = lax.all_gather(arrived, "tensor", axis=1, tiled=True)
 
     by_kind = w_qkv.reshape(-1, heads, 3, HDIM).transpose(0, 2, 1, 3).reshape(-1, 3 * group)
-    qkv = lax.all_gather(by_kind, "fsdp", axis=0, tiled=True)
     both = ("tensor", "fsdp")
-    up = lax.all_gather(w_up, both, axis=0, tiled=True).reshape(tensor, depth, part_width)
-    down = lax.all_gather(w_down.T, both, axis=0, tiled=True).reshape(tensor, depth, part_width)
     out_weight = (
         lax.all_gather(w_out, both, axis=0, tiled=False)
         .reshape(tensor, fsdp, group, depth // fsdp)
@@ -1489,13 +1885,10 @@
         .reshape(depth, depth)
     )
 
-    all_steps = lax.all_gather(steps, "fsdp", axis=0, tiled=True)
+    numbers = jnp.arange(table.shape[0], dtype=jnp.int32)
     ada_full = ada_w.astype(f32)
-    choose = (all_steps[:, None] == jnp.arange(table.shape[0], dtype=jnp.int32)[None, :]).astype(f32)
-    before = exact_product(choose, table.astype(f32))
-    embedding, silu_back = jax.vjp(jax.nn.silu, before)
-    modulation = exact_product(embedding, ada_full) + ada_b.astype(f32)
-    local_mods = lax.dynamic_slice_in_dim(modulation, fsdp_rank * sequences, sequences, axis=0)
+    raw = exact_product((steps[:, None] == numbers[None, :]).astype(f32), table.astype(f32))
+    local_mods = exact_product(jax.nn.silu(raw), ada_full) + ada_b.astype(f32)
     local_mods = local_mods.reshape(sequences, 6, depth)
     gain_first, gain_second = gain_one.astype(f32), gain_two.astype(f32)
     own_mods = lax.dynamic_index_in_dim(local_mods, context_rank, 0, keepdims=False)
@@ -1522,21 +1915,21 @@
     first_key = jnp.sum(jnp.where(same, starts[:, None], 0), axis=0)[::tile]
     last_key = jnp.sum(jnp.where(same, ends[:, None], 0), axis=0)[tile - 1 :: tile]
 
-    entry = partial(
-        entry_call,
-        gain=gain_column,
-        shift=shift_column,
-        weight=qkv.T,
-        cosine=cosine,
-        sine=sine,
-        segment=segment[None, :],
+    queries, keys, keys_t, values, values_t, hat_t, scaling, norms, qkv, forward = entry_call(
+        tokens,
+        by_kind,
+        jnp.where(context_rank == 0, w_up, w_down.T),
+        gain_column,
+        shift_column,
+        cosine,
+        sine,
+        segment[None, :],
+        groups=fsdp,
         tile=tile,
     )
-    per_block = own_rows // tile
-    made = entry(context_rank * per_block, tokens, context_rank, earlier=None)
-    other = lax.rem(context_rank + context - 1, context)
-    made = entry(other * per_block, other_rows, jnp.zeros_like(other), earlier=made)
-    queries, keys, keys_t, values, values_t, hat_t, scaling, norms = made
+    across = [(k, (k + 2) % tensor) for k in range(tensor)]
+    across_weight = lax.ppermute(forward, "tensor", across)
+    other_weight = lax.ppermute(forward, "context", partner)
     largest = jnp.max(norms, axis=1)[: 2 * heads].reshape(heads, 2)
     safe = jnp.max(largest[:, 0] * largest[:, 1]) <= SAFE_EXPONENT**2
     ranges = jnp.stack(
@@ -1572,13 +1965,13 @@
         b_up.astype(f32).reshape(tensor, 1, part_width),
         b_down.astype(f32)[None, :],
         out_weight,
-        up,
-        down,
+        forward,
+        other_weight,
+        across_weight,
         fsdp,
         tile=min(tile, 256),
     )
     result = result.reshape(sequences, quarter, depth)
-    across = [(k, (k + 2) % tensor) for k in range(tensor)]
     result_in = lax.ppermute(result, "tensor", across)
     middle_in = lax.ppermute(
         lax.dynamic_index_in_dim(grad_middle, 1 - context_rank, 0, keepdims=False), "context", partner
@@ -1590,7 +1983,12 @@
         ]
     )
     small_rows = small.shape[0]
-    small = jnp.pad(small, ((0, -small_rows % 8), (0, 0)))
+    cond = raw.shape[1]
+    leads = (context_rank == 0) & (tensor_rank == 0)
+    embedded = jnp.concatenate([raw, steps.astype(f32)[:, None]], axis=1)
+    embedded = jnp.pad(jnp.where(leads, embedded, 0.0), ((0, 0), (0, depth - cond - 1)))
+    small = jnp.concatenate([small, embedded])
+    small = jnp.pad(small, ((0, -small.shape[0] % 8), (0, 0)))
 
     up_sum = add(up_keep, lax.ppermute(up_send, "tensor", across))
     down_sum = add(down_keep, lax.ppermute(down_send, "context", partner))
@@ -1633,8 +2031,12 @@
     grad_w_up = pieces[0]
     grad_w_down = pieces[1].T
     grad_w_out = grad_out.reshape(group, depth // fsdp)
-    small_sums = small[:, :10].reshape(fsdp * sequences, 5, depth)
-    grad_b_up = jnp.sum(small[:, 10:small_rows], axis=0).reshape(-1)
+    small_sums = small[:, : 5 * sequences].reshape(fsdp * sequences, 5, depth)
+    embedded = small[:, small_rows : small_rows + sequences].reshape(fsdp * sequences, depth)
+    choose = (embedded[:, cond].astype(jnp.int32)[:, None] == numbers[None, :]).astype(f32)
+    embedding, silu_back = jax.vjp(jax.nn.silu, embedded[:, :cond])
+    modulation = exact_product(embedding, ada_full) + ada_b.astype(f32)
+    grad_b_up = jnp.sum(small[:, 5 * sequences : small_rows], axis=0).reshape(-1)
     grad_b_down = jnp.sum(small_sums[:, 4], axis=0)
     grad_gain_two = jnp.sum(small_sums[:, 2] * (1.0 + modulation[:, 4 * depth : 5 * depth]), axis=0)
     middle_mod = jnp.concatenate(

time: 540 us -> 477 us (0.88); the launches traced: 530 us -> 475 us
  waiting for transfers between devices: 67.7 us -> 0.06 us
  Pallas kernels: 337 us -> 387 us
  blocking collectives: 28.5 us -> 0 us
    all_gather x3 -> x0, waiting for transfers between devices: 48.2 us -> none  [the longest x1 48.2 us: by_sequence(): lax.all_gather(w_down.T, both, axis=0, tiled=True)]
    pallas_call x2 -> x1, Pallas kernels: 21.3 us -> 56 us  [entry_call(): pl.pallas_call(partial(entry_kernel, heads=heads, groups=groups), grid=(2...]
    pallas_call x1, Pallas kernels: 33.1 us -> 57.4 us  [attend_call(): pl.pallas_call(partial(attend_kernel, block=block), grid_spec=pltpu.Prefe...]
    all_gather x1 -> x0, blocking collectives: 19.8 us -> none  [by_sequence(): qkv = lax.all_gather(by_kind, 'fsdp', axis=0, tiled=True)]
    pallas_call x1, Pallas kernels: 105 us -> 86.4 us  [entry_back_call(): pl.pallas_call(partial(entry_back_kernel, tiles=tiles, groups=groups), gr...]
    ppermute x1 -> x2, waiting for transfers between devices: 17.5 us -> 0.01 us  [the longest x1 0.01 us: by_sequence(): other_weight = lax.ppermute(forward, 'context', partner)]
    pallas_call x1, Pallas kernels: 95.5 us -> 105 us  [middle_call(): pl.pallas_call(partial(middle_kernel, tile=tile, tiles=tiles, parts=parts...]
    unnamed x1 -> x0, blocking collectives: 8.66 us -> none
  transfers between devices with their start and end apart: 10 -> 8, of which waited for: 2 -> 0; matrix products, arithmetic and copies ran while one was open for 9% -> 7% of each run, Pallas kernels for 26% -> 29%
where the time goes in v3:
time: 477 us; the launch traced here: 475 us
  Pallas kernels  387 us (81%)
  local copies, waits for them, and re-layouts  39.9 us (8%)
  other arithmetic  18.9 us (4%)
  between operations  15.4 us (3%)
  starting transfers between devices  7.07 us (1%)
  matrix products  6.82 us (1%)
    pallas_call x1, Pallas kernels, middle_call(): pl.pallas_call(partial(middle_kernel, tile=tile, tiles=tiles, parts=parts...  105 us
    pallas_call x1, Pallas kernels, entry_back_call(): pl.pallas_call(partial(entry_back_kernel, tiles=tiles, groups=groups), gr...  86.4 us
    pallas_call x1, Pallas kernels, attend_back_call(): pl.pallas_call(partial(attend_back_kernel, block=block), grid_spec=pltpu....  82.2 us
    pallas_call x1, Pallas kernels, attend_call(): pl.pallas_call(partial(attend_kernel, block=block), grid_spec=pltpu.Prefe...  57.4 us
    pallas_call x1, Pallas kernels, entry_call(): pl.pallas_call(partial(entry_kernel, heads=heads, groups=groups), grid=(2...  56 us
    unnamed x55, local copies, waits for them, and re-layouts  9.68 us
  transfers between devices with their start and end apart: 8, of which 0 were waited for; matrix products, arithmetic and copies ran while one was open for 7% of the time, Pallas kernels for 29%

profile of v3, /device:TPU:0, one launch (start us, length us, event | category | flops | bytes accessed | tf_op | source)
XLA Modules:
  0.0 475.5 jit_solution(18241935330060558449)
XLA Ops:
  7.3 1.2 copy.58
  8.6 0.9 copy.60.shard_ref
  10.8 0.9 broadcast_in_dim.78.gain_ref
  11.7 1.0 copy.62.shift_ref
  13.0 2.8 multiply_sine_fusion
  15.8 0.7 bitcast_select_fusion.own_forward_ref
  16.6 56.0 %entry.1 = (bf16[3,128,4096]{2,1,0:T(8,128)(2,1)}, bf16[3,4096,128]{2,1,0:T(8,128)(2,1)}, bf16[3,64,4096]{2,1,0:T(8,128)(2,1)}, bf16[3,4096,128]{2,1,0:T(8,128)(...) custom-call(bf16[2,2048,768]{2,1,0:T(8,128)(2,1)} %rows_ref.1, ...), custom_call_target="tpu_custom_call" | custom-call | flops 3623878656 | bytes 27770880 | tf_op jit(solution)/shard_map/entry/pallas_call | solution.py:430
  72.6 2.8 collective-permute-start
  75.7 1.1 reduce_max.28
  76.8 0.7 multiply_reduce_fusion
  78.2 0.6 add_add_fusion.range_ref
  78.9 57.4 %attend.1 = (bf16[8,192,512]{2,1,0:T(8,128)(2,1)}, bf16[3,128,4096]{2,1,0:T(8,128)(2,1)}) custom-call(s32[3,8]{1,0:T(4,128)} %add_add_fusion.range_ref, bf16[3,128,4096]{2,1,0:T(8,128)(2,1)} %get-tuple-element.52.query_ref, bf16[3,4096,128]{2,1,0:T(8,128)(2,1)} %get-tuple-element.53.key_ref, bf16[3,80,4096]{2,1,0:T(8,128)(2,1)} %get-tuple-element.54.value_ref), custom_call_target="tpu_custom_call" | custom-call | flops 25769803776 | bytes 8257536 | tf_op jit(solution)/shard_map/attend/pallas_call | solution.py:555
  136.4 1.0 copy.86
  137.5 0.6 reshape.166
  138.1 0.6 reshape.168.down_bias_ref
  138.8 3.8 constant_dynamic-slice_fusion
  142.6 0.7 maximum_maximum_fusion.mod_ref
  143.3 2.6 copy.107
  145.9 2.3 reshape.152.out_weight_ref
  148.2 105.3 %middle.1 = (bf16[1024,768]{1,0:T(8,128)(2,1)}, bf16[8,192,512]{2,1,0:T(8,128)(2,1)}, bf16[2,768,512]{2,1,0:T(8,128)(2,1)}, f32[768,768]{1,0:T(8,128)}, f32[2,8,...) custom-call(bf16[8,192,512]{2,1,0:T(8,128)(2,1)} %get-tuple-element., ...), custom_call_target="tpu_custom_call" | custom-call | flops 47110422528 | bytes 4718592 | tf_op jit(solution)/shard_map/middle/pallas_call | solution.py:1172
  253.5 1.3 collective-permute-start.2
  255.2 1.2 collective-permute-start.4
  256.4 1.2 dynamic-slice_bitcast_fusion
  257.6 1.2 collective-permute-start.5
  258.9 2.8 convert_element_type.84
  261.7 3.5 reshape.154
  265.1 1.4 copy.106
  266.6 3.9 reshape.155
  270.5 82.2 %attend_back.1 = (bf16[192,4096]{1,0:T(8,128)(2,1)}, bf16[192,4096]{1,0:T(8,128)(2,1)}, bf16[192,4096]{1,0:T(8,128)(2,1)}) custom-call(s32[3,8]{1,0:T(4,128)} %add_add_fusion.range_ref, bf16[3,128,4096]{2,1,0:T(8,128)(2,1)} %get-tuple-element.55.query_ref, bf16[3,4096,128]{2,1,0:T(8,128)(2,1)} %get-tuple-element.53.key_ref, ...), custom_call_target="tpu_custom_call" | custom-call | flops 64424509440 | bytes 9437184 | tf_op jit(solution)/shard_map/attend_back/pallas_call | solution.py:666
  352.8 0.6 select_maximum_fusion.small_ref
  353.4 2.7 add_convert_fusion.1.up_ref
  356.1 2.6 add_convert_fusion.down_ref
  358.7 86.4 %entry_back.1 = (bf16[2,4,192,512]{3,2,1,0:T(8,128)(2,1)}, f32[192,576]{1,0:T(8,128)}, f32[8,8,768]{2,1,0:T(8,128)}, f32[4,16,768]{2,1,0:T(8,128)}, bf16[2,2,96,...) custom-call(bf16[192,4096]{1,0:T(8,128)(2,1)} %get-tuple-element.69.grad_query_ref, ...), custom_call_target="tpu_custom_call" | custom-call | flops 7247757312 | bytes 14155776 | tf_op jit(solution)/shard_map/entry_back/pallas_call | solution.py:1733
  445.1 1.0 slice.111
  446.1 1.0 copy.70
  447.1 0.9 slice.108
  448.8 0.7 slice_reduce_fusion.1
  449.5 0.6 fusion.1
  450.1 1.0 fusion.41
  451.1 3.5 fusion.34
  454.6 0.6 reduce_sum.69
  455.7 2.0 copy.84
  457.9 1.0 copy.77
  458.9 0.8 reshape.162
  459.8 1.1 fusion.40
  460.9 0.6 reshape.163
  461.5 1.0 fusion.9
  462.5 5.9 %copy.115 = bf16[2,2048,768]{2,1,0:T(8,128)(2,1)} copy(bf16[2,2048,768]{2,1,0:T(8,128)(2,1)} %get-tuple-element.152) | data formatting | bytes 12582912
  (105 shorter events, 4.5 us)
Async XLA Ops:
  7.2 2.9 copy-start
  7.2 2.2 copy-start.16
  7.2 2.2 copy-start.21
  7.2 2.2 copy-start.22
  7.2 136.1 %all-gather.3.cloned.1.call-start = ((), (), s32[]{:S(2)}) async-start(), calls=%async_computation.2 | async-start | bytes 1671168 | tf_op jit(solution)/shard_map/all_gather | solution.py:1882
  7.3 3.4 copy-start.14
  7.3 3.4 copy-start.17
  9.4 0.6 copy-start.10
  10.1 5.7 %copy-start.7 = (bf16[192,768]{1,0:T(8,128)(2,1)S(1)}, bf16[192,768]{1,0:T(8,128)(2,1)}, u32[]{:S(2)}) copy-start(bf16[192,768]{1,0:T(8,128)(2,1)} %param.26) | copy-start | bytes 884740
  10.1 5.7 %copy-start.8 = (bf16[768,192]{0,1:T(8,128)(2,1)S(1)}, bf16[768,192]{0,1:T(8,128)(2,1)}, u32[]{:S(2)}) copy-start(bf16[768,192]{0,1:T(8,128)(2,1)} %param.28) | copy-start | bytes 884740
  10.7 5.8 %copy-start.9 = (s32[1,4096]{1,0:T(1,128)}, s32[1,4096]{1,0:T(1,128)S(1)}, u32[]{:S(2)}) copy-start(s32[1,4096]{1,0:T(1,128)S(1)} %constant_dynamic-slice_fusion.2.segment_ref) | copy-start | bytes 49156
  72.6 75.6 %collective-permute-start = (bf16[768,768]{1,0:T(8,128)(2,1)}, bf16[768,768]{1,0:T(8,128)(2,1)}, u32[]{:S(2)}, u32[]{:S(2)}) collective-permute-start(bf16[768,768]{1,0:T(8,128)(2,1)} %get-tuple-element.59.own_ref), channel_id=1, source_target_pairs={{0,4},{4,0},{1,5},{5,1},{2,6},{6,2},{3,7},{7,3},{8,12},{12,8},{9,1... | collective-permute-start | bytes 3538952 | tf_op jit(solution)/shard_map/ppermute | solution.py:1932
  75.4 72.8 %collective-permute-start.1 = (bf16[768,768]{1,0:T(8,128)(2,1)}, bf16[768,768]{1,0:T(8,128)(2,1)}, u32[]{:S(2)}, u32[]{:S(2)}) collective-permute-start(bf16[768,768]{1,0:T(8,128)(2,1)} %get-tuple-element.59.own_ref), channel_id=1, source_target_pairs={{0,2},{1,3},{2,0},{3,1},{4,6},{5,7},{6,4},{7,5},{8,10},{9,11},{10,... | collective-permute-start | bytes 3538952 | tf_op jit(solution)/shard_map/ppermute | solution.py:1931
  75.4 283.3 %reduce-scatter.2.cloned.1.call-start = ((), (), s32[]{:S(2)}) async-start(), calls=%async_computation.1 | async-start | bytes 1253376 | tf_op jit(solution)/shard_map/reduce_scatter | solution.py:2001
  78.9 58.6 %copy-start.19 = (bf16[768]{0:T(1024)(128)(2,1)S(1)}, bf16[768]{0:T(1024)(128)(2,1)}, u32[]{:S(2)}) copy-start(bf16[768]{0:T(1024)(128)(2,1)} %param.25) | copy-start | bytes 4612
  78.9 58.6 %copy-start.18 = (bf16[3072]{0:T(1024)(128)(2,1)S(1)}, bf16[3072]{0:T(1024)(128)(2,1)}, u32[]{:S(2)}) copy-start(bf16[3072]{0:T(1024)(128)(2,1)} %param.27) | copy-start | bytes 18436
  78.9 59.2 %copy-start.20 = (bf16[768]{0:T(1024)(128)(2,1)S(1)}, bf16[768]{0:T(1024)(128)(2,1)}, u32[]{:S(2)}) copy-start(bf16[768]{0:T(1024)(128)(2,1)} %param.29) | copy-start | bytes 4612
  253.5 99.9 %collective-permute-start.2 = (bf16[2,4,96,768]{3,2,1,0:T(8,128)(2,1)}, bf16[2,4,96,768]{3,2,1,0:T(8,128)(2,1)}, u32[]{:S(2)}, u32[]{:S(2)}) collective-permute-start(bf16[2,4,96,768]{3,2,1,0:T(8,128)(2,1)} %get-tuple-element.63), channel_id=1, source_target_pairs={{0,2},{1,3},{2,0},{3,1},{4,6},{5,7},{6,4},{7,5},{8,10},{9,11},{10,... | collective-permute-start | bytes 3538952 | tf_op jit(solution)/shard_map/ppermute | solution.py:1993
  254.8 101.3 %collective-permute-start.3 = (bf16[2,4,96,768]{3,2,1,0:T(8,128)(2,1)}, bf16[2,4,96,768]{3,2,1,0:T(8,128)(2,1)}, u32[]{:S(2)}, u32[]{:S(2)}) collective-permute-start(bf16[2,4,96,768]{3,2,1,0:T(8,128)(2,1)} %get-tuple-element.65), channel_id=1, source_target_pairs={{0,4},{4,0},{1,5},{5,1},{2,6},{6,2},{3,7},{7,3},{8,12},{12,8},{9,1... | collective-permute-start | bytes 3538952 | tf_op jit(solution)/shard_map/ppermute | solution.py:1994
  255.2 103.4 %collective-permute-start.4 = (bf16[2,512,768]{2,1,0:T(8,128)(2,1)}, bf16[2,512,768]{2,1,0:T(8,128)(2,1)}, u32[]{:S(2)}, u32[]{:S(2)}) collective-permute-start(bf16[2,512,768]{2,1,0:T(8,128)(2,1)} %bitcast.111), channel_id=1, source_target_pairs={{0,2},{1,3},{2,0},{3,1},{4,6},{5,7},{6,4},{7,5},{8,10},{9,11},{10,... | collective-permute-start | bytes 4718600 | tf_op jit(solution)/shard_map/ppermute | solution.py:1975
  257.6 101.0 %collective-permute-start.5 = (bf16[768,512]{1,0:T(8,128)(2,1)S(1)}, bf16[768,512]{1,0:T(8,128)(2,1)}, u32[]{:S(2)}, u32[]{:S(2)}) collective-permute-start(bf16[768,512]{1,0:T(8,128)(2,1)S(1)} %dynamic-slice_bitcast_fusion), channel_id=1, source_target_pairs={{0,4},{4,0},{1,5},{5,1},{2,6},{6,2},{3,7},{7,3},{8,12},{12,8},{9,1... | collective-permute-start | bytes 2359304 | tf_op jit(solution)/shard_map/ppermute | solution.py:1976
  270.5 82.2 %copy-start.15 = (f32[4,1,768]{2,1,0:T(1,128)S(1)}, f32[4,1,768]{2,1,0:T(1,128)}, u32[]{:S(2)}) copy-start(f32[4,1,768]{2,1,0:T(1,128)} %get-tuple-element.77) | copy-start | bytes 36868
  270.5 82.2 %copy-start.13 = (f32[2,8,768]{2,1,0:T(8,128)S(1)}, f32[2,8,768]{2,1,0:T(8,128)}, u32[]{:S(2)}) copy-start(f32[2,8,768]{2,1,0:T(8,128)} %get-tuple-element.76) | copy-start | bytes 147460
  270.5 82.9 %copy-start.3 = (bf16[2,4,96,768]{3,2,1,0:T(8,128)(2,1)S(1)}, bf16[2,4,96,768]{3,2,1,0:T(8,128)(2,1)}, u32[]{:S(2)}) copy-start(bf16[2,4,96,768]{3,2,1,0:T(8,128)(2,1)} %get-tuple-element.62) | copy-start | bytes 3538948
  353.4 2.7 copy-start.2
  358.7 89.3 %copy-start.11 = (f32[4608]{0:T(1024)S(1)}, f32[4608]{0:T(1024)}, u32[]{:S(2)}) copy-start(f32[4608]{0:T(1024)} %copy-done.10) | copy-start | bytes 55300
  445.1 3.6 copy-start.6
  451.1 4.2 copy-start.1
  455.7 2.0 copy-start.5
  457.7 1.3 copy-start.12
  457.9 1.8 copy-start.4
Sparse Core Ops, SparseCore 0:
  75.6 40.0 all-gather.2
  270.6 60.4 reduce-scatter.1

commit v4 on v3

--- a/solution.py
+++ b/solution.py
@@ -125,7 +125,6 @@
     query_ref,
     key_ref,
     key_t_ref,
-    value_ref,
     value_t_ref,
     hat_ref,
     scale_ref,
@@ -377,11 +376,10 @@
         norms.append(jnp.sum(queries * queries, axis=0, keepdims=True))
         norms.append(jnp.sum(keys * keys, axis=0, keepdims=True))
         query_ref[head] = jnp.concatenate([queries, extra_query], axis=0).astype(bf16)
-        key_ref[head] = jnp.concatenate([keys, extra_key], axis=0).T.astype(bf16)
-        key_t_ref[head] = keys.astype(bf16)
-        wide_values = jnp.concatenate([values, extra_value], axis=0)
-        value_ref[head] = wide_values.T.astype(bf16)
-        value_t_ref[head] = wide_values[: value_t_ref.shape[1]].astype(bf16)
+        wide_keys = jnp.concatenate([keys, extra_key], axis=0)
+        key_ref[head] = wide_keys.T.astype(bf16)
+        key_t_ref[head] = wide_keys.astype(bf16)
+        value_t_ref[head] = jnp.concatenate([values, extra_value], axis=0).astype(bf16)
     norms += [jnp.zeros_like(norms[0])] * (norm_ref.shape[0] - len(norms))
     norm_ref[...] = jnp.concatenate(norms, axis=0)
 
@@ -417,9 +415,8 @@
     shapes = [
         jax.ShapeDtypeStruct((heads, WIDE, length), bf16),
         jax.ShapeDtypeStruct((heads, length, WIDE), bf16),
-        jax.ShapeDtypeStruct((heads, HDIM, length), bf16),
-        jax.ShapeDtypeStruct((heads, length, WIDE), bf16),
-        jax.ShapeDtypeStruct((heads, HDIM + 16, length), bf16),
+        jax.ShapeDtypeStruct((heads, WIDE, length), bf16),
+        jax.ShapeDtypeStruct((heads, WIDE, length), bf16),
         jax.ShapeDtypeStruct((depth, length), bf16),
         jax.ShapeDtypeStruct((1, length), f32),
         jax.ShapeDtypeStruct((8, length), f32),
@@ -447,9 +444,8 @@
         out_specs=[
             pl.BlockSpec((heads, WIDE, tile), heads_lanes),
             pl.BlockSpec((heads, tile, WIDE), heads_rows),
-            pl.BlockSpec((heads, HDIM, tile), heads_lanes),
-            pl.BlockSpec((heads, tile, WIDE), heads_rows),
-            pl.BlockSpec((heads, HDIM + 16, tile), heads_lanes),
+            pl.BlockSpec((heads, WIDE, tile), heads_lanes),
+            pl.BlockSpec((heads, WIDE, tile), heads_lanes),
             pl.BlockSpec((depth, tile), lanes),
             pl.BlockSpec((1, tile), lanes),
             pl.BlockSpec((8, tile), lanes),
@@ -480,38 +476,48 @@
     )(tokens, tokens, shard, forward_shard, gain, shift, cosine, sine, segment)
 
 
-def attend_kernel(range_ref, query_ref, key_ref, value_ref, out_ref, told_ref, total_ref, top_ref, *, block):
+def attend_kernel(
+    range_ref, query_ref, key_ref, value_ref, norm_ref, out_ref, told_ref, total_ref, top_ref, safe_ref, *, block
+):
     step = pl.program_id(0)
-    first, last = range_ref[0, step], range_ref[1, step]
+    first, count = range_ref[0, step], range_ref[1, step]
     heads = query_ref.shape[0]
     total_ref[...] = jnp.zeros_like(total_ref)
 
+    @pl.when(step == 0)
+    def _():
+        largest = 0.0
+        for head in range(heads):
+            queries, keys = norm_ref[2 * head : 2 * head + 1], norm_ref[2 * head + 1 : 2 * head + 2]
+            largest = jnp.maximum(largest, jnp.max(queries) * jnp.max(keys))
+        safe_ref[0] = (largest <= SAFE_EXPONENT**2).astype(jnp.int32)
+
     def scores(head, at):
         return product(key_ref[head, pl.ds(at, block), :], query_ref[head])
 
     def mix(head, at, weights):
         return product(value_ref[head, :, pl.ds(at, block)], weights)
 
-    @pl.when(range_ref[2, 0] == 1)
+    @pl.when(safe_ref[0] == 1)
     def _():
         top_ref[...] = jnp.zeros_like(top_ref)
 
         def body(number, carry):
-            at = pl.multiple_of(number * block, block)
+            at = pl.multiple_of(first + number * block, WIDE)
             raw = [scores(head, at) for head in range(heads)]
             weights = [jnp.exp2(one).astype(bf16) for one in raw]
             for head in range(heads):
                 total_ref[head] += mix(head, at, weights[head])
             return carry
 
-        lax.fori_loop(first, last, body, 0)
-
-    @pl.when(range_ref[2, 0] != 1)
+        lax.fori_loop(0, count, body, 0)
+
+    @pl.when(safe_ref[0] != 1)
     def _():
         top_ref[...] = jnp.full_like(top_ref, -3e38)
 
         def body(number, carry):
-            at = pl.multiple_of(number * block, block)
+            at = pl.multiple_of(first + number * block, WIDE)
             for head in range(heads):
                 raw = scores(head, at)
                 before = top_ref[head]
@@ -521,7 +527,7 @@
                 top_ref[head] = top
             return carry
 
-        lax.fori_loop(first, last, body, 0)
+        lax.fori_loop(0, count, body, 0)
 
     tile = query_ref.shape[2]
     number = lax.broadcasted_iota(jnp.int32, (16, tile), 0)
@@ -549,9 +555,9 @@
     )
 
 
-def attend_call(ranges, queries, keys, values_t, tile, block):
+def attend_call(ranges, queries, keys, values_t, norms, tile, block):
     heads, _, length = queries.shape
-    rows = values_t.shape[1]
+    rows = HDIM + 16
     return pl.pallas_call(
         partial(attend_kernel, block=block),
         grid_spec=pltpu.PrefetchScalarGridSpec(
@@ -561,6 +567,7 @@
                 pl.BlockSpec((heads, WIDE, tile), lambda i, r: (0, 0, i)),
                 pl.BlockSpec((heads, length, WIDE), lambda i, r: (0, 0, 0)),
                 pl.BlockSpec((heads, rows, length), lambda i, r: (0, 0, 0)),
+                pl.BlockSpec(norms.shape, lambda i, r: (0, 0)),
             ],
             out_specs=[
                 pl.BlockSpec((1, heads * HDIM, tile), lambda i, r: (i, 0, 0)),
@@ -569,6 +576,7 @@
             scratch_shapes=[
                 pltpu.VMEM((heads, rows, tile), f32),
                 pltpu.VMEM((heads, 1, tile), f32),
+                pltpu.SMEM((1,), jnp.int32),
             ],
         ),
         out_shape=[
@@ -578,14 +586,13 @@
         compiler_params=pltpu.CompilerParams(vmem_limit_bytes=VMEM),
         cost_estimate=cost(4 * heads * length * length * WIDE, queries, keys, values_t),
         name="attend",
-    )(ranges, queries, keys, values_t)
+    )(ranges, queries, keys, values_t, norms)
 
 
 def attend_back_kernel(
     range_ref,
     query_ref,
     key_ref,
-    key_t_ref,
     value_ref,
     mixture_ref,
     grad_ref,
@@ -595,6 +602,8 @@
     grad_key_ref,
     grad_value_ref,
     wide_ref,
+    query_rows,
+    grad_rows,
     query_total,
     key_total,
     value_total,
@@ -602,7 +611,7 @@
     block,
 ):
     step = pl.program_id(0)
-    first, last = range_ref[0, step], range_ref[1, step]
+    first, count = range_ref[0, step], range_ref[1, step]
     heads, _, tile = query_ref.shape
 
     @pl.when(step == 0)
@@ -619,21 +628,22 @@
         delta = jnp.sum(grad.astype(f32) * mixture_ref[0, at, :].astype(f32), axis=0, keepdims=True)
         wide_ref[head, :HDIM, :] = grad
         wide_ref[head, HDIM : HDIM + 16, :] = split_rows(-delta, number, 0).astype(bf16)
+        query_rows[head] = query_ref[head].T
+        grad_rows[head] = wide_ref[head].T
 
     def body(number, carry):
-        at = pl.multiple_of(number * block, block)
-        rows = pl.ds(at, block)
-        raw = [product(key_ref[head, rows, :], query_ref[head]) for head in range(heads)]
-        slope = [product(value_ref[head, rows, :], wide_ref[head]) for head in range(heads)]
+        at = pl.ds(pl.multiple_of(first + number * block, WIDE), block)
+        raw = [product(query_rows[head], key_ref[head, :, at]) for head in range(heads)]
+        slope = [product(grad_rows[head], value_ref[head, :, at]) for head in range(heads)]
         for head in range(heads):
             weights = jnp.exp2(raw[head])
             grad_scores = (weights * slope[head]).astype(bf16)
-            query_total[head] += product(key_t_ref[head, :, rows], grad_scores)
-            key_total[head, :, rows] += against(query_ref[head, :HDIM, :], grad_scores)
-            value_total[head, :, rows] += against(wide_ref[head, :HDIM, :], weights.astype(bf16))
+            value_total[head, :, at] += product(wide_ref[head, :HDIM, :], weights.astype(bf16))
+            key_total[head, :, at] += product(query_ref[head, :HDIM, :], grad_scores)
+            query_total[head] += against(key_ref[head, :HDIM, at], grad_scores)
         return carry
 
-    lax.fori_loop(first, last, body, 0)
+    lax.fori_loop(0, count, body, 0)
 
     def turned_back(grads, cosine, sine):
         front, back = grads[:HALF], grads[HALF:]
@@ -657,7 +667,7 @@
 
 
 def attend_back_call(
-    ranges, queries, keys, keys_t, values, mixture, grad_mixture, cosine, sine, tile, block
+    ranges, queries, keys_t, values_t, mixture, grad_mixture, cosine, sine, tile, block
 ):
     heads, _, length = queries.shape
     group = heads * HDIM
@@ -670,9 +680,8 @@
             grid=(length // tile,),
             in_specs=[
                 pl.BlockSpec((heads, WIDE, tile), lambda i, r: (0, 0, i)),
-                pl.BlockSpec((heads, length, WIDE), whole3),
-                pl.BlockSpec((heads, HDIM, length), whole3),
-                pl.BlockSpec((heads, length, WIDE), whole3),
+                pl.BlockSpec((heads, WIDE, length), whole3),
+                pl.BlockSpec((heads, WIDE, length), whole3),
                 pl.BlockSpec((1, group, tile), lambda i, r: (i, 0, 0)),
                 pl.BlockSpec((1, group, tile), lambda i, r: (i, 0, 0)),
                 pl.BlockSpec((HALF, length), whole2),
@@ -685,6 +694,8 @@
             ],
             scratch_shapes=[
                 pltpu.VMEM((heads, WIDE, tile), bf16),
+                pltpu.VMEM((heads, tile, WIDE), bf16),
+                pltpu.VMEM((heads, tile, WIDE), bf16),
                 pltpu.VMEM((heads, HDIM, tile), f32),
                 pltpu.VMEM((heads, HDIM, length), f32),
                 pltpu.VMEM((heads, HDIM, length), f32),
@@ -692,9 +703,9 @@
         ),
         out_shape=[jax.ShapeDtypeStruct((group, length), bf16)] * 3,
         compiler_params=pltpu.CompilerParams(vmem_limit_bytes=VMEM),
-        cost_estimate=cost(10 * heads * length * length * WIDE, queries, keys, values),
+        cost_estimate=cost(10 * heads * length * length * WIDE, queries, keys_t, values_t),
         name="attend_back",
-    )(ranges, queries, keys, keys_t, values, mixture, grad_mixture, cosine, sine)
+    )(ranges, queries, keys_t, values_t, mixture, grad_mixture, cosine, sine)
 
 
 def middle_kernel(
@@ -705,14 +716,14 @@
     mod_ref,
     up_bias_ref,
     down_bias_ref,
-    out_weight_ref,
+    out_blocks_ref,
     own_ref,
     other_ref,
     across_ref,
     result_ref,
     grad_mixture_ref,
     grad_middle_ref,
-    grad_out_ref,
+    grad_out_blocks_ref,
     sums_ref,
     bias_sums_ref,
     up_keep_ref,
@@ -720,6 +731,8 @@
     down_keep_ref,
     down_send_ref,
     own_mixture,
+    out_weight_ref,
+    grad_out_ref,
     entry_rows,
     entry_columns,
     grad_output_rows,
@@ -766,7 +779,7 @@
     place = context * ranks + tensor
     core = lax.rem(tensor, 2)
     sibling = tensor + 1 - 2 * core
-    depth = rows_ref.shape[1]
+    depth = rows_ref.shape[2]
     group = depth // ranks
     per_sequence = tiles // 2
     per_part = tiles + 1
@@ -820,6 +833,12 @@
             got_next.at[kind],
             tensor=sibling,
         )
+
+    def out_blocks():
+        for rank in range(ranks):
+            for number in range(groups):
+                rows = slice(rank * group, (rank + 1) * group)
+                yield rank * groups + number, (rows, slice(number * height, (number + 1) * height))
 
     def weight_loads():
         return [
@@ -903,7 +922,7 @@
         return rows, mixture_t, tuple(mods[k : k + 1] for k in range(4))
 
     def normal(attended, gate_one):
-        middle = rows_ref[...].astype(f32) + gate_one * attended
+        middle = rows_ref[0].astype(f32) + gate_one * attended
         center = middle - jnp.mean(middle, axis=-1, keepdims=True)
         scaling = lax.rsqrt(jnp.mean(center * center, axis=-1, keepdims=True) + EPSILON)
         return middle, center * scaling, scaling
@@ -921,6 +940,8 @@
                 def _():
                     mixture_copy(away).start()
 
+        for block, at in out_blocks():
+            out_weight_ref[at] = out_blocks_ref[block]
         sums_ref[...] = jnp.zeros_like(sums_ref)
         bias_sums_ref[...] = jnp.zeros_like(bias_sums_ref)
         grad_out_ref[...] = jnp.zeros_like(grad_out_ref)
@@ -976,7 +997,7 @@
         attended_rows[rows, :] = attended
         _, hat, _ = normal(attended, gate_one)
         entry = (hat * gain_two + shift_two).astype(bf16)
-        grad_output = (gate_two * (cotangent_ref[...].astype(f32) * valid_ref[...])).astype(bf16)
+        grad_output = (gate_two * (cotangent_ref[0].astype(f32) * valid_ref[...])).astype(bf16)
         entry_rows[rows, :] = entry
         entry_columns[:, rows] = entry.T
         grad_output_rows[rows, :] = grad_output
@@ -1059,7 +1080,7 @@
         middle, hat, scaling = normal(attended, gate_one)
         output = output_rows[rows, :]
         grad_entry = grad_entry_rows[rows, :]
-        grad_result = cotangent_ref[...].astype(f32) * valid_ref[...]
+        grad_result = cotangent_ref[0].astype(f32) * valid_ref[...]
         result_ref[...] = (middle + gate_two * output).astype(bf16)
         grad_lifted = grad_entry * gain_two
         grad_middle = grad_result + scaling * (
@@ -1096,6 +1117,8 @@
 
     @pl.when(step == last_step)
     def _():
+        for block, at in out_blocks():
+            grad_out_blocks_ref[block] = grad_out_ref[at].astype(bf16)
         for source in range(everyone):
             for number in range(per_sequence):
 
@@ -1133,10 +1156,11 @@
 
 
 def middle_call(
-    mixture, rows, cotangent, valid, mods, up_bias, down_bias, out_weight, own_weight, other_weight, across, groups, tile
+    mixture, rows, cotangent, valid, mods, up_bias, down_bias, out_blocks, own_weight, other_weight, across, groups, tile
 ):
     pieces, group, own = mixture.shape
-    tokens, depth = rows.shape
+    depth = rows.shape[2]
+    tokens = rows.shape[0] * own
     parts, _, part_width = up_bias.shape
     tiles = tokens // tile
     per_sequence = tiles // 2
@@ -1151,9 +1175,15 @@
     def back_number(i):
         return lax.rem(jnp.clip(i - back_from, 0, tiles - 1) + per_sequence, tiles)
 
+    def token_place(i):
+        return in_order(jnp.where(i < tiles, i, back_number(i)))
+
     def token_tile(i):
-        at = jnp.where(i < tiles, i, back_number(i))
-        sequence, number = in_order(at)
+        sequence, number = token_place(i)
+        return sequence, lax.axis_index("tensor") * per_sequence + number, 0
+
+    def valid_tile(i):
+        sequence, number = token_place(i)
         return sequence * per_sequence + number, 0
 
     def part_block(i):
@@ -1174,13 +1204,13 @@
         grid=(back_from + tiles + 1,),
         in_specs=[
             hbm,
-            pl.BlockSpec((tile, depth), token_tile),
-            pl.BlockSpec((tile, depth), token_tile),
-            pl.BlockSpec((tile, 1), token_tile),
+            pl.BlockSpec((1, tile, depth), token_tile),
+            pl.BlockSpec((1, tile, depth), token_tile),
+            pl.BlockSpec((tile, 1), valid_tile),
             pl.BlockSpec(mods.shape, whole3, pipeline_mode=once),
             pl.BlockSpec((1, 1, part_width), part_block),
             pl.BlockSpec((1, depth), whole2, pipeline_mode=once),
-            pl.BlockSpec((depth, depth), whole2, pipeline_mode=once),
+            pl.BlockSpec(out_blocks.shape, whole3, pipeline_mode=once),
             hbm,
             hbm,
             hbm,
@@ -1194,7 +1224,7 @@
                 (1, depth, tile),
                 lambda i: (back_tile(i)[0], 0, back_tile(i)[1]),
             ),
-            pl.BlockSpec((depth, depth), whole2),
+            pl.BlockSpec(out_blocks.shape, whole3),
             pl.BlockSpec((2, 8, depth), whole3),
             pl.BlockSpec((parts, 1, part_width), whole3),
             hbm,
@@ -1206,7 +1236,7 @@
             jax.ShapeDtypeStruct((tokens, depth), bf16),
             jax.ShapeDtypeStruct(mixture.shape, bf16),
             jax.ShapeDtypeStruct((2, depth, own), bf16),
-            jax.ShapeDtypeStruct((depth, depth), f32),
+            jax.ShapeDtypeStruct(out_blocks.shape, bf16),
             jax.ShapeDtypeStruct((2, 8, depth), f32),
             jax.ShapeDtypeStruct((parts, 1, part_width), f32),
             kept,
@@ -1216,6 +1246,8 @@
         ],
         scratch_shapes=[
             pltpu.VMEM(mixture.shape, bf16),
+            pltpu.VMEM((depth, depth), bf16),
+            pltpu.VMEM((depth, depth), f32),
             pltpu.VMEM(wide, bf16),
             pltpu.VMEM((depth, tokens), bf16),
             pltpu.VMEM(wide, bf16),
@@ -1252,7 +1284,7 @@
         ),
         cost_estimate=cost(6 * tokens * depth * (depth + 3 * parts * part_width), rows, rows, rows),
         name="middle",
-    )(mixture, rows, cotangent, valid, mods, up_bias, down_bias, out_weight, own_weight, other_weight, across)
+    )(mixture, rows, cotangent, valid, mods, up_bias, down_bias, out_blocks, own_weight, other_weight, across)
 
 
 def entry_back_kernel(
@@ -1873,17 +1905,11 @@
     heads = group // HDIM
     quarter = own_rows // tensor
 
-    mine = lax.dynamic_slice_in_dim(tokens, tensor_rank * quarter, quarter, axis=1)
     partner = [(k, (k + 1) % context) for k in range(context)]
 
     by_kind = w_qkv.reshape(-1, heads, 3, HDIM).transpose(0, 2, 1, 3).reshape(-1, 3 * group)
     both = ("tensor", "fsdp")
-    out_weight = (
-        lax.all_gather(w_out, both, axis=0, tiled=False)
-        .reshape(tensor, fsdp, group, depth // fsdp)
-        .transpose(0, 2, 1, 3)
-        .reshape(depth, depth)
-    )
+    out_blocks = lax.all_gather(w_out, both, axis=0, tiled=False)
 
     numbers = jnp.arange(table.shape[0], dtype=jnp.int32)
     ada_full = ada_w.astype(f32)
@@ -1915,7 +1941,17 @@
     first_key = jnp.sum(jnp.where(same, starts[:, None], 0), axis=0)[::tile]
     last_key = jnp.sum(jnp.where(same, ends[:, None], 0), axis=0)[tile - 1 :: tile]
 
-    queries, keys, keys_t, values, values_t, hat_t, scaling, norms, qkv, forward = entry_call(
+    low_key = first_key // WIDE * WIDE
+    high_key = (last_key + WIDE - 1) // WIDE * WIDE
+
+    def ranges_of(size):
+        count = (high_key - low_key + size - 1) // size
+        return jnp.stack([jnp.maximum(high_key - count * size, 0), count]).astype(jnp.int32)
+
+    back_block = block // 2
+    ranges, back_ranges = ranges_of(block), ranges_of(back_block)
+
+    queries, keys, keys_t, values_t, hat_t, scaling, norms, qkv, forward = entry_call(
         tokens,
         by_kind,
         jnp.where(context_rank == 0, w_up, w_down.T),
@@ -1930,21 +1966,11 @@
     across = [(k, (k + 2) % tensor) for k in range(tensor)]
     across_weight = lax.ppermute(forward, "tensor", across)
     other_weight = lax.ppermute(forward, "context", partner)
-    largest = jnp.max(norms, axis=1)[: 2 * heads].reshape(heads, 2)
-    safe = jnp.max(largest[:, 0] * largest[:, 1]) <= SAFE_EXPONENT**2
-    ranges = jnp.stack(
-        [
-            first_key // block,
-            (last_key + block - 1) // block,
-            jnp.broadcast_to(safe.astype(jnp.int32), first_key.shape),
-        ]
-    ).astype(jnp.int32)
-    mixture, told = attend_call(ranges, queries, keys, values_t, tile, block)
+    mixture, told = attend_call(ranges, queries, keys, values_t, norms, tile, block)
 
     own_segments = lax.dynamic_slice_in_dim(
         segments, context_rank * own_rows + tensor_rank * quarter, quarter, axis=1
     )
-    own_cotangent = lax.dynamic_slice_in_dim(cotangent, tensor_rank * quarter, quarter, axis=1)
     (
         result,
         grad_mixture,
@@ -1958,13 +1984,13 @@
         down_send,
     ) = middle_call(
         mixture,
-        mine.reshape(-1, depth),
-        own_cotangent.reshape(-1, depth),
+        tokens,
+        cotangent,
         (own_segments != 0).astype(f32).reshape(-1, 1),
         mods,
         b_up.astype(f32).reshape(tensor, 1, part_width),
         b_down.astype(f32)[None, :],
-        out_weight,
+        out_blocks,
         forward,
         other_weight,
         across_weight,
@@ -1992,16 +2018,10 @@
 
     up_sum = add(up_keep, lax.ppermute(up_send, "tensor", across))
     down_sum = add(down_keep, lax.ppermute(down_send, "context", partner))
-    grad_out = (
-        grad_out.astype(bf16)
-        .reshape(tensor, group, fsdp, depth // fsdp)
-        .transpose(0, 2, 1, 3)
-        .reshape(tensor * fsdp, group * (depth // fsdp) // part_width, part_width)
-    )
     grad_out = lax.psum_scatter(grad_out, both, scatter_dimension=0, tiled=True)[0]
 
     grad_query, grad_key, grad_value = attend_back_call(
-        ranges, told, keys, keys_t, values, mixture, grad_mixture, cosine, sine, tile, block
+        back_ranges, told, keys_t, values_t, mixture, grad_mixture, cosine, sine, tile, back_block
     )
     (grad_query, up_sum, down_sum, result_in, middle_in, grad_out) = lax.optimization_barrier(
         (grad_query, up_sum, down_sum, result_in, middle_in, grad_out)
@@ -2030,7 +2050,7 @@
     pieces = pieces.reshape(2, depth // fsdp, part_width).astype(f32)
     grad_w_up = pieces[0]
     grad_w_down = pieces[1].T
-    grad_w_out = grad_out.reshape(group, depth // fsdp)
+    grad_w_out = grad_out
     small_sums = small[:, : 5 * sequences].reshape(fsdp * sequences, 5, depth)
     embedded = small[:, small_rows : small_rows + sequences].reshape(fsdp * sequences, depth)
     choose = (embedded[:, cond].astype(jnp.int32)[:, None] == numbers[None, :]).astype(f32)

time: 477 us -> 446 us (0.935)
  Pallas kernels: 387 us -> 352 us
  waiting for transfers between devices: 0.06 us -> 20.8 us
  local copies, waits for them, and re-layouts: 39.9 us -> 24.4 us
    pallas_call x1, Pallas kernels: 57.4 us -> 26.8 us  [attend_call(): pl.pallas_call(partial(attend_kernel, block=block), grid_spec=pltpu.Prefe...]
    pallas_call x1, Pallas kernels: 82.2 us -> 63.4 us  [attend_back_call(): pl.pallas_call(partial(attend_back_kernel, block=block), grid_spec=pltpu....]
    pallas_call x1, Pallas kernels: 86.4 us -> 103 us  [entry_back_call(): pl.pallas_call(partial(entry_back_kernel, tiles=tiles, groups=groups), gr...]
    reshape x7 -> x0, local copies, waits for them, and re-layouts: 14.6 us -> none  [the longest x3 8.8 us: by_sequence(): grad_out = grad_out.astype(bf16).reshape(tensor, group, fsdp, depth // fs...]
    reduce_scatter x1, waiting for transfers between devices: 0.01 us -> 13.1 us  [by_sequence(): lax.psum_scatter(grad_out, both, scatter_dimension=0, tiled=True)[0]]
    all_gather x1, waiting for transfers between devices: 0.01 us -> 7.65 us  [by_sequence(): out_blocks = lax.all_gather(w_out, both, axis=0, tiled=False)]
    unnamed x55 -> x58, local copies, waits for them, and re-layouts: 9.68 us -> 10.4 us
  transfers between devices with their start and end apart: 8 -> 8, of which waited for: 0 -> 2; matrix products, arithmetic and copies ran while one was open for 7% -> 3% of each run, Pallas kernels for 29% -> 20%
where the time goes in v4:
time: 446 us; the launch traced here: 442 us
  Pallas kernels  352 us (79%)
  local copies, waits for them, and re-layouts  24.4 us (5%)
  waiting for transfers between devices  20.8 us (5%)
  other arithmetic  15.7 us (4%)
  between operations  14.9 us (3%)
  starting transfers between devices  6.96 us (2%)
  matrix products  6.82 us (2%)
    pallas_call x1, Pallas kernels, middle_call(): pl.pallas_call(partial(middle_kernel, tile=tile, tiles=tiles, parts=parts...  103 us
    pallas_call x1, Pallas kernels, entry_back_call(): pl.pallas_call(partial(entry_back_kernel, tiles=tiles, groups=groups), gr...  103 us
    pallas_call x1, Pallas kernels, attend_back_call(): pl.pallas_call(partial(attend_back_kernel, block=block), grid_spec=pltpu....  63.4 us
    pallas_call x1, Pallas kernels, entry_call(): pl.pallas_call(partial(entry_kernel, heads=heads, groups=groups), grid=(2...  55.7 us
    pallas_call x1, Pallas kernels, attend_call(): pl.pallas_call(partial(attend_kernel, block=block), grid_spec=pltpu.Prefe...  26.8 us
    reduce_scatter x1, waiting for transfers between devices, by_sequence(): lax.psum_scatter(grad_out, both, scatter_dimension=0, tiled=True)[0]  13.1 us
    unnamed x58, local copies, waits for them, and re-layouts  10.4 us
  transfers between devices with their start and end apart: 8, of which 2 were waited for; matrix products, arithmetic and copies ran while one was open for 3% of the time, Pallas kernels for 20%

profile of v4, /device:TPU:0, one launch (start us, length us, event | category | flops | bytes accessed | tf_op | source)
XLA Modules:
  0.0 441.9 jit_solution(6553705133278809114)
XLA Ops:
  7.3 1.2 copy.54
  8.6 0.9 copy.56.shard_ref
  10.1 0.6 convolution_add_fusion.1
  10.8 0.9 broadcast_in_dim.78.gain_ref
  11.7 0.9 copy.58.shift_ref
  13.0 2.8 multiply_sine_fusion
  15.8 0.7 bitcast_select_fusion.own_forward_ref
  16.5 55.7 %entry.1 = (bf16[3,128,4096]{2,1,0:T(8,128)(2,1)}, bf16[3,4096,128]{2,1,0:T(8,128)(2,1)}, bf16[3,128,4096]{2,1,0:T(8,128)(2,1)}, bf16[3,128,4096]{2,1,0:T(8,128)...) custom-call(bf16[2,2048,768]{2,1,0:T(8,128)(2,1)} %rows_ref.3, ...), custom_call_target="tpu_custom_call" | custom-call | flops 3623878656 | bytes 27377664 | tf_op jit(solution)/shard_map/entry/pallas_call | solution.py:427
  72.2 2.8 collective-permute-start
  75.3 0.6 pad_add_fusion.1.range_ref
  75.9 26.8 %attend.1 = (bf16[8,192,512]{2,1,0:T(8,128)(2,1)}, bf16[3,128,4096]{2,1,0:T(8,128)(2,1)}) custom-call(s32[2,8]{1,0:T(2,128)} %pad_add_fusion.1.range_ref, bf16[3,128,4096]{2,1,0:T(8,128)(2,1)} %get-tuple-element.50.query_ref, bf16[3,4096,128]{2,1,0:T(8,128)(2,1)} %get-tuple-element.51.key_ref, bf16[3,128,4096]{2,1,0:T(8,128)(2,1)} %get-tuple-element.52.value_ref, ...), custom_call_target="tpu_custom_call" | custom-call | flops 25769803776 | bytes 9437184 | tf_op jit(solution)/shard_map/attend/pallas_call | solution.py:561
  102.7 0.6 convert_element_type.67
  103.3 1.0 copy.80
  104.3 0.6 reshape.125
  104.9 0.6 reshape.127.down_bias_ref
  105.7 0.6 pad_add_fusion.range_ref
  106.3 0.6 maximum_select_fusion
  106.9 0.7 maximum_maximum_fusion.mod_ref
  107.6 7.6 %all-gather.3.cloned.1.call-done = bf16[3072,192]{1,0:T(8,128)(2,1)} async-done(((bf16[192,192]{1,0:T(8,128)(2,1)}), bf16[3072,192]{1,0:T(8,128)(2,1)}) %all-gather.3.cloned.1.call-update) | async-done | bytes 1179664 | tf_op jit(solution)/shard_map/all_gather | solution.py:1912
  115.2 103.4 %middle.1 = (bf16[1024,768]{1,0:T(8,128)(2,1)}, bf16[8,192,512]{2,1,0:T(8,128)(2,1)}, bf16[2,768,512]{2,1,0:T(8,128)(2,1)}, bf16[16,192,192]{2,1,0:T(8,128)(2,1)...) custom-call(bf16[8,192,512]{2,1,0:T(8,128)(2,1)} %get-tuple-element., ...), custom_call_target="tpu_custom_call" | custom-call | flops 47110422528 | bytes 18874368 | tf_op jit(solution)/shard_map/middle/pallas_call | solution.py:1202
  218.6 1.0 collective-permute-start.2
  219.7 1.5 collective-permute-start.3
  221.2 1.0 collective-permute-start.4
  222.2 2.0 dynamic-slice_bitcast_fusion
  224.2 0.6 collective-permute-start.5
  224.8 63.4 %attend_back.1 = (bf16[192,4096]{1,0:T(8,128)(2,1)}, bf16[192,4096]{1,0:T(8,128)(2,1)}, bf16[192,4096]{1,0:T(8,128)(2,1)}) custom-call(s32[2,8]{1,0:T(2,128)} %pad_add_fusion.range_ref, bf16[3,128,4096]{2,1,0:T(8,128)(2,1)} %get-tuple-element.54.query_ref, bf16[3,128,4096]{2,1,0:T(8,128)(2,1)} %get-tuple-element.55.key_ref, ...), custom_call_target="tpu_custom_call" | custom-call | flops 64424509440 | bytes 9437184 | tf_op jit(solution)/shard_map/attend_back/pallas_call | solution.py:676
  288.2 1.4 reshape.116
  289.6 1.4 select_maximum_fusion.small_ref
  291.1 2.7 add_convert_fusion.1.up_ref
  293.8 1.3 add_convert_fusion.down_ref
  295.1 13.1 %reduce-scatter.2.cloned.1.call-done = bf16[1,192,192]{2,1,0:T(8,128)(2,1)} async-done(((bf16[16,192,192]{2,1,0:T(8,128)(2,1)}), bf16[1,192,192]{2,1,0:T(8,128)(2,1)}) %reduce-scatter.2.cloned.1.call-update) | async-done | bytes 73744 | tf_op jit(solution)/shard_map/reduce_scatter | solution.py:2021
  308.3 103.0 %entry_back.1 = (bf16[2,4,192,512]{3,2,1,0:T(8,128)(2,1)}, f32[192,576]{1,0:T(8,128)}, f32[8,8,768]{2,1,0:T(8,128)}, f32[4,16,768]{2,1,0:T(8,128)}, bf16[2,2,96,...) custom-call(bf16[192,4096]{1,0:T(8,128)(2,1)} %get-tuple-element.67.grad_query_ref, ...), custom_call_target="tpu_custom_call" | custom-call | flops 7247757312 | bytes 14155776 | tf_op jit(solution)/shard_map/entry_back/pallas_call | solution.py:1765
  411.3 1.0 slice.91
  412.3 1.0 copy.64
  413.3 0.9 slice.88
  414.3 0.6 convolution_add_fusion
  415.0 0.7 slice_reduce_fusion.1
  415.7 0.6 fusion.1
  416.3 1.0 fusion.41
  417.3 3.5 fusion.33
  420.8 0.6 reduce_sum.69
  421.9 2.0 copy.78
  424.2 1.0 copy.71
  425.3 1.1 fusion.40
  426.4 0.6 reshape.122
  427.0 1.0 fusion.9
  428.0 5.9 %copy.106 = bf16[2,2048,768]{2,1,0:T(8,128)(2,1)} copy(bf16[2,2048,768]{2,1,0:T(8,128)(2,1)} %get-tuple-element.152) | data formatting | bytes 12582912
  433.9 0.7 copy.107
  (98 shorter events, 2.7 us)
Async XLA Ops:
  7.2 2.9 copy-start
  7.2 2.2 copy-start.16
  7.2 2.2 copy-start.22
  7.2 2.2 copy-start.23
  7.2 108.0 %all-gather.3.cloned.1.call-start = ((), (), s32[]{:S(2)}) async-start(), calls=%async_computation.2 | async-start | bytes 1671168 | tf_op jit(solution)/shard_map/all_gather | solution.py:1912
  7.3 3.4 copy-start.14
  7.3 3.5 copy-start.17
  9.4 0.6 copy-start.11
  10.1 5.7 %copy-start.7 = (bf16[192,768]{1,0:T(8,128)(2,1)S(1)}, bf16[192,768]{1,0:T(8,128)(2,1)}, u32[]{:S(2)}) copy-start(bf16[192,768]{1,0:T(8,128)(2,1)} %param.26) | copy-start | bytes 884740
  10.1 5.7 %copy-start.8 = (bf16[768,192]{0,1:T(8,128)(2,1)S(1)}, bf16[768,192]{0,1:T(8,128)(2,1)}, u32[]{:S(2)}) copy-start(bf16[768,192]{0,1:T(8,128)(2,1)} %param.28) | copy-start | bytes 884740
  10.7 5.8 %copy-start.9 = (s32[1,4096]{1,0:T(1,128)}, s32[1,4096]{1,0:T(1,128)S(1)}, u32[]{:S(2)}) copy-start(s32[1,4096]{1,0:T(1,128)S(1)} %constant_dynamic-slice_fusion.segment_ref) | copy-start | bytes 49156
  72.2 35.3 %collective-permute-start = (bf16[768,768]{1,0:T(8,128)(2,1)}, bf16[768,768]{1,0:T(8,128)(2,1)S(1)}, u32[]{:S(2)}, u32[]{:S(2)}) collective-permute-start(bf16[768,768]{1,0:T(8,128)(2,1)} %get-tuple-element.57.own_ref), channel_id=1, source_target_pairs={{0,4},{4,0},{1,5},{5,1},{2,6},{6,2},{3,7},{7,3},{8,12},{12,8},{9,1... | collective-permute-start | bytes 3538952 | tf_op jit(solution)/shard_map/ppermute | solution.py:1968
  75.0 32.6 %collective-permute-start.1 = (bf16[768,768]{1,0:T(8,128)(2,1)}, bf16[768,768]{1,0:T(8,128)(2,1)}, u32[]{:S(2)}, u32[]{:S(2)}) collective-permute-start(bf16[768,768]{1,0:T(8,128)(2,1)} %get-tuple-element.57.own_ref), channel_id=1, source_target_pairs={{0,2},{1,3},{2,0},{3,1},{4,6},{5,7},{6,4},{7,5},{8,10},{9,11},{10,... | collective-permute-start | bytes 3538952 | tf_op jit(solution)/shard_map/ppermute | solution.py:1967
  75.0 233.2 %reduce-scatter.2.cloned.1.call-start = ((), (), s32[]{:S(2)}) async-start(), calls=%async_computation.1 | async-start | bytes 1671168 | tf_op jit(solution)/shard_map/reduce_scatter | solution.py:2021
  75.8 28.5 %copy-start.19 = (bf16[768]{0:T(1024)(128)(2,1)S(1)}, bf16[768]{0:T(1024)(128)(2,1)}, u32[]{:S(2)}) copy-start(bf16[768]{0:T(1024)(128)(2,1)} %param.25) | copy-start | bytes 4612
  75.8 28.5 %copy-start.18 = (bf16[3072]{0:T(1024)(128)(2,1)S(1)}, bf16[3072]{0:T(1024)(128)(2,1)}, u32[]{:S(2)}) copy-start(bf16[3072]{0:T(1024)(128)(2,1)} %param.27) | copy-start | bytes 18436
  75.8 29.1 %copy-start.20 = (bf16[768]{0:T(1024)(128)(2,1)S(1)}, bf16[768]{0:T(1024)(128)(2,1)}, u32[]{:S(2)}) copy-start(bf16[768]{0:T(1024)(128)(2,1)} %param.29) | copy-start | bytes 4612
  107.6 7.7 %copy-start.21 = (bf16[768,768]{1,0:T(8,128)(2,1)}, bf16[768,768]{1,0:T(8,128)(2,1)S(1)}, u32[]{:S(2)}) copy-start(bf16[768,768]{1,0:T(8,128)(2,1)S(1)} %collective-permute-done.other_ref) | copy-start | bytes 3538948
  218.6 72.5 %collective-permute-start.2 = (bf16[2,4,96,768]{3,2,1,0:T(8,128)(2,1)}, bf16[2,4,96,768]{3,2,1,0:T(8,128)(2,1)}, u32[]{:S(2)}, u32[]{:S(2)}) collective-permute-start(bf16[2,4,96,768]{3,2,1,0:T(8,128)(2,1)} %get-tuple-element.61), channel_id=1, source_target_pairs={{0,2},{1,3},{2,0},{3,1},{4,6},{5,7},{6,4},{7,5},{8,10},{9,11},{10,... | collective-permute-start | bytes 3538952 | tf_op jit(solution)/shard_map/ppermute | solution.py:2019
  219.7 74.1 %collective-permute-start.3 = (bf16[2,4,96,768]{3,2,1,0:T(8,128)(2,1)}, bf16[2,4,96,768]{3,2,1,0:T(8,128)(2,1)S(1)}, u32[]{:S(2)}, u32[]{:S(2)}) collective-permute-start(bf16[2,4,96,768]{3,2,1,0:T(8,128)(2,1)} %get-tuple-element.63), channel_id=1, source_target_pairs={{0,4},{4,0},{1,5},{5,1},{2,6},{6,2},{3,7},{7,3},{8,12},{12,8},{9,1... | collective-permute-start | bytes 3538952 | tf_op jit(solution)/shard_map/ppermute | solution.py:2020
  221.2 73.9 %collective-permute-start.4 = (bf16[2,512,768]{2,1,0:T(8,128)(2,1)}, bf16[2,512,768]{2,1,0:T(8,128)(2,1)}, u32[]{:S(2)}, u32[]{:S(2)}) collective-permute-start(bf16[2,512,768]{2,1,0:T(8,128)(2,1)} %bitcast.98), channel_id=1, source_target_pairs={{0,2},{1,3},{2,0},{3,1},{4,6},{5,7},{6,4},{7,5},{8,10},{9,11},{10,... | collective-permute-start | bytes 4718600 | tf_op jit(solution)/shard_map/ppermute | solution.py:2001
  224.2 70.9 %collective-permute-start.5 = (bf16[768,512]{1,0:T(8,128)(2,1)}, bf16[768,512]{1,0:T(8,128)(2,1)}, u32[]{:S(2)}, u32[]{:S(2)}) collective-permute-start(bf16[768,512]{1,0:T(8,128)(2,1)} %dynamic-slice_bitcast_fusion), channel_id=1, source_target_pairs={{0,4},{4,0},{1,5},{5,1},{2,6},{6,2},{3,7},{7,3},{8,12},{12,8},{9,1... | collective-permute-start | bytes 2359304 | tf_op jit(solution)/shard_map/ppermute | solution.py:2002
  224.8 63.4 %copy-start.15 = (f32[4,1,768]{2,1,0:T(1,128)S(1)}, f32[4,1,768]{2,1,0:T(1,128)}, u32[]{:S(2)}) copy-start(f32[4,1,768]{2,1,0:T(1,128)} %get-tuple-element.75) | copy-start | bytes 36868
  224.8 66.3 %copy-start.3 = (bf16[2,4,96,768]{3,2,1,0:T(8,128)(2,1)S(1)}, bf16[2,4,96,768]{3,2,1,0:T(8,128)(2,1)}, u32[]{:S(2)}) copy-start(bf16[2,4,96,768]{3,2,1,0:T(8,128)(2,1)} %get-tuple-element.60) | copy-start | bytes 3538948
  291.1 2.7 copy-start.2
  308.3 106.0 %copy-start.12 = (f32[4608]{0:T(1024)S(1)}, f32[4608]{0:T(1024)}, u32[]{:S(2)}) copy-start(f32[4608]{0:T(1024)} %copy-done.11) | copy-start | bytes 55300
  411.3 3.6 copy-start.6
  411.3 4.4 copy-start.13
  417.3 4.2 copy-start.1
  421.9 2.0 copy-start.5
  423.9 1.3 copy-start.4
  428.0 5.9 %copy-start.10 = (f32[192,192]{1,0:T(8,128)S(1)}, f32[192,192]{1,0:T(8,128)}, u32[]{:S(2)}) copy-start(f32[192,192]{1,0:T(8,128)} %get-tuple-element.159) | copy-start | bytes 442372
Sparse Core Ops, SparseCore 0:
  75.1 40.0 all-gather.2
  224.9 83.2 reduce-scatter.1

commit v5 on v4

--- a/solution.py
+++ b/solution.py
@@ -17,6 +17,8 @@
 SAFE_EXPONENT = 60.0
 EPSILON = 1e-05
 VMEM = 56 * 2**20
+PART_TILES = 2
+PART_CUTS = 1
 VMEM_MOST = 60 * 2**20
 
 
@@ -782,7 +784,8 @@
     depth = rows_ref.shape[2]
     group = depth // ranks
     per_sequence = tiles // 2
-    per_part = tiles + 1
+    part_tiles = tiles // PART_TILES
+    per_part = part_tiles + 1
     back_from = tiles + parts * per_part - 1
     last_step = back_from + tiles
     root = math.sqrt(2.0 / math.pi)
@@ -976,11 +979,11 @@
         for kind in range(2):
             next_copy(kind).wait_recv()
 
-    @pl.when(step == tiles + 2 * per_part - 2)
+    @pl.when(step == tiles + 2 * per_part - 1)
     def _():
         take_other(range(groups // 2))
 
-    @pl.when(step == tiles + 2 * per_part - 1)
+    @pl.when(step == tiles + 2 * per_part)
     def _():
         take_other(range(groups // 2, groups))
 
@@ -1010,44 +1013,47 @@
     in_parts = (step >= tiles) & (step < back_from)
 
     def part_tile(up, down):
-        rows = pl.ds(pl.multiple_of(inner * tile, tile), tile)
         number = part_at(position, tensor)
-        hidden = product(entry_rows[rows, :], up[...]) + up_bias_ref[0]
-        square = hidden * hidden
-        bent = jnp.tanh(root * hidden * (1.0 + 0.044715 * square))
-        half = 0.5 * (1.0 + bent)
-        activated = (hidden * half).astype(bf16)
-        slope = half + (0.5 * root) * hidden * (1.0 - bent * bent) * (1.0 + 0.134145 * square)
-        grads = (product(grad_output_rows[rows, :], down[...]) * slope).astype(bf16)
-        output_rows[rows, :] += against(activated, down[...])
-        grad_entry_rows[rows, :] += against(grads, up[...])
-        active[rows, :] = activated
-        grad_hidden[rows, :] = grads
-        bias_sums_ref[number] += jnp.sum(grads.astype(f32), axis=0, keepdims=True)
-
-    @pl.when(in_parts & (inner < tiles) & (position == 0))
+        size = tile * PART_TILES // PART_CUTS
+        for sub in range(PART_CUTS):
+            rows = pl.ds(pl.multiple_of((inner * PART_CUTS + sub) * size, size), size)
+            hidden = product(entry_rows[rows, :], up[...]) + up_bias_ref[0]
+            square = hidden * hidden
+            bent = jnp.tanh(root * hidden * (1.0 + 0.044715 * square))
+            half = 0.5 * (1.0 + bent)
+            activated = (hidden * half).astype(bf16)
+            slope = half + (0.5 * root) * hidden * (1.0 - bent * bent) * (1.0 + 0.134145 * square)
+            grads = (product(grad_output_rows[rows, :], down[...]) * slope).astype(bf16)
+            output_rows[rows, :] += against(activated, down[...])
+            grad_entry_rows[rows, :] += against(grads, up[...])
+            active[rows, :] = activated
+            grad_hidden[rows, :] = grads
+            bias_sums_ref[number] += jnp.sum(grads.astype(f32), axis=0, keepdims=True)
+
+    @pl.when(in_parts & (inner < part_tiles) & (position == 0))
     def _():
         part_tile(forward_ref.at[0], forward_ref.at[1])
 
-    @pl.when(in_parts & (inner < tiles) & (position > 0))
+    @pl.when(in_parts & (inner < part_tiles) & (position > 0))
     def _():
         place = lax.rem((position - 1) * 2, 3)
         part_tile(landed.at[place, 0], landed.at[place, 1])
 
-    def products(other):
-        at = rows_of(other)
-        return [
-            product(entry_columns[at, :], grad_hidden[...]),
-            product(grad_output_columns[at, :], active[...]),
-        ]
+    def products():
+        both = [product(entry_columns[...], grad_hidden[...]), product(grad_output_columns[...], active[...])]
+        return lambda other: [one[other * height : (other + 1) * height] for one in both]
+
+    def kept_terms():
+        return lambda other: [home_grads[kind, rows_of(other), :].astype(f32) for kind in range(2)]
 
     def gather_home(slot, own):
         part_copy(slot).wait_recv()
         if slot:
             for one in kept_copies(0):
                 one.wait()
+        terms = own()
         for other in range(groups):
-            for kind, (staged, term) in enumerate(zip((staged_up, staged_down), own(other))):
+            for kind, (staged, term) in enumerate(zip((staged_up, staged_down), terms(other))):
                 total = (term + from_sibling[slot, kind, rows_of(other), :].astype(f32)).astype(bf16)
                 staged[context, other] = total[: height // 2]
                 staged[1 - context, other] = total[height // 2 :]
@@ -1056,17 +1062,18 @@
 
     for turn in range(parts):
 
-        @pl.when(step == (tiles + turn * per_part + tiles if turn < parts - 1 else last_step))
+        @pl.when(step == (tiles + turn * per_part + part_tiles if turn < parts - 1 else last_step))
         def _():
             if turn == 2:
-                gather_home(0, lambda other: [home_grads[kind, rows_of(other), :].astype(f32) for kind in range(2)])
+                gather_home(0, kept_terms)
                 part_copy(0).wait_send()
             if turn == 3:
                 gather_home(1, products)
                 return
             target = home_grads if turn == 0 else to_sibling
+            terms = products()
             for other in range(groups):
-                for kind, term in enumerate(products(other)):
+                for kind, term in enumerate(terms(other)):
                     target[kind, rows_of(other), :] = term.astype(bf16)
             if turn:
                 part_copy(turn - 1).start()
@@ -1164,7 +1171,7 @@
     parts, _, part_width = up_bias.shape
     tiles = tokens // tile
     per_sequence = tiles // 2
-    per_part = tiles + 1
+    per_part = tiles // PART_TILES + 1
     back_from = tiles + parts * per_part - 1
     half = depth // groups // 2
 
@@ -1287,6 +1294,60 @@
     )(mixture, rows, cotangent, valid, mods, up_bias, down_bias, out_blocks, own_weight, other_weight, across)
 
 
+class Relay:
+    def __init__(self, own, out, arrived, sent, got, fsdp, groups):
+        self.own, self.out, self.arrived, self.sent, self.got = own, out, arrived, sent, got
+        self.fsdp, self.groups = fsdp, groups
+
+    def copy(self, side, target):
+        return copy_to(
+            self.out.at[side, target],
+            self.arrived.at[side, target],
+            self.sent.at[side, target],
+            self.got.at[side, target],
+            fsdp=self.fsdp - 1 if side else self.fsdp + 1,
+        )
+
+    def begin(self, target):
+        for side, end in ((0, 0), (1, self.groups - 1)):
+            if target != end:
+
+                @pl.when(self.fsdp == end)
+                def _():
+                    self.out[side, target] = self.own[target]
+                    self.copy(side, target).start()
+
+    def turn(self, number):
+        last = self.groups - 1
+        for side in range(2):
+            behind = last - self.fsdp if side else self.fsdp
+
+            @pl.when((behind >= 1) & (behind <= number))
+            def _():
+                target = self.fsdp + (number - last if side else last - number)
+                self.copy(side, target).wait_recv()
+                if number < last:
+                    total = self.own[target].astype(f32) + self.arrived[side, target].astype(f32)
+                    self.out[side, target] = total.astype(bf16)
+                    self.copy(side, target).start()
+
+    def total(self, sum_ref):
+        sum_ref[...] = self.own[self.fsdp].astype(f32)
+        for side, end in ((0, 0), (1, self.groups - 1)):
+
+            @pl.when(self.fsdp != end)
+            def _():
+                sum_ref[...] += self.arrived[side, self.fsdp].astype(f32)
+
+    def finish(self):
+        for target in range(self.groups):
+            for side, sends in ((0, self.fsdp < target), (1, self.fsdp > target)):
+
+                @pl.when(sends)
+                def _():
+                    self.copy(side, target).wait_send()
+
+
 def entry_back_kernel(
     grad_query_ref,
     grad_key_ref,
@@ -1306,8 +1367,8 @@
     result_in_ref,
     out_ref,
     grad_weight_ref,
-    all_sums_ref,
-    all_small_ref,
+    lines_ref,
+    vectors_ref,
     pieces_ref,
     grad_out_sum_ref,
     block_ref,
@@ -1316,9 +1377,14 @@
     down_own,
     down_in,
     slices,
+    slices_out,
     slices_in,
+    slice_sum,
     context_slice,
     context_in,
+    all_sums_ref,
+    all_small_ref,
+    small_part,
     small_in,
     small_sum,
     small_groups,
@@ -1352,7 +1418,9 @@
     chip,
     chip_in,
     piece,
+    piece_out,
     piece_in,
+    piece_sum,
     block_piece,
     block_in,
     rank_sums,
@@ -1389,22 +1457,6 @@
     depth = hat_ref.shape[0]
     slice_rows = depth // ranks
     weight_rows = depth // groups
-    everyone = groups * 2
-
-    def group_member(away):
-        other = lax.rem(place + away, everyone)
-        return {"fsdp": other // 2, "context": lax.rem(other, 2)}
-
-    def group_away(number):
-        return {"fsdp": lax.rem(fsdp + number // 2, groups), "context": number % 2}
-
-    plane = context * ranks + tensor
-    in_plane = 2 * ranks
-
-    def plane_member(away):
-        other = lax.rem(plane + away, in_plane)
-        return {"context": other // ranks, "tensor": lax.rem(other, ranks)}
-
     def up_copy(other):
         return copy_to(
             up_ref.at[1, other], up_in.at[other], sent_up.at[other], got_up.at[other], context=1 - context
@@ -1421,26 +1473,18 @@
             pltpu.make_async_copy(down_ref.at[1], down_own, loaded.at[1]),
         ]
 
-    def slice_copy(away):
-        other = lax.rem(fsdp + away, groups)
-        return copy_to(
-            slices.at[other],
-            slices_in.at[away - 1],
-            sent_slice.at[away - 1],
-            got_slice.at[away - 1],
-            fsdp=other,
-        )
+    far_first = [groups - 1, 0] + list(range(groups - 2, 0, -1))
+    slice_relay = Relay(slices, slices_out, slices_in, sent_slice, got_slice, fsdp, groups)
+    piece_relay = Relay(piece, piece_out, piece_in, sent_piece, got_piece, fsdp, groups)
 
     def context_copy():
         return copy_to(context_slice, context_in, sent_context, got_context, context=1 - context)
 
-    def small_copy(away):
+    rounds = [{"tensor": sibling}, {"tensor": across}, {"context": 1 - context}]
+
+    def small_copy(number):
         return copy_to(
-            small_ref,
-            small_in.at[away - 1],
-            sent_small.at[away - 1],
-            got_small.at[away - 1],
-            **plane_member(away),
+            small_part.at[number], small_in.at[number], sent_small.at[number], got_small.at[number], **rounds[number]
         )
 
     def sum_copy(away):
@@ -1495,26 +1539,12 @@
             chip.at[tile], chip_in.at[tile], sent_chip.at[tile], got_chip.at[tile], context=1 - context
         )
 
-    def piece_copy(away):
-        other = lax.rem(fsdp + away, groups)
-        return copy_to(
-            piece.at[other],
-            piece_in.at[away - 1],
-            sent_piece.at[away - 1],
-            got_piece.at[away - 1],
-            fsdp=other,
-        )
-
     def block_copy():
         return copy_to(block_piece, block_in, sent_block, got_block, context=1 - context)
 
-    def rank_copy(away):
+    def rank_copy(number):
         return copy_to(
-            rank_sums,
-            rank_in.at[away - 1],
-            sent_rank.at[away - 1],
-            got_rank.at[away - 1],
-            tensor=lax.rem(tensor + away, ranks),
+            rank_sums.at[number], rank_in.at[number], sent_rank.at[number], got_rank.at[number], **rounds[number]
         )
 
     def group_copy(away):
@@ -1523,22 +1553,20 @@
             group_in.at[away - 1],
             sent_group.at[away - 1],
             got_group.at[away - 1],
-            **group_member(away),
+            fsdp=lax.rem(fsdp + away, groups),
         )
 
     @pl.when(step == 0)
     def _():
         greet(
-            [plane_member(away) for away in range(1, in_plane)]
-            + [group_away(away) for away in range(2, everyone)]
-        )
-        for away in range(1, groups + 1):
-            other = lax.rem(fsdp + away, groups)
+            rounds + [{"fsdp": lax.rem(fsdp + away, groups)} for away in range(1, groups)]
+        )
+        for other in far_first:
             up_copy(other).start()
             down_copy(other).start()
         out_copy().start()
-        for away in range(1, in_plane):
-            small_copy(away).start()
+        small_part[0] = small_ref[...]
+        small_copy(0).start()
         for one in result_loads() + loads():
             one.start()
         weight_total[...] = jnp.zeros_like(weight_total)
@@ -1582,8 +1610,8 @@
     def _():
         for other in range(groups):
             piece[other] = weight_total[other * weight_rows : (other + 1) * weight_rows].astype(bf16)
-        for away in range(1, groups):
-            piece_copy(away).start()
+        for target in far_first:
+            piece_relay.begin(target)
 
     @pl.when((step >= 1) & (step < tiles + 1))
     def _():
@@ -1592,9 +1620,9 @@
         pair[tile] = (part[tile, core].astype(f32) + part_in[tile].astype(f32)).astype(bf16)
         pair_copy(tile).start()
 
-    @pl.when((step >= 3) & (step < tiles + 3))
-    def _():
-        tile = step - 3
+    @pl.when((step >= 5) & (step < tiles + 5))
+    def _():
+        tile = step - 5
         pair_copy(tile).wait_recv()
         total = (pair[tile, chip_x].astype(f32) + pair_in[tile].astype(f32)).astype(bf16)
 
@@ -1607,54 +1635,64 @@
         def _():
             out_ref[context, tile - half] = total
 
-    @pl.when((step >= tiles - 1) & (step < tiles - 1 + half))
-    def _():
-        tile = step - tiles + 1
+    @pl.when((step >= tiles + 1) & (step < tiles + 1 + half))
+    def _():
+        tile = step - tiles - 1
         chip_copy(tile).wait_recv()
         out_ref[1 - context, tile] = chip_in[tile]
 
-    @pl.when(step == 4)
-    def _():
-        for away in range(1, in_plane):
-            small_copy(away).wait_recv()
-        small_sum[...] = ordered_sum(small_ref[...], [small_in[k] for k in range(in_plane - 1)], plane)
-        for away in range(1, groups):
-            sum_copy(away).start()
-
-    for away in range(1, groups + 1):
-
-        @pl.when(step == 1 + away)
+    for number in range(3):
+
+        @pl.when(step == (2, 5, 7)[number])
         def _():
-            if away == 1:
+            small_copy(number).wait_recv()
+            total = small_part[number] + small_in[number]
+            if number < 2:
+                small_part[number + 1] = total
+                small_copy(number + 1).start()
+            else:
+                small_sum[...] = total
+                for away in range(1, groups):
+                    sum_copy(away).start()
+
+    for number, other in enumerate(far_first):
+
+        @pl.when(step == 1 + number)
+        def _():
+            if number == 0:
                 for one in loads():
                     one.wait()
-            other = lax.rem(fsdp + away, groups)
             up_copy(other).wait_recv()
             down_copy(other).wait_recv()
             slices[other, 0] = (up_own[other].astype(f32) + up_in[other].astype(f32)).astype(bf16)
             slices[other, 1] = (down_own[other].astype(f32) + down_in[other].astype(f32)).astype(bf16)
-            if away < groups:
-                slice_copy(away).start()
+            slice_relay.begin(other)
+
+    for number in range(1, groups):
+
+        @pl.when(step == tiles - 2 * (groups - 1 - number))
+        def _():
+            slice_relay.turn(number)
 
     @pl.when(step == tiles)
     def _():
-        total = slices[fsdp].astype(f32)
-        for away in range(1, groups):
-            slice_copy(away).wait_recv()
-            total = total + slices_in[away - 1].astype(f32)
-        context_slice[...] = total.astype(bf16)
+        slice_relay.total(slice_sum)
+        context_slice[...] = slice_sum[...].astype(bf16)
         context_copy().start()
 
+    for number in range(1, groups):
+
+        @pl.when(step == tiles + number - 1)
+        def _():
+            piece_relay.turn(number)
+
     @pl.when(step == tiles + 2)
     def _():
-        total = piece[fsdp].astype(f32)
-        for away in range(1, groups):
-            piece_copy(away).wait_recv()
-            total = total + piece_in[away - 1].astype(f32)
-        block_piece[...] = total.astype(bf16)
+        piece_relay.total(piece_sum)
+        block_piece[...] = piece_sum[...].astype(bf16)
         block_copy().start()
 
-    @pl.when(step == tiles + 2)
+    @pl.when(step == tiles + 4)
     def _():
         block_copy().wait_recv()
         grad_weight_ref[...] = block_piece[...].astype(f32) + block_in[...].astype(f32)
@@ -1662,27 +1700,36 @@
     @pl.when(step == tiles - 1)
     def _():
         rows = [jnp.sum(sums[kind].T, axis=0, keepdims=True) for kind in range(2)]
-        rank_sums[...] = jnp.concatenate(rows + [jnp.zeros((6, depth), f32)], axis=0)
-        for away in range(1, ranks):
-            rank_copy(away).start()
+        rank_sums[0] = jnp.concatenate(rows + [jnp.zeros((6, depth), f32)], axis=0)
+        rank_copy(0).start()
 
     @pl.when(step == tiles)
     def _():
-        for away in range(1, ranks):
-            rank_copy(away).wait_recv()
-        pairs = [rank_sums[...] + rank_in[1], rank_in[0] + rank_in[2]]
-        group_sums[...] = pairs[0] + pairs[1]
-        for away in range(1, everyone):
+        rank_copy(0).wait_recv()
+        rank_sums[1] = rank_sums[0] + rank_in[0]
+        rank_copy(1).start()
+
+    @pl.when(step == tiles + 3)
+    def _():
+        rank_copy(1).wait_recv()
+        rank_sums[2] = rank_sums[1] + rank_in[1]
+        rank_copy(2).start()
+
+    @pl.when(step == tiles + 4)
+    def _():
+        rank_copy(2).wait_recv()
+        group_sums[context] = rank_sums[2]
+        group_sums[1 - context] = rank_in[2]
+        for away in range(1, groups):
             group_copy(away).start()
 
-    @pl.when(step == tiles + 2)
+    @pl.when(step == tiles + 4)
     def _():
         all_small_ref[fsdp] = small_sum[...]
         for away in range(1, groups):
             sum_copy(away).wait_recv()
             all_small_ref[lax.rem(fsdp + groups - away, groups)] = small_groups[away - 1]
             sum_copy(away).wait_send()
-            slice_copy(away).wait_send()
         context_copy().wait()
         pieces_ref[context] = context_slice[...]
         pieces_ref[1 - context] = context_in[...]
@@ -1691,38 +1738,40 @@
         for other in range(groups):
             up_copy(other).wait_send()
             down_copy(other).wait_send()
-        for away in range(1, in_plane):
-            small_copy(away).wait_send()
+        for number in range(3):
+            small_copy(number).wait_send()
+            rank_copy(number).wait_send()
         for one in result_copies() + result_moves():
             one.wait()
-        all_sums_ref[place] = group_sums[...]
-        for away in range(1, everyone):
+        for number in range(2):
+            all_sums_ref[2 * fsdp + number] = group_sums[number]
+        for away in range(1, groups):
             group_copy(away).wait_recv()
-            all_sums_ref[lax.rem(place + everyone - away, everyone)] = group_in[away - 1]
+            for number in range(2):
+                source = lax.rem(fsdp + groups - away, groups)
+                all_sums_ref[2 * source + number] = group_in[away - 1, number]
+            group_copy(away).wait_send()
+        for source in range(2 * groups):
+            line = slice(source, source + 1)
+            for kind in range(2):
+                lines_ref[kind, line] = all_sums_ref[source, kind : kind + 1]
+            first = source % 2 * 5
+            for kind in range(4):
+                lines_ref[2 + kind, line] = all_small_ref[source // 2, first + kind : first + kind + 1]
+            last = 10 + ranks + source % 2
+            lines_ref[6, line] = all_small_ref[source // 2, last : last + 1]
+        vectors_ref[...] = jnp.zeros_like(vectors_ref)
+        for source in range(groups):
+            vectors_ref[0:ranks] += all_small_ref[source, 10 : 10 + ranks]
+            vectors_ref[ranks : ranks + 1] += all_small_ref[source, 4:5] + all_small_ref[source, 9:10]
         for tile in range(tiles):
             part_copy(tile).wait_send()
             pair_copy(tile).wait_send()
         for tile in range(half):
             chip_copy(tile).wait_send()
-        for away in range(1, groups):
-            piece_copy(away).wait_send()
+        slice_relay.finish()
+        piece_relay.finish()
         block_copy().wait_send()
-        for away in range(1, ranks):
-            rank_copy(away).wait_send()
-        for away in range(1, everyone):
-            group_copy(away).wait_send()
-
-
-def ordered_sum(own, others, place):
-    count = len(others) + 1
-    total = 0.0
-    for source in range(count):
-        away = lax.rem(place - source + count, count)
-        term = own
-        for k, other in enumerate(others):
-            term = jnp.where(away == k + 1, other, term)
-        total = total + term
-    return total
 
 
 def entry_back_call(
@@ -1764,7 +1813,7 @@
     piece = up.shape[1:]
     return pl.pallas_call(
         partial(entry_back_kernel, tiles=tiles, groups=groups),
-        grid=(tiles + 3,),
+        grid=(tiles + 5,),
         in_specs=[
             pl.BlockSpec((group, tile), lanes),
             pl.BlockSpec((group, tile), lanes),
@@ -1786,8 +1835,8 @@
         out_specs=[
             pl.BlockSpec((2, half, rows, tile), whole4),
             pl.BlockSpec((weight_rows, 3 * group), whole),
-            pl.BlockSpec((2 * groups, 8, depth), whole3),
-            pl.BlockSpec((groups, *small.shape), whole3),
+            pl.BlockSpec((7, 2 * groups, depth), whole3),
+            pl.BlockSpec((8, depth), whole),
             pl.BlockSpec((2, 2, *piece[1:]), whole4),
             pl.BlockSpec(grad_out.shape, whole),
             hbm,
@@ -1795,8 +1844,8 @@
         out_shape=[
             jax.ShapeDtypeStruct((2, half, rows, tile), bf16),
             jax.ShapeDtypeStruct((weight_rows, 3 * group), f32),
-            jax.ShapeDtypeStruct((2 * groups, 8, depth), f32),
-            jax.ShapeDtypeStruct((groups, *small.shape), f32),
+            jax.ShapeDtypeStruct((7, 2 * groups, depth), f32),
+            jax.ShapeDtypeStruct((8, depth), f32),
             jax.ShapeDtypeStruct((2, 2, *piece[1:]), bf16),
             jax.ShapeDtypeStruct(grad_out.shape, f32),
             jax.ShapeDtypeStruct((2, 4 * result.shape[1], depth), bf16),
@@ -1804,19 +1853,22 @@
         scratch_shapes=[
             *[pltpu.VMEM(piece, bf16)] * 4,
             pltpu.VMEM((groups, 2, *piece[1:]), bf16),
-            pltpu.VMEM((groups - 1, 2, *piece[1:]), bf16),
+            *[pltpu.VMEM((2, groups, 2, *piece[1:]), bf16)] * 2,
+            pltpu.VMEM((2, *piece[1:]), f32),
             pltpu.VMEM((2, *piece[1:]), bf16),
             pltpu.VMEM((2, *piece[1:]), bf16),
-            pltpu.VMEM((7, *small.shape), f32),
+            pltpu.VMEM((2 * groups, 8, depth), f32),
+            pltpu.VMEM((groups, *small.shape), f32),
+            *[pltpu.VMEM((3, *small.shape), f32)] * 2,
             pltpu.VMEM(small.shape, f32),
             pltpu.VMEM((groups - 1, *small.shape), f32),
             pltpu.VMEM(grad_out.shape, bf16),
             pltpu.SemaphoreType.DMA((2,)),
             *dma(groups),
             *dma(groups),
-            *dma(groups - 1),
+            *dma(2, groups),
             *[pltpu.SemaphoreType.DMA] * 2,
-            *dma(7),
+            *dma(3),
             *dma(groups - 1),
             *[pltpu.SemaphoreType.DMA] * 2,
             *dma(4),
@@ -1832,20 +1884,20 @@
             pltpu.VMEM((half, rows, tile), bf16),
             pltpu.VMEM((half, rows, tile), bf16),
             pltpu.VMEM((groups, weight_rows, 3 * group), bf16),
-            pltpu.VMEM((groups - 1, weight_rows, 3 * group), bf16),
+            *[pltpu.VMEM((2, groups, weight_rows, 3 * group), bf16)] * 2,
+            pltpu.VMEM((weight_rows, 3 * group), f32),
             pltpu.VMEM((weight_rows, 3 * group), bf16),
             pltpu.VMEM((weight_rows, 3 * group), bf16),
-            pltpu.VMEM((8, depth), f32),
-            pltpu.VMEM((3, 8, depth), f32),
-            pltpu.VMEM((8, depth), f32),
-            pltpu.VMEM((2 * groups - 1, 8, depth), f32),
+            *[pltpu.VMEM((3, 8, depth), f32)] * 2,
+            pltpu.VMEM((2, 8, depth), f32),
+            pltpu.VMEM((groups - 1, 2, 8, depth), f32),
             *dma(tiles),
             *dma(tiles),
             *dma(half),
-            *dma(groups - 1),
+            *dma(2, groups),
             *[pltpu.SemaphoreType.DMA] * 2,
             *dma(3),
-            *dma(2 * groups - 1),
+            *dma(groups - 1),
         ],
         compiler_params=pltpu.CompilerParams(
             vmem_limit_bytes=VMEM, collective_id=3, has_side_effects=True
@@ -2026,7 +2078,7 @@
     (grad_query, up_sum, down_sum, result_in, middle_in, grad_out) = lax.optimization_barrier(
         (grad_query, up_sum, down_sum, result_in, middle_in, grad_out)
     )
-    part, grad_qkv, entry_sums, small, pieces, grad_out, block_out = entry_back_call(
+    part, grad_qkv, lines, vectors, pieces, grad_out, block_out = entry_back_call(
         grad_query,
         grad_key,
         grad_value,
@@ -2051,26 +2103,26 @@
     grad_w_up = pieces[0]
     grad_w_down = pieces[1].T
     grad_w_out = grad_out
-    small_sums = small[:, : 5 * sequences].reshape(fsdp * sequences, 5, depth)
-    embedded = small[:, small_rows : small_rows + sequences].reshape(fsdp * sequences, depth)
+    embedded = lines[6]
     choose = (embedded[:, cond].astype(jnp.int32)[:, None] == numbers[None, :]).astype(f32)
     embedding, silu_back = jax.vjp(jax.nn.silu, embedded[:, :cond])
-    modulation = exact_product(embedding, ada_full) + ada_b.astype(f32)
-    grad_b_up = jnp.sum(small[:, 5 * sequences : small_rows], axis=0).reshape(-1)
-    grad_b_down = jnp.sum(small_sums[:, 4], axis=0)
-    grad_gain_two = jnp.sum(small_sums[:, 2] * (1.0 + modulation[:, 4 * depth : 5 * depth]), axis=0)
-    middle_mod = jnp.concatenate(
-        [small_sums[:, 0], small_sums[:, 1], small_sums[:, 2] * gain_second, small_sums[:, 3]], axis=1
-    )
+    scale_columns = [slice(k * depth, (k + 1) * depth) for k in (1, 4)]
+    scales_one, scales_two = (
+        exact_product(embedding, ada_full[:, columns]) + ada_b[columns].astype(f32)
+        for columns in scale_columns
+    )
+    grad_b_up = vectors[:tensor].reshape(-1)
+    grad_b_down = vectors[tensor]
+    grad_gain_one = jnp.sum(lines[1] * (1.0 + scales_one), axis=0)
+    grad_gain_two = jnp.sum(lines[4] * (1.0 + scales_two), axis=0)
     part = part.transpose(0, 1, 3, 2).reshape(sequences, own_rows, depth // tensor)
     grad_tokens = part.astype(f32)
     grad_w_qkv = (
         grad_qkv.reshape(-1, 3, heads, HDIM).transpose(0, 2, 1, 3).reshape(-1, 3 * group)
     )
     grad_mod = jnp.concatenate(
-        [entry_sums[:, 0], entry_sums[:, 1] * gain_first, middle_mod], axis=1
-    )
-    grad_gain_one = jnp.sum(entry_sums[:, 1] * (1.0 + modulation[:, depth : 2 * depth]), axis=0)
+        [lines[0], lines[1] * gain_first, lines[2], lines[3], lines[4] * gain_second, lines[5]], axis=1
+    )
     grad_ada_b = jnp.sum(grad_mod, axis=0)
     grad_ada_w = exact_transposed(embedding, grad_mod)
     grad_before = silu_back(exact_against(grad_mod, ada_full))[0]

time: 446 us -> 430 us (0.964); the launches traced: 442 us -> 431 us
  waiting for transfers between devices: 20.8 us -> 2.35 us
  Pallas kernels: 352 us -> 361 us
    pallas_call x1, Pallas kernels: 103 us -> 74.1 us  [entry_back_call(): pl.pallas_call(partial(entry_back_kernel, tiles=tiles, groups=groups), gr...]
    pallas_call x1, Pallas kernels: 103 us -> 122 us  [middle_call(): pl.pallas_call(partial(middle_kernel, tile=tile, tiles=tiles, parts=parts...]
    reduce_scatter x1, waiting for transfers between devices: 13.1 us -> 0.01 us  [by_sequence(): lax.psum_scatter(grad_out, both, scatter_dimension=0, tiled=True)[0]]
    pallas_call x1, Pallas kernels: 63.4 us -> 75.2 us  [attend_back_call(): pl.pallas_call(partial(attend_back_kernel, block=block), grid_spec=pltpu....]
    pallas_call x1, Pallas kernels: 26.8 us -> 33.4 us  [attend_call(): pl.pallas_call(partial(attend_kernel, block=block), grid_spec=pltpu.Prefe...]
    all_gather x1, waiting for transfers between devices: 7.65 us -> 2.3 us  [by_sequence(): out_blocks = lax.all_gather(w_out, both, axis=0, tiled=False)]
    unnamed x58 -> x60, local copies, waits for them, and re-layouts: 10.4 us -> 12.2 us
  transfers between devices with their start and end apart: 8 -> 8, of which waited for: 2 -> 1; matrix products, arithmetic and copies ran while one was open for 3% -> 2% of each run, Pallas kernels for 20% -> 25%
where the time goes in v5:
time: 430 us; the launch traced here: 431 us
  Pallas kernels  361 us (84%)
  local copies, waits for them, and re-layouts  23.2 us (5%)
  between operations  14.9 us (3%)
  other arithmetic  13.9 us (3%)
  matrix products  9.32 us (2%)
  starting transfers between devices  7.08 us (2%)
    pallas_call x1, Pallas kernels, middle_call(): pl.pallas_call(partial(middle_kernel, tile=tile, tiles=tiles, parts=parts...  122 us
    pallas_call x1, Pallas kernels, attend_back_call(): pl.pallas_call(partial(attend_back_kernel, block=block), grid_spec=pltpu....  75.2 us
    pallas_call x1, Pallas kernels, entry_back_call(): pl.pallas_call(partial(entry_back_kernel, tiles=tiles, groups=groups), gr...  74.1 us
    pallas_call x1, Pallas kernels, entry_call(): pl.pallas_call(partial(entry_kernel, heads=heads, groups=groups), grid=(2...  55.6 us
    pallas_call x1, Pallas kernels, attend_call(): pl.pallas_call(partial(attend_kernel, block=block), grid_spec=pltpu.Prefe...  33.4 us
    unnamed x60, local copies, waits for them, and re-layouts  12.2 us
  transfers between devices with their start and end apart: 8, of which 1 were waited for; matrix products, arithmetic and copies ran while one was open for 2% of the time, Pallas kernels for 25%

profile of v5, /device:TPU:0, one launch (start us, length us, event | category | flops | bytes accessed | tf_op | source)
XLA Modules:
  0.0 431.4 jit_solution(14671736675440593403)
XLA Ops:
  7.3 1.2 copy.44
  8.6 0.9 copy.46.shard_ref
  9.7 0.6 convolution_add_fusion
  10.4 0.9 broadcast_in_dim.79.gain_ref
  11.3 1.0 copy.48.shift_ref
  12.6 2.8 multiply_sine_fusion
  15.4 0.7 bitcast_select_fusion.own_forward_ref
  16.2 55.6 %entry.1 = (bf16[3,128,4096]{2,1,0:T(8,128)(2,1)}, bf16[3,4096,128]{2,1,0:T(8,128)(2,1)}, bf16[3,128,4096]{2,1,0:T(8,128)(2,1)}, bf16[3,128,4096]{2,1,0:T(8,128)...) custom-call(bf16[2,2048,768]{2,1,0:T(8,128)(2,1)} %rows_ref.3, ...), custom_call_target="tpu_custom_call" | custom-call | flops 3623878656 | bytes 27377664 | tf_op jit(solution)/shard_map/entry/pallas_call | solution.py:429
  71.8 2.8 collective-permute-start
  74.9 0.6 pad_add_fusion.1.range_ref
  75.5 33.4 %attend.1 = (bf16[8,192,512]{2,1,0:T(8,128)(2,1)}, bf16[3,128,4096]{2,1,0:T(8,128)(2,1)}) custom-call(s32[2,8]{1,0:T(2,128)} %pad_add_fusion.1.range_ref, bf16[3,128,4096]{2,1,0:T(8,128)(2,1)} %get-tuple-element.50.query_ref, bf16[3,4096,128]{2,1,0:T(8,128)(2,1)} %get-tuple-element.51.key_ref, bf16[3,128,4096]{2,1,0:T(8,128)(2,1)} %get-tuple-element.52.value_ref, ...), custom_call_target="tpu_custom_call" | custom-call | flops 25769803776 | bytes 9437184 | tf_op jit(solution)/shard_map/attend/pallas_call | solution.py:563
  108.9 1.0 copy.60
  110.0 0.6 reshape.119
  110.6 0.6 reshape.121.down_bias_ref
  111.3 0.6 pad_add_fusion.range_ref
  111.9 0.7 maximum_maximum_fusion.mod_ref
  112.6 2.3 all-gather.3.cloned.1.call-done
  115.0 122.5 %middle.1 = (bf16[1024,768]{1,0:T(8,128)(2,1)}, bf16[8,192,512]{2,1,0:T(8,128)(2,1)}, bf16[2,768,512]{2,1,0:T(8,128)(2,1)}, bf16[16,192,192]{2,1,0:T(8,128)(2,1)...) custom-call(bf16[8,192,512]{2,1,0:T(8,128)(2,1)} %get-tuple-element., ...), custom_call_target="tpu_custom_call" | custom-call | flops 47110422528 | bytes 18874368 | tf_op jit(solution)/shard_map/middle/pallas_call | solution.py:1209
  237.4 0.7 collective-permute-start.2
  238.2 0.5 collective-permute-start.3
  238.6 1.4 collective-permute-start.4
  240.1 1.2 dynamic-slice_bitcast_fusion
  241.2 1.6 collective-permute-start.5
  242.9 75.2 %attend_back.1 = (bf16[192,4096]{1,0:T(8,128)(2,1)}, bf16[192,4096]{1,0:T(8,128)(2,1)}, bf16[192,4096]{1,0:T(8,128)(2,1)}) custom-call(s32[2,8]{1,0:T(2,128)} %pad_add_fusion.range_ref, bf16[3,128,4096]{2,1,0:T(8,128)(2,1)} %get-tuple-element.54.query_ref, bf16[3,128,4096]{2,1,0:T(8,128)(2,1)} %get-tuple-element.55.key_ref, ...), custom_call_target="tpu_custom_call" | custom-call | flops 64424509440 | bytes 9437184 | tf_op jit(solution)/shard_map/attend_back/pallas_call | solution.py:678
  318.1 0.6 select_maximum_fusion.small_ref
  318.7 2.7 add_convert_fusion.1.up_ref
  321.4 1.3 add_convert_fusion.down_ref
  322.8 74.1 %entry_back.1 = (bf16[2,4,192,512]{3,2,1,0:T(8,128)(2,1)}, f32[192,576]{1,0:T(8,128)}, f32[7,8,768]{2,1,0:T(8,128)}, f32[8,768]{1,0:T(8,128)}, bf16[2,2,96,768]{...) custom-call(bf16[192,4096]{1,0:T(8,128)(2,1)} %get-tuple-element.67.grad_query_ref, ...), custom_call_target="tpu_custom_call" | custom-call | flops 7247757312 | bytes 14155776 | tf_op jit(solution)/shard_map/entry_back/pallas_call | solution.py:1814
  396.9 0.7 bitcast_dynamic-update-slice_fusion.3
  397.6 0.7 slice_bitcast_fusion
  398.3 0.7 fusion.9
  399.1 0.7 bitcast_dynamic-update-slice_fusion.2
  399.8 0.7 bitcast_dynamic-update-slice_fusion.1
  400.6 0.7 fusion.8
  401.3 0.7 bitcast_dynamic-update-slice_fusion
  402.0 1.0 fusion.41
  403.2 3.5 fusion.37
  406.6 0.6 reduce_sum.51
  407.3 0.6 slice_reduce_fusion
  408.3 2.0 copy.58
  410.3 1.5 fusion.4
  412.1 1.0 copy.56
  413.1 1.5 fusion.5
  414.8 1.1 fusion.40
  415.9 0.6 reshape.116
  416.5 1.0 fusion.10
  417.5 5.9 %copy.70 = bf16[2,2048,768]{2,1,0:T(8,128)(2,1)} copy(bf16[2,2048,768]{2,1,0:T(8,128)(2,1)} %get-tuple-element.146) | data formatting | bytes 12582912
  423.4 0.7 copy.71
  (98 shorter events, 2.3 us)
Async XLA Ops:
  7.2 2.3 copy-start
  7.2 2.3 copy-start.14
  7.2 2.3 copy-start.24
  7.2 2.5 copy-start.2
  7.2 107.7 %all-gather.3.cloned.1.call-start = ((), (), s32[]{:S(2)}) async-start(), calls=%async_computation.2 | async-start | bytes 1671168 | tf_op jit(solution)/shard_map/all_gather | solution.py:1964
  7.3 3.0 copy-start.15
  7.3 3.1 copy-start.18
  9.7 5.8 %copy-start.9 = (bf16[192,768]{1,0:T(8,128)(2,1)S(1)}, bf16[192,768]{1,0:T(8,128)(2,1)}, u32[]{:S(2)}) copy-start(bf16[192,768]{1,0:T(8,128)(2,1)} %param.26) | copy-start | bytes 884740
  9.7 5.8 %copy-start.10 = (bf16[768,192]{0,1:T(8,128)(2,1)S(1)}, bf16[768,192]{0,1:T(8,128)(2,1)}, u32[]{:S(2)}) copy-start(bf16[768,192]{0,1:T(8,128)(2,1)} %param.28) | copy-start | bytes 884740
  10.3 5.9 %copy-start.11 = (s32[1,4096]{1,0:T(1,128)}, s32[1,4096]{1,0:T(1,128)S(1)}, u32[]{:S(2)}) copy-start(s32[1,4096]{1,0:T(1,128)S(1)} %constant_dynamic-slice_fusion.segment_ref) | copy-start | bytes 49156
  71.8 40.8 %collective-permute-start = (bf16[768,768]{1,0:T(8,128)(2,1)}, bf16[768,768]{1,0:T(8,128)(2,1)S(1)}, u32[]{:S(2)}, u32[]{:S(2)}) collective-permute-start(bf16[768,768]{1,0:T(8,128)(2,1)} %get-tuple-element.57.own_ref), channel_id=1, source_target_pairs={{0,4},{4,0},{1,5},{5,1},{2,6},{6,2},{3,7},{7,3},{8,12},{12,8},{9,1... | collective-permute-start | bytes 3538952 | tf_op jit(solution)/shard_map/ppermute | solution.py:2020
  74.6 38.0 %collective-permute-start.1 = (bf16[768,768]{1,0:T(8,128)(2,1)}, bf16[768,768]{1,0:T(8,128)(2,1)S(1)}, u32[]{:S(2)}, u32[]{:S(2)}) collective-permute-start(bf16[768,768]{1,0:T(8,128)(2,1)} %get-tuple-element.57.own_ref), channel_id=1, source_target_pairs={{0,2},{1,3},{2,0},{3,1},{4,6},{5,7},{6,4},{7,5},{8,10},{9,11},{10,... | collective-permute-start | bytes 3538952 | tf_op jit(solution)/shard_map/ppermute | solution.py:2019
  74.6 248.1 %reduce-scatter.2.cloned.1.call-start = ((), (), s32[]{:S(2)}) async-start(), calls=%async_computation.1 | async-start | bytes 1671168 | tf_op jit(solution)/shard_map/reduce_scatter | solution.py:2073
  75.5 34.5 %copy-start.20 = (bf16[768]{0:T(1024)(128)(2,1)S(1)}, bf16[768]{0:T(1024)(128)(2,1)}, u32[]{:S(2)}) copy-start(bf16[768]{0:T(1024)(128)(2,1)} %param.25) | copy-start | bytes 4612
  75.5 34.5 %copy-start.19 = (bf16[3072]{0:T(1024)(128)(2,1)S(1)}, bf16[3072]{0:T(1024)(128)(2,1)}, u32[]{:S(2)}) copy-start(bf16[3072]{0:T(1024)(128)(2,1)} %param.27) | copy-start | bytes 18436
  75.5 35.1 %copy-start.21 = (bf16[768]{0:T(1024)(128)(2,1)S(1)}, bf16[768]{0:T(1024)(128)(2,1)}, u32[]{:S(2)}) copy-start(bf16[768]{0:T(1024)(128)(2,1)} %param.29) | copy-start | bytes 4612
  112.6 2.3 copy-start.22
  112.6 2.3 copy-start.23
  237.4 81.3 %collective-permute-start.2 = (bf16[2,4,96,768]{3,2,1,0:T(8,128)(2,1)}, bf16[2,4,96,768]{3,2,1,0:T(8,128)(2,1)}, u32[]{:S(2)}, u32[]{:S(2)}) collective-permute-start(bf16[2,4,96,768]{3,2,1,0:T(8,128)(2,1)} %get-tuple-element.61), channel_id=1, source_target_pairs={{0,2},{1,3},{2,0},{3,1},{4,6},{5,7},{6,4},{7,5},{8,10},{9,11},{10,... | collective-permute-start | bytes 3538952 | tf_op jit(solution)/shard_map/ppermute | solution.py:2071
  238.2 83.3 %collective-permute-start.3 = (bf16[2,4,96,768]{3,2,1,0:T(8,128)(2,1)}, bf16[2,4,96,768]{3,2,1,0:T(8,128)(2,1)S(1)}, u32[]{:S(2)}, u32[]{:S(2)}) collective-permute-start(bf16[2,4,96,768]{3,2,1,0:T(8,128)(2,1)} %get-tuple-element.63), channel_id=1, source_target_pairs={{0,4},{4,0},{1,5},{5,1},{2,6},{6,2},{3,7},{7,3},{8,12},{12,8},{9,1... | collective-permute-start | bytes 3538952 | tf_op jit(solution)/shard_map/ppermute | solution.py:2072
  238.6 84.1 %collective-permute-start.4 = (bf16[2,512,768]{2,1,0:T(8,128)(2,1)}, bf16[2,512,768]{2,1,0:T(8,128)(2,1)}, u32[]{:S(2)}, u32[]{:S(2)}) collective-permute-start(bf16[2,512,768]{2,1,0:T(8,128)(2,1)} %bitcast.88), channel_id=1, source_target_pairs={{0,2},{1,3},{2,0},{3,1},{4,6},{5,7},{6,4},{7,5},{8,10},{9,11},{10,... | collective-permute-start | bytes 4718600 | tf_op jit(solution)/shard_map/ppermute | solution.py:2053
  241.2 81.5 %collective-permute-start.5 = (bf16[768,512]{1,0:T(8,128)(2,1)S(1)}, bf16[768,512]{1,0:T(8,128)(2,1)}, u32[]{:S(2)}, u32[]{:S(2)}) collective-permute-start(bf16[768,512]{1,0:T(8,128)(2,1)S(1)} %dynamic-slice_bitcast_fusion), channel_id=1, source_target_pairs={{0,4},{4,0},{1,5},{5,1},{2,6},{6,2},{3,7},{7,3},{8,12},{12,8},{9,1... | collective-permute-start | bytes 2359304 | tf_op jit(solution)/shard_map/ppermute | solution.py:2054
  242.8 75.2 %copy-start.16 = (f32[4,1,768]{2,1,0:T(1,128)S(1)}, f32[4,1,768]{2,1,0:T(1,128)}, u32[]{:S(2)}) copy-start(f32[4,1,768]{2,1,0:T(1,128)} %get-tuple-element.75) | copy-start | bytes 36868
  242.8 75.2 %copy-start.13 = (f32[2,8,768]{2,1,0:T(8,128)S(1)}, f32[2,8,768]{2,1,0:T(8,128)}, u32[]{:S(2)}) copy-start(f32[2,8,768]{2,1,0:T(8,128)} %get-tuple-element.74) | copy-start | bytes 147460
  242.8 75.9 %copy-start.6 = (bf16[2,4,96,768]{3,2,1,0:T(8,128)(2,1)S(1)}, bf16[2,4,96,768]{3,2,1,0:T(8,128)(2,1)}, u32[]{:S(2)}) copy-start(bf16[2,4,96,768]{3,2,1,0:T(8,128)(2,1)} %get-tuple-element.60) | copy-start | bytes 3538948
  318.7 2.7 copy-start.5
  322.8 79.3 %copy-start.3 = (bf16[128,4608]{1,0:T(8,128)(2,1)S(1)}, bf16[128,4608]{1,0:T(8,128)(2,1)}, u32[]{:S(2)}) copy-start(bf16[128,4608]{1,0:T(8,128)(2,1)} %param.20) | copy-start | bytes 3538948
  403.0 4.3 copy-start.17
  403.0 4.9 %copy-start.4 = (bf16[2,4,192,512]{3,2,1,0:T(8,128)(2,1)S(1)}, bf16[2,4,192,512]{3,2,1,0:T(8,128)(2,1)}, u32[]{:S(2)}) copy-start(bf16[2,4,192,512]{3,2,1,0:T(8,128)(2,1)} %get-tuple-element.81) | copy-start | bytes 4718596
  408.3 3.5 copy-start.8
  411.9 2.8 copy-start.7
  417.5 5.9 %copy-start.12 = (f32[192,192]{1,0:T(8,128)S(1)}, f32[192,192]{1,0:T(8,128)}, u32[]{:S(2)}) copy-start(f32[192,192]{1,0:T(8,128)} %get-tuple-element.153) | copy-start | bytes 442372
  417.5 6.6 %copy-start.1 = (bf16[256,128]{1,0:T(8,128)(2,1)S(1)}, bf16[256,128]{1,0:T(8,128)(2,1)}, u32[]{:S(2)}) copy-start(bf16[256,128]{1,0:T(8,128)(2,1)} %param.19) | copy-start | bytes 196612
Sparse Core Ops, SparseCore 0:
  74.8 40.1 all-gather.2
  242.9 61.5 reduce-scatter.1

commit v6 on v5

--- a/solution.py
+++ b/solution.py
@@ -1368,6 +1368,7 @@
     out_ref,
     grad_weight_ref,
     lines_ref,
+    embedded_ref,
     vectors_ref,
     pieces_ref,
     grad_out_sum_ref,
@@ -1753,13 +1754,13 @@
             group_copy(away).wait_send()
         for source in range(2 * groups):
             line = slice(source, source + 1)
-            for kind in range(2):
-                lines_ref[kind, line] = all_sums_ref[source, kind : kind + 1]
             first = source % 2 * 5
-            for kind in range(4):
-                lines_ref[2 + kind, line] = all_small_ref[source // 2, first + kind : first + kind + 1]
+            terms = [all_sums_ref[source, kind : kind + 1] for kind in range(2)]
+            terms += [all_small_ref[source // 2, first + kind : first + kind + 1] for kind in range(4)]
+            for kind, term in enumerate(terms):
+                lines_ref[line, kind * depth : (kind + 1) * depth] = term
             last = 10 + ranks + source % 2
-            lines_ref[6, line] = all_small_ref[source // 2, last : last + 1]
+            embedded_ref[line] = all_small_ref[source // 2, last : last + 1]
         vectors_ref[...] = jnp.zeros_like(vectors_ref)
         for source in range(groups):
             vectors_ref[0:ranks] += all_small_ref[source, 10 : 10 + ranks]
@@ -1835,7 +1836,8 @@
         out_specs=[
             pl.BlockSpec((2, half, rows, tile), whole4),
             pl.BlockSpec((weight_rows, 3 * group), whole),
-            pl.BlockSpec((7, 2 * groups, depth), whole3),
+            pl.BlockSpec((2 * groups, 6 * depth), whole),
+            pl.BlockSpec((2 * groups, depth), whole),
             pl.BlockSpec((8, depth), whole),
             pl.BlockSpec((2, 2, *piece[1:]), whole4),
             pl.BlockSpec(grad_out.shape, whole),
@@ -1844,7 +1846,8 @@
         out_shape=[
             jax.ShapeDtypeStruct((2, half, rows, tile), bf16),
             jax.ShapeDtypeStruct((weight_rows, 3 * group), f32),
-            jax.ShapeDtypeStruct((7, 2 * groups, depth), f32),
+            jax.ShapeDtypeStruct((2 * groups, 6 * depth), f32),
+            jax.ShapeDtypeStruct((2 * groups, depth), f32),
             jax.ShapeDtypeStruct((8, depth), f32),
             jax.ShapeDtypeStruct((2, 2, *piece[1:]), bf16),
             jax.ShapeDtypeStruct(grad_out.shape, f32),
@@ -2078,7 +2081,7 @@
     (grad_query, up_sum, down_sum, result_in, middle_in, grad_out) = lax.optimization_barrier(
         (grad_query, up_sum, down_sum, result_in, middle_in, grad_out)
     )
-    part, grad_qkv, lines, vectors, pieces, grad_out, block_out = entry_back_call(
+    part, grad_qkv, lines, embedded, vectors, pieces, grad_out, block_out = entry_back_call(
         grad_query,
         grad_key,
         grad_value,
@@ -2103,7 +2106,6 @@
     grad_w_up = pieces[0]
     grad_w_down = pieces[1].T
     grad_w_out = grad_out
-    embedded = lines[6]
     choose = (embedded[:, cond].astype(jnp.int32)[:, None] == numbers[None, :]).astype(f32)
     embedding, silu_back = jax.vjp(jax.nn.silu, embedded[:, :cond])
     scale_columns = [slice(k * depth, (k + 1) * depth) for k in (1, 4)]
@@ -2113,16 +2115,15 @@
     )
     grad_b_up = vectors[:tensor].reshape(-1)
     grad_b_down = vectors[tensor]
-    grad_gain_one = jnp.sum(lines[1] * (1.0 + scales_one), axis=0)
-    grad_gain_two = jnp.sum(lines[4] * (1.0 + scales_two), axis=0)
+    grad_gain_one = jnp.sum(lines[:, scale_columns[0]] * (1.0 + scales_one), axis=0)
+    grad_gain_two = jnp.sum(lines[:, scale_columns[1]] * (1.0 + scales_two), axis=0)
     part = part.transpose(0, 1, 3, 2).reshape(sequences, own_rows, depth // tensor)
     grad_tokens = part.astype(f32)
     grad_w_qkv = (
         grad_qkv.reshape(-1, 3, heads, HDIM).transpose(0, 2, 1, 3).reshape(-1, 3 * group)
     )
-    grad_mod = jnp.concatenate(
-        [lines[0], lines[1] * gain_first, lines[2], lines[3], lines[4] * gain_second, lines[5]], axis=1
-    )
+    ones = jnp.ones((depth,), f32)
+    grad_mod = lines * jnp.concatenate([ones, gain_first, ones, ones, gain_second, ones])[None, :]
     grad_ada_b = jnp.sum(grad_mod, axis=0)
     grad_ada_w = exact_transposed(embedding, grad_mod)
     grad_before = silu_back(exact_against(grad_mod, ada_full))[0]

time: 430 us -> 425 us (0.988)
    unnamed x60 -> x63, local copies, waits for them, and re-layouts: 12.2 us -> 10.1 us
  transfers between devices with their start and end apart: 8 -> 8, of which waited for: 1 -> 1; matrix products, arithmetic and copies ran while one was open for 2% -> 2% of each run, Pallas kernels for 25% -> 26%
where the time goes in v6:
time: 425 us
  Pallas kernels  358 us (84%)
  local copies, waits for them, and re-layouts  19.5 us (5%)
  between operations  14.9 us (4%)
  other arithmetic  13 us (3%)
  matrix products  9.8 us (2%)
  starting transfers between devices  6.98 us (2%)
    pallas_call x1, Pallas kernels, middle_call(): pl.pallas_call(partial(middle_kernel, tile=tile, tiles=tiles, parts=parts...  121 us
    pallas_call x1, Pallas kernels, attend_back_call(): pl.pallas_call(partial(attend_back_kernel, block=block), grid_spec=pltpu....  76.1 us
    pallas_call x1, Pallas kernels, entry_back_call(): pl.pallas_call(partial(entry_back_kernel, tiles=tiles, groups=groups), gr...  72 us
    pallas_call x1, Pallas kernels, entry_call(): pl.pallas_call(partial(entry_kernel, heads=heads, groups=groups), grid=(2...  55.7 us
    pallas_call x1, Pallas kernels, attend_call(): pl.pallas_call(partial(attend_kernel, block=block), grid_spec=pltpu.Prefe...  33.2 us
    unnamed x63, local copies, waits for them, and re-layouts  10.1 us
  transfers between devices with their start and end apart: 8, of which 1 were waited for; matrix products, arithmetic and copies ran while one was open for 2% of the time, Pallas kernels for 26%

profile of v6, /device:TPU:0, one launch (start us, length us, event | category | flops | bytes accessed | tf_op | source)
XLA Modules:
  0.0 424.8 jit_solution(15529667617634590861)
XLA Ops:
  7.3 1.2 copy.44
  8.6 0.9 copy.46.shard_ref
  9.5 0.2 fusion.24
  9.7 0.6 convolution_add_fusion
  10.4 0.9 broadcast_in_dim.78.gain_ref
  11.3 1.0 copy.48.shift_ref
  12.3 0.2 select_reduce_fusion.1
  12.5 0.2 select_reduce_fusion
  12.7 2.8 multiply_sine_fusion
  15.5 0.7 bitcast_select_fusion.own_forward_ref
  16.2 55.7 %entry.1 = (bf16[3,128,4096]{2,1,0:T(8,128)(2,1)}, bf16[3,4096,128]{2,1,0:T(8,128)(2,1)}, bf16[3,128,4096]{2,1,0:T(8,128)(2,1)}, bf16[3,128,4096]{2,1,0:T(8,128)...) custom-call(bf16[2,2048,768]{2,1,0:T(8,128)(2,1)} %rows_ref.3, ...), custom_call_target="tpu_custom_call" | custom-call | flops 3623878656 | bytes 27377664 | tf_op jit(solution)/shard_map/entry/pallas_call | solution.py:429
  71.9 2.7 collective-permute-start
  74.9 0.6 pad_add_fusion.1.range_ref
  75.5 33.2 %attend.1 = (bf16[8,192,512]{2,1,0:T(8,128)(2,1)}, bf16[3,128,4096]{2,1,0:T(8,128)(2,1)}) custom-call(s32[2,8]{1,0:T(2,128)} %pad_add_fusion.1.range_ref, bf16[3,128,4096]{2,1,0:T(8,128)(2,1)} %get-tuple-element.51.query_ref, bf16[3,4096,128]{2,1,0:T(8,128)(2,1)} %get-tuple-element.52.key_ref, bf16[3,128,4096]{2,1,0:T(8,128)(2,1)} %get-tuple-element.53.value_ref, ...), custom_call_target="tpu_custom_call" | custom-call | flops 25769803776 | bytes 9437184 | tf_op jit(solution)/shard_map/attend/pallas_call | solution.py:563
  108.7 0.1 copy.50
  108.8 0.6 pad_add_fusion.range_ref
  109.4 1.0 copy.60
  110.5 0.6 reshape.119
  111.1 0.6 reshape.121.down_bias_ref
  111.8 0.7 maximum_maximum_fusion.mod_ref
  112.5 2.3 all-gather.3.cloned.1.call-done
  114.8 121.2 %middle.1 = (bf16[1024,768]{1,0:T(8,128)(2,1)}, bf16[8,192,512]{2,1,0:T(8,128)(2,1)}, bf16[2,768,512]{2,1,0:T(8,128)(2,1)}, bf16[16,192,192]{2,1,0:T(8,128)(2,1)...) custom-call(bf16[8,192,512]{2,1,0:T(8,128)(2,1)} %get-tuple-element., ...), custom_call_target="tpu_custom_call" | custom-call | flops 47110422528 | bytes 18874368 | tf_op jit(solution)/shard_map/middle/pallas_call | solution.py:1209
  236.1 0.7 collective-permute-start.2
  236.7 1.6 collective-permute-start.3
  238.3 1.4 collective-permute-start.4
  239.7 1.2 dynamic-slice_bitcast_fusion
  240.9 0.5 collective-permute-start.5
  241.5 76.1 %attend_back.1 = (bf16[192,4096]{1,0:T(8,128)(2,1)}, bf16[192,4096]{1,0:T(8,128)(2,1)}, bf16[192,4096]{1,0:T(8,128)(2,1)}) custom-call(s32[2,8]{1,0:T(2,128)} %pad_add_fusion.range_ref, bf16[3,128,4096]{2,1,0:T(8,128)(2,1)} %get-tuple-element.55.query_ref, bf16[3,128,4096]{2,1,0:T(8,128)(2,1)} %get-tuple-element.56.key_ref, ...), custom_call_target="tpu_custom_call" | custom-call | flops 64424509440 | bytes 9437184 | tf_op jit(solution)/shard_map/attend_back/pallas_call | solution.py:678
  317.6 0.6 select_maximum_fusion.small_ref
  318.2 2.7 add_convert_fusion.1.up_ref
  320.9 1.3 add_convert_fusion.down_ref
  322.2 72.0 %entry_back.1 = (bf16[2,4,192,512]{3,2,1,0:T(8,128)(2,1)}, f32[192,576]{1,0:T(8,128)}, f32[8,4608]{1,0:T(8,128)}, f32[8,768]{1,0:T(8,128)}, f32[8,768]{1,0:T(8,1...) custom-call(bf16[192,4096]{1,0:T(8,128)(2,1)} %get-tuple-element.68.grad_query_ref, ...), custom_call_target="tpu_custom_call" | custom-call | flops 7247757312 | bytes 14155776 | tf_op jit(solution)/shard_map/entry_back/pallas_call | solution.py:1815
  394.3 0.8 convert_reduce_fusion
  395.1 1.9 fusion.6
  397.0 4.5 %fusion.4 = f32[128,4608]{1,0:T(8,128)} fusion(f32[8,4608]{1,0:T(8,128)} %get-tuple-element.84, f32[4608]{0:T(1024)S(1)} %constant_dynamic-update-slice_fusion, f32[8,768]{1,0:T(8,128)} %get-tuple-element.83), kind=kOutput, calls=%fused_computation.21 | convolution fusion | flops 56664064 | bytes 2529280 | tf_op jit(solution)/shard_map/dot_general | solution.py:56
  401.5 0.7 multiply_reduce_fusion
  402.2 0.6 slice_reduce_fusion
  402.8 0.4 convert_bitcast_fusion
  403.2 2.0 copy.58
  405.2 0.8 multiply_reduce_fusion.2
  406.0 0.2 copy.54
  406.3 1.0 copy.56
  407.3 0.8 multiply_reduce_fusion.1
  408.2 1.1 fusion.42
  409.3 0.6 reshape.116
  409.9 1.0 fusion.14
  410.9 5.9 %copy.70 = bf16[2,2048,768]{2,1,0:T(8,128)(2,1)} copy(bf16[2,2048,768]{2,1,0:T(8,128)(2,1)} %get-tuple-element.150) | data formatting | bytes 12582912
  416.8 0.7 copy.71
  (99 shorter events, 0.9 us)
Async XLA Ops:
  7.2 2.3 copy-start
  7.2 2.3 copy-start.15
  7.2 2.3 copy-start.26
  7.2 2.5 copy-start.2
  7.2 107.6 %all-gather.3.cloned.1.call-start = ((), (), s32[]{:S(2)}) async-start(), calls=%async_computation.2 | async-start | bytes 1671168 | tf_op jit(solution)/shard_map/all_gather | solution.py:1967
  7.3 3.0 copy-start.16
  7.3 3.1 copy-start.22
  9.7 5.8 %copy-start.10 = (bf16[192,768]{1,0:T(8,128)(2,1)S(1)}, bf16[192,768]{1,0:T(8,128)(2,1)}, u32[]{:S(2)}) copy-start(bf16[192,768]{1,0:T(8,128)(2,1)} %param.26) | copy-start | bytes 884740
  9.7 5.8 %copy-start.11 = (bf16[768,192]{0,1:T(8,128)(2,1)S(1)}, bf16[768,192]{0,1:T(8,128)(2,1)}, u32[]{:S(2)}) copy-start(bf16[768,192]{0,1:T(8,128)(2,1)} %param.28) | copy-start | bytes 884740
  10.4 5.8 %copy-start.12 = (s32[1,4096]{1,0:T(1,128)}, s32[1,4096]{1,0:T(1,128)S(1)}, u32[]{:S(2)}) copy-start(s32[1,4096]{1,0:T(1,128)S(1)} %constant_dynamic-slice_fusion.segment_ref) | copy-start | bytes 49156
  71.9 40.6 %collective-permute-start = (bf16[768,768]{1,0:T(8,128)(2,1)}, bf16[768,768]{1,0:T(8,128)(2,1)S(1)}, u32[]{:S(2)}, u32[]{:S(2)}) collective-permute-start(bf16[768,768]{1,0:T(8,128)(2,1)} %get-tuple-element.58.own_ref), channel_id=1, source_target_pairs={{0,4},{4,0},{1,5},{5,1},{2,6},{6,2},{3,7},{7,3},{8,12},{12,8},{9,1... | collective-permute-start | bytes 3538952 | tf_op jit(solution)/shard_map/ppermute | solution.py:2023
  74.6 37.9 %collective-permute-start.1 = (bf16[768,768]{1,0:T(8,128)(2,1)}, bf16[768,768]{1,0:T(8,128)(2,1)S(1)}, u32[]{:S(2)}, u32[]{:S(2)}) collective-permute-start(bf16[768,768]{1,0:T(8,128)(2,1)} %get-tuple-element.58.own_ref), channel_id=1, source_target_pairs={{0,2},{1,3},{2,0},{3,1},{4,6},{5,7},{6,4},{7,5},{8,10},{9,11},{10,... | collective-permute-start | bytes 3538952 | tf_op jit(solution)/shard_map/ppermute | solution.py:2022
  74.6 247.6 %reduce-scatter.2.cloned.1.call-start = ((), (), s32[]{:S(2)}) async-start(), calls=%async_computation.1 | async-start | bytes 1671168 | tf_op jit(solution)/shard_map/reduce_scatter | solution.py:2076
  75.5 35.0 %copy-start.19 = (bf16[768]{0:T(1024)(128)(2,1)S(1)}, bf16[768]{0:T(1024)(128)(2,1)}, u32[]{:S(2)}) copy-start(bf16[768]{0:T(1024)(128)(2,1)} %param.25) | copy-start | bytes 4612
  75.5 35.0 %copy-start.21 = (bf16[3072]{0:T(1024)(128)(2,1)S(1)}, bf16[3072]{0:T(1024)(128)(2,1)}, u32[]{:S(2)}) copy-start(bf16[3072]{0:T(1024)(128)(2,1)} %param.27) | copy-start | bytes 18436
  75.5 35.6 %copy-start.23 = (bf16[768]{0:T(1024)(128)(2,1)S(1)}, bf16[768]{0:T(1024)(128)(2,1)}, u32[]{:S(2)}) copy-start(bf16[768]{0:T(1024)(128)(2,1)} %param.29) | copy-start | bytes 4612
  112.5 2.3 copy-start.24
  112.5 2.3 copy-start.25
  236.1 82.2 %collective-permute-start.2 = (bf16[2,4,96,768]{3,2,1,0:T(8,128)(2,1)}, bf16[2,4,96,768]{3,2,1,0:T(8,128)(2,1)}, u32[]{:S(2)}, u32[]{:S(2)}) collective-permute-start(bf16[2,4,96,768]{3,2,1,0:T(8,128)(2,1)} %get-tuple-element.62), channel_id=1, source_target_pairs={{0,2},{1,3},{2,0},{3,1},{4,6},{5,7},{6,4},{7,5},{8,10},{9,11},{10,... | collective-permute-start | bytes 3538952 | tf_op jit(solution)/shard_map/ppermute | solution.py:2074
  236.7 84.2 %collective-permute-start.3 = (bf16[2,4,96,768]{3,2,1,0:T(8,128)(2,1)}, bf16[2,4,96,768]{3,2,1,0:T(8,128)(2,1)S(1)}, u32[]{:S(2)}, u32[]{:S(2)}) collective-permute-start(bf16[2,4,96,768]{3,2,1,0:T(8,128)(2,1)} %get-tuple-element.64), channel_id=1, source_target_pairs={{0,4},{4,0},{1,5},{5,1},{2,6},{6,2},{3,7},{7,3},{8,12},{12,8},{9,1... | collective-permute-start | bytes 3538952 | tf_op jit(solution)/shard_map/ppermute | solution.py:2075
  238.3 83.9 %collective-permute-start.4 = (bf16[2,512,768]{2,1,0:T(8,128)(2,1)}, bf16[2,512,768]{2,1,0:T(8,128)(2,1)}, u32[]{:S(2)}, u32[]{:S(2)}) collective-permute-start(bf16[2,512,768]{2,1,0:T(8,128)(2,1)} %bitcast.66), channel_id=1, source_target_pairs={{0,2},{1,3},{2,0},{3,1},{4,6},{5,7},{6,4},{7,5},{8,10},{9,11},{10,... | collective-permute-start | bytes 4718600 | tf_op jit(solution)/shard_map/ppermute | solution.py:2056
  240.9 81.3 %collective-permute-start.5 = (bf16[768,512]{1,0:T(8,128)(2,1)S(1)}, bf16[768,512]{1,0:T(8,128)(2,1)}, u32[]{:S(2)}, u32[]{:S(2)}) collective-permute-start(bf16[768,512]{1,0:T(8,128)(2,1)S(1)} %dynamic-slice_bitcast_fusion), channel_id=1, source_target_pairs={{0,4},{4,0},{1,5},{5,1},{2,6},{6,2},{3,7},{7,3},{8,12},{12,8},{9,1... | collective-permute-start | bytes 2359304 | tf_op jit(solution)/shard_map/ppermute | solution.py:2057
  241.4 76.1 %copy-start.17 = (f32[4,1,768]{2,1,0:T(1,128)S(1)}, f32[4,1,768]{2,1,0:T(1,128)}, u32[]{:S(2)}) copy-start(f32[4,1,768]{2,1,0:T(1,128)} %get-tuple-element.76) | copy-start | bytes 36868
  241.5 76.1 %copy-start.14 = (f32[2,8,768]{2,1,0:T(8,128)S(1)}, f32[2,8,768]{2,1,0:T(8,128)}, u32[]{:S(2)}) copy-start(f32[2,8,768]{2,1,0:T(8,128)} %get-tuple-element.75) | copy-start | bytes 147460
  241.5 76.8 %copy-start.7 = (bf16[2,4,96,768]{3,2,1,0:T(8,128)(2,1)S(1)}, bf16[2,4,96,768]{3,2,1,0:T(8,128)(2,1)}, u32[]{:S(2)}) copy-start(bf16[2,4,96,768]{3,2,1,0:T(8,128)(2,1)} %get-tuple-element.61) | copy-start | bytes 3538948
  318.2 2.7 copy-start.6
  322.2 72.8 %copy-start.3 = (bf16[128,4608]{1,0:T(8,128)(2,1)S(1)}, bf16[128,4608]{1,0:T(8,128)(2,1)}, u32[]{:S(2)}) copy-start(bf16[128,4608]{1,0:T(8,128)(2,1)} %param.20) | copy-start | bytes 3538948
  397.0 4.5 %copy-start.5 = (f32[8,4608]{1,0:T(8,128)S(1)}, f32[8,4608]{1,0:T(8,128)}, u32[]{:S(2)}) copy-start(f32[8,4608]{1,0:T(8,128)} %get-tuple-element.84) | copy-start | bytes 442372
  397.0 5.2 %copy-start.18 = (f32[8,768]{1,0:T(8,128)S(1)}, f32[8,768]{1,0:T(8,128)}, u32[]{:S(2)}) copy-start(f32[8,768]{1,0:T(8,128)} %get-tuple-element.88) | copy-start | bytes 73732
  397.0 5.8 %copy-start.4 = (bf16[2,4,192,512]{3,2,1,0:T(8,128)(2,1)S(1)}, bf16[2,4,192,512]{3,2,1,0:T(8,128)(2,1)}, u32[]{:S(2)}) copy-start(bf16[2,4,192,512]{3,2,1,0:T(8,128)(2,1)} %get-tuple-element.82) | copy-start | bytes 4718596
  403.2 2.0 copy-start.20
  403.2 2.8 copy-start.9
  406.0 2.1 copy-start.8
  410.9 5.9 %copy-start.13 = (f32[192,192]{1,0:T(8,128)S(1)}, f32[192,192]{1,0:T(8,128)}, u32[]{:S(2)}) copy-start(f32[192,192]{1,0:T(8,128)} %get-tuple-element.157) | copy-start | bytes 442372
  410.9 6.6 %copy-start.1 = (bf16[256,128]{1,0:T(8,128)(2,1)S(1)}, bf16[256,128]{1,0:T(8,128)(2,1)}, u32[]{:S(2)}) copy-start(bf16[256,128]{1,0:T(8,128)(2,1)} %param.19) | copy-start | bytes 196612
Sparse Core Ops, SparseCore 0:
  74.7 40.0 all-gather.2
  241.6 62.8 reduce-scatter.1

commit v7 on v6

--- a/solution.py
+++ b/solution.py
@@ -316,9 +316,9 @@
 
     half = 4
 
-    for distance in range(1, groups):
-
-        @pl.when(step == 1 + 2 * distance)
+    for distance in range(1, groups - 1):
+
+        @pl.when(step == 3 * distance - 1)
         def _():
             hand_over(distance)
 
@@ -394,6 +394,7 @@
             across_copy(number).wait_send()
             sibling_copy(number).wait_send()
             on_copy(number).wait_send()
+        hand_over(groups - 1)
         finish_forward()
 
 

time: 425 us -> 422 us (level)
  Pallas kernels: 358 us -> 353 us
    pallas_call x1, Pallas kernels: 33.2 us -> 57.7 us  [attend_call(): pl.pallas_call(partial(attend_kernel, block=block), grid_spec=pltpu.Prefe...]
    pallas_call x1, Pallas kernels: 121 us -> 97.8 us  [middle_call(): pl.pallas_call(partial(middle_kernel, tile=tile, tiles=tiles, parts=parts...]
  transfers between devices with their start and end apart: 8 -> 8, of which waited for: 1 -> 0; matrix products, arithmetic and copies ran while one was open for 2% -> 2% of each run, Pallas kernels for 26% -> 32%
where the time goes in v7:
time: 422 us; the launch traced here: 420 us
  Pallas kernels  353 us (84%)
  local copies, waits for them, and re-layouts  20.9 us (5%)
  between operations  14.9 us (4%)
  other arithmetic  13 us (3%)
  matrix products  9.79 us (2%)
  starting transfers between devices  7.52 us (2%)
    pallas_call x1, Pallas kernels, middle_call(): pl.pallas_call(partial(middle_kernel, tile=tile, tiles=tiles, parts=parts...  97.8 us
    pallas_call x1, Pallas kernels, attend_back_call(): pl.pallas_call(partial(attend_back_kernel, block=block), grid_spec=pltpu....  76.1 us
    pallas_call x1, Pallas kernels, entry_back_call(): pl.pallas_call(partial(entry_back_kernel, tiles=tiles, groups=groups), gr...  69.7 us
    pallas_call x1, Pallas kernels, attend_call(): pl.pallas_call(partial(attend_kernel, block=block), grid_spec=pltpu.Prefe...  57.7 us
    pallas_call x1, Pallas kernels, entry_call(): pl.pallas_call(partial(entry_kernel, heads=heads, groups=groups), grid=(2...  52.2 us
    unnamed x63, local copies, waits for them, and re-layouts  11.4 us
  transfers between devices with their start and end apart: 8, of which 0 were waited for; matrix products, arithmetic and copies ran while one was open for 2% of the time, Pallas kernels for 32%

profile of v7, /device:TPU:0, one launch (start us, length us, event | category | flops | bytes accessed | tf_op | source)
XLA Modules:
  0.0 419.7 jit_solution(4515714192168773777)
XLA Ops:
  7.3 1.2 copy.44
  8.6 0.9 copy.46.shard_ref
  9.5 0.2 fusion.24
  9.7 0.6 convolution_add_fusion
  10.4 0.9 broadcast_in_dim.78.gain_ref
  11.3 1.0 copy.48.shift_ref
  12.3 0.2 select_reduce_fusion.1
  12.7 2.8 multiply_sine_fusion
  15.5 0.7 bitcast_select_fusion.own_forward_ref
  16.2 52.2 %entry.1 = (bf16[3,128,4096]{2,1,0:T(8,128)(2,1)}, bf16[3,4096,128]{2,1,0:T(8,128)(2,1)}, bf16[3,128,4096]{2,1,0:T(8,128)(2,1)}, bf16[3,128,4096]{2,1,0:T(8,128)...) custom-call(bf16[2,2048,768]{2,1,0:T(8,128)(2,1)} %rows_ref.3, ...), custom_call_target="tpu_custom_call" | custom-call | flops 3623878656 | bytes 27377664 | tf_op jit(solution)/shard_map/entry/pallas_call | solution.py:430
  68.4 2.5 collective-permute-start
  70.8 0.8 collective-permute-start.1
  71.9 0.6 pad_add_fusion.1.range_ref
  72.5 57.7 %attend.1 = (bf16[8,192,512]{2,1,0:T(8,128)(2,1)}, bf16[3,128,4096]{2,1,0:T(8,128)(2,1)}) custom-call(s32[2,8]{1,0:T(2,128)} %pad_add_fusion.1.range_ref, bf16[3,128,4096]{2,1,0:T(8,128)(2,1)} %get-tuple-element.51.query_ref, bf16[3,4096,128]{2,1,0:T(8,128)(2,1)} %get-tuple-element.52.key_ref, bf16[3,128,4096]{2,1,0:T(8,128)(2,1)} %get-tuple-element.53.value_ref, ...), custom_call_target="tpu_custom_call" | custom-call | flops 25769803776 | bytes 9437184 | tf_op jit(solution)/shard_map/attend/pallas_call | solution.py:564
  130.3 0.6 pad_add_fusion.range_ref
  130.9 1.0 copy.60
  132.0 0.6 reshape.119
  132.6 0.6 reshape.121.down_bias_ref
  133.3 0.7 maximum_maximum_fusion.mod_ref
  134.1 1.0 copy-done.24
  135.0 0.4 copy-done.25
  135.4 97.8 %middle.1 = (bf16[1024,768]{1,0:T(8,128)(2,1)}, bf16[8,192,512]{2,1,0:T(8,128)(2,1)}, bf16[2,768,512]{2,1,0:T(8,128)(2,1)}, bf16[16,192,192]{2,1,0:T(8,128)(2,1)...) custom-call(bf16[8,192,512]{2,1,0:T(8,128)(2,1)} %get-tuple-element., ...), custom_call_target="tpu_custom_call" | custom-call | flops 47110422528 | bytes 18874368 | tf_op jit(solution)/shard_map/middle/pallas_call | solution.py:1210
  233.2 1.5 collective-permute-start.2
  234.7 0.5 collective-permute-start.3
  235.2 0.6 collective-permute-start.4
  235.8 1.2 dynamic-slice_bitcast_fusion
  237.0 1.6 collective-permute-start.5
  238.6 76.1 %attend_back.1 = (bf16[192,4096]{1,0:T(8,128)(2,1)}, bf16[192,4096]{1,0:T(8,128)(2,1)}, bf16[192,4096]{1,0:T(8,128)(2,1)}) custom-call(s32[2,8]{1,0:T(2,128)} %pad_add_fusion.range_ref, bf16[3,128,4096]{2,1,0:T(8,128)(2,1)} %get-tuple-element.55.query_ref, bf16[3,128,4096]{2,1,0:T(8,128)(2,1)} %get-tuple-element.56.key_ref, ...), custom_call_target="tpu_custom_call" | custom-call | flops 64424509440 | bytes 9437184 | tf_op jit(solution)/shard_map/attend_back/pallas_call | solution.py:679
  314.8 0.6 select_maximum_fusion.small_ref
  315.4 2.7 add_convert_fusion.1.up_ref
  318.1 1.3 add_convert_fusion.down_ref
  319.4 69.7 %entry_back.1 = (bf16[2,4,192,512]{3,2,1,0:T(8,128)(2,1)}, f32[192,576]{1,0:T(8,128)}, f32[8,4608]{1,0:T(8,128)}, f32[8,768]{1,0:T(8,128)}, f32[8,768]{1,0:T(8,1...) custom-call(bf16[192,4096]{1,0:T(8,128)(2,1)} %get-tuple-element.68.grad_query_ref, ...), custom_call_target="tpu_custom_call" | custom-call | flops 7247757312 | bytes 14155776 | tf_op jit(solution)/shard_map/entry_back/pallas_call | solution.py:1816
  389.2 0.8 convert_reduce_fusion
  390.0 1.9 fusion.6
  391.9 4.5 %fusion.4 = f32[128,4608]{1,0:T(8,128)} fusion(f32[8,4608]{1,0:T(8,128)} %get-tuple-element.84, f32[4608]{0:T(1024)S(1)} %constant_dynamic-update-slice_fusion, f32[8,768]{1,0:T(8,128)} %get-tuple-element.83), kind=kOutput, calls=%fused_computation.21 | convolution fusion | flops 56664064 | bytes 2529280 | tf_op jit(solution)/shard_map/dot_general | solution.py:56
  396.4 0.7 multiply_reduce_fusion
  397.1 0.6 slice_reduce_fusion
  397.7 0.4 convert_bitcast_fusion
  398.1 2.0 copy.58
  400.1 0.8 multiply_reduce_fusion.2
  400.9 0.2 copy.54
  401.2 1.0 copy.56
  402.2 0.8 multiply_reduce_fusion.1
  403.1 1.1 fusion.42
  404.2 0.6 reshape.116
  404.8 1.0 fusion.14
  405.8 5.9 %copy.70 = bf16[2,2048,768]{2,1,0:T(8,128)(2,1)} copy(bf16[2,2048,768]{2,1,0:T(8,128)(2,1)} %get-tuple-element.150) | data formatting | bytes 12582912
  411.7 0.7 copy.71
  (99 shorter events, 1.2 us)
Async XLA Ops:
  7.2 2.3 copy-start
  7.2 2.3 copy-start.15
  7.2 2.3 copy-start.26
  7.2 2.5 copy-start.2
  7.2 126.8 %all-gather.3.cloned.1.call-start = ((), (), s32[]{:S(2)}) async-start(), calls=%async_computation.2 | async-start | bytes 1671168 | tf_op jit(solution)/shard_map/all_gather | solution.py:1968
  7.3 3.0 copy-start.16
  7.3 3.1 copy-start.22
  9.7 5.8 %copy-start.10 = (bf16[192,768]{1,0:T(8,128)(2,1)S(1)}, bf16[192,768]{1,0:T(8,128)(2,1)}, u32[]{:S(2)}) copy-start(bf16[192,768]{1,0:T(8,128)(2,1)} %param.26) | copy-start | bytes 884740
  9.7 5.8 %copy-start.11 = (bf16[768,192]{0,1:T(8,128)(2,1)S(1)}, bf16[768,192]{0,1:T(8,128)(2,1)}, u32[]{:S(2)}) copy-start(bf16[768,192]{0,1:T(8,128)(2,1)} %param.28) | copy-start | bytes 884740
  10.4 5.8 %copy-start.12 = (s32[1,4096]{1,0:T(1,128)}, s32[1,4096]{1,0:T(1,128)S(1)}, u32[]{:S(2)}) copy-start(s32[1,4096]{1,0:T(1,128)S(1)} %constant_dynamic-slice_fusion.segment_ref) | copy-start | bytes 49156
  68.4 65.6 %collective-permute-start = (bf16[768,768]{1,0:T(8,128)(2,1)}, bf16[768,768]{1,0:T(8,128)(2,1)S(1)}, u32[]{:S(2)}, u32[]{:S(2)}) collective-permute-start(bf16[768,768]{1,0:T(8,128)(2,1)} %get-tuple-element.58.own_ref), channel_id=1, source_target_pairs={{0,4},{4,0},{1,5},{5,1},{2,6},{6,2},{3,7},{7,3},{8,12},{12,8},{9,1... | collective-permute-start | bytes 3538952 | tf_op jit(solution)/shard_map/ppermute | solution.py:2024
  70.8 63.2 %collective-permute-start.1 = (bf16[768,768]{1,0:T(8,128)(2,1)}, bf16[768,768]{1,0:T(8,128)(2,1)S(1)}, u32[]{:S(2)}, u32[]{:S(2)}) collective-permute-start(bf16[768,768]{1,0:T(8,128)(2,1)} %get-tuple-element.58.own_ref), channel_id=1, source_target_pairs={{0,2},{1,3},{2,0},{3,1},{4,6},{5,7},{6,4},{7,5},{8,10},{9,11},{10,... | collective-permute-start | bytes 3538952 | tf_op jit(solution)/shard_map/ppermute | solution.py:2023
  71.7 247.8 %reduce-scatter.2.cloned.1.call-start = ((), (), s32[]{:S(2)}) async-start(), calls=%async_computation.1 | async-start | bytes 1671168 | tf_op jit(solution)/shard_map/reduce_scatter | solution.py:2077
  72.5 59.5 %copy-start.19 = (bf16[768]{0:T(1024)(128)(2,1)S(1)}, bf16[768]{0:T(1024)(128)(2,1)}, u32[]{:S(2)}) copy-start(bf16[768]{0:T(1024)(128)(2,1)} %param.25) | copy-start | bytes 4612
  72.5 59.5 %copy-start.21 = (bf16[3072]{0:T(1024)(128)(2,1)S(1)}, bf16[3072]{0:T(1024)(128)(2,1)}, u32[]{:S(2)}) copy-start(bf16[3072]{0:T(1024)(128)(2,1)} %param.27) | copy-start | bytes 18436
  72.5 60.1 %copy-start.23 = (bf16[768]{0:T(1024)(128)(2,1)S(1)}, bf16[768]{0:T(1024)(128)(2,1)}, u32[]{:S(2)}) copy-start(bf16[768]{0:T(1024)(128)(2,1)} %param.29) | copy-start | bytes 4612
  134.0 1.0 copy-start.24
  134.0 1.4 copy-start.25
  233.2 82.2 %collective-permute-start.2 = (bf16[2,4,96,768]{3,2,1,0:T(8,128)(2,1)}, bf16[2,4,96,768]{3,2,1,0:T(8,128)(2,1)}, u32[]{:S(2)}, u32[]{:S(2)}) collective-permute-start(bf16[2,4,96,768]{3,2,1,0:T(8,128)(2,1)} %get-tuple-element.62), channel_id=1, source_target_pairs={{0,2},{1,3},{2,0},{3,1},{4,6},{5,7},{6,4},{7,5},{8,10},{9,11},{10,... | collective-permute-start | bytes 3538952 | tf_op jit(solution)/shard_map/ppermute | solution.py:2075
  234.7 83.4 %collective-permute-start.3 = (bf16[2,4,96,768]{3,2,1,0:T(8,128)(2,1)}, bf16[2,4,96,768]{3,2,1,0:T(8,128)(2,1)S(1)}, u32[]{:S(2)}, u32[]{:S(2)}) collective-permute-start(bf16[2,4,96,768]{3,2,1,0:T(8,128)(2,1)} %get-tuple-element.64), channel_id=1, source_target_pairs={{0,4},{4,0},{1,5},{5,1},{2,6},{6,2},{3,7},{7,3},{8,12},{12,8},{9,1... | collective-permute-start | bytes 3538952 | tf_op jit(solution)/shard_map/ppermute | solution.py:2076
  235.2 84.2 %collective-permute-start.4 = (bf16[2,512,768]{2,1,0:T(8,128)(2,1)}, bf16[2,512,768]{2,1,0:T(8,128)(2,1)}, u32[]{:S(2)}, u32[]{:S(2)}) collective-permute-start(bf16[2,512,768]{2,1,0:T(8,128)(2,1)} %bitcast.66), channel_id=1, source_target_pairs={{0,2},{1,3},{2,0},{3,1},{4,6},{5,7},{6,4},{7,5},{8,10},{9,11},{10,... | collective-permute-start | bytes 4718600 | tf_op jit(solution)/shard_map/ppermute | solution.py:2057
  237.0 82.4 %collective-permute-start.5 = (bf16[768,512]{1,0:T(8,128)(2,1)S(1)}, bf16[768,512]{1,0:T(8,128)(2,1)}, u32[]{:S(2)}, u32[]{:S(2)}) collective-permute-start(bf16[768,512]{1,0:T(8,128)(2,1)S(1)} %dynamic-slice_bitcast_fusion), channel_id=1, source_target_pairs={{0,4},{4,0},{1,5},{5,1},{2,6},{6,2},{3,7},{7,3},{8,12},{12,8},{9,1... | collective-permute-start | bytes 2359304 | tf_op jit(solution)/shard_map/ppermute | solution.py:2058
  238.6 76.1 %copy-start.17 = (f32[4,1,768]{2,1,0:T(1,128)S(1)}, f32[4,1,768]{2,1,0:T(1,128)}, u32[]{:S(2)}) copy-start(f32[4,1,768]{2,1,0:T(1,128)} %get-tuple-element.76) | copy-start | bytes 36868
  238.6 76.1 %copy-start.14 = (f32[2,8,768]{2,1,0:T(8,128)S(1)}, f32[2,8,768]{2,1,0:T(8,128)}, u32[]{:S(2)}) copy-start(f32[2,8,768]{2,1,0:T(8,128)} %get-tuple-element.75) | copy-start | bytes 147460
  238.6 76.8 %copy-start.7 = (bf16[2,4,96,768]{3,2,1,0:T(8,128)(2,1)S(1)}, bf16[2,4,96,768]{3,2,1,0:T(8,128)(2,1)}, u32[]{:S(2)}) copy-start(bf16[2,4,96,768]{3,2,1,0:T(8,128)(2,1)} %get-tuple-element.61) | copy-start | bytes 3538948
  315.4 2.7 copy-start.6
  319.4 70.5 %copy-start.3 = (bf16[128,4608]{1,0:T(8,128)(2,1)S(1)}, bf16[128,4608]{1,0:T(8,128)(2,1)}, u32[]{:S(2)}) copy-start(bf16[128,4608]{1,0:T(8,128)(2,1)} %param.20) | copy-start | bytes 3538948
  391.9 4.5 %copy-start.5 = (f32[8,4608]{1,0:T(8,128)S(1)}, f32[8,4608]{1,0:T(8,128)}, u32[]{:S(2)}) copy-start(f32[8,4608]{1,0:T(8,128)} %get-tuple-element.84) | copy-start | bytes 442372
  391.9 5.2 %copy-start.18 = (f32[8,768]{1,0:T(8,128)S(1)}, f32[8,768]{1,0:T(8,128)}, u32[]{:S(2)}) copy-start(f32[8,768]{1,0:T(8,128)} %get-tuple-element.88) | copy-start | bytes 73732
  391.9 5.8 %copy-start.4 = (bf16[2,4,192,512]{3,2,1,0:T(8,128)(2,1)S(1)}, bf16[2,4,192,512]{3,2,1,0:T(8,128)(2,1)}, u32[]{:S(2)}) copy-start(bf16[2,4,192,512]{3,2,1,0:T(8,128)(2,1)} %get-tuple-element.82) | copy-start | bytes 4718596
  398.1 2.0 copy-start.20
  398.1 2.8 copy-start.9
  400.9 2.1 copy-start.8
  405.8 5.9 %copy-start.13 = (f32[192,192]{1,0:T(8,128)S(1)}, f32[192,192]{1,0:T(8,128)}, u32[]{:S(2)}) copy-start(f32[192,192]{1,0:T(8,128)} %get-tuple-element.157) | copy-start | bytes 442372
  405.8 6.6 %copy-start.1 = (bf16[256,128]{1,0:T(8,128)(2,1)S(1)}, bf16[256,128]{1,0:T(8,128)(2,1)}, u32[]{:S(2)}) copy-start(bf16[256,128]{1,0:T(8,128)(2,1)} %param.19) | copy-start | bytes 196612
Sparse Core Ops, SparseCore 0:
  71.8 39.2 all-gather.2
  238.7 62.7 reduce-scatter.1
